TPU v7x, 128 devices: a whole 4x4x4 slice. The times are simulated.
128 devices in a mesh: samp: 4 (over y_hi, core), par: 32 (over z, x, y_lo).
Axes of the slice: x: 4, y: 4 (y_hi: 2, y_lo: 2; y = y_hi * 2 + y_lo), z: 4, core: 2. Of those that a mesh axis runs over, the one named last changes fastest.
Arguments:
- jacobian: bfloat16 [512, 65536], P('samp', 'par'), as said below
- energies: float32 [512], P('samp'), as said below
Outputs:
- update: float32 [65536], P('par')
- coefficients: float32 [512], P('samp')
Inputs may be any that keep to these rules, and one draw needn't show every extreme that they name: `jacobian`: real log-derivatives; each sample's row and each parameter's column carries its own scale. Real local energies.
All inputs are finite; a program needn't handle non-finite values.
Results may differ from a plain program's by a relative error of at most 0.0049.
Values may be sent and summed in bfloat16 or wider, within the bound.
No kernel may reach another device: no remote copies, remote signals or barrier semaphores. Data moves between devices by JAX's collectives and lax.ppermute only.
A program may use at most 64 MiB of HBM per device.

v0:
```python
import math

import jax
import jax.numpy as jnp
from jax import lax
from jax.sharding import PartitionSpec as P


def chol_solve(factor, rhs):
    column = rhs[:, None]
    lower_sol = lax.linalg.triangular_solve(factor, column, left_side=True, lower=True)
    upper_sol = lax.linalg.triangular_solve(
        factor, lower_sol, left_side=True, lower=True, transpose_a=True
    )
    return upper_sol[:, 0]


def row_product(left, right):
    return lax.dot_general(
        left, right, (((1,), (1,)), ((), ())), preferred_element_type=jnp.float32
    )


def per_device(jacobian, energies):
    groups = lax.axis_size("samp")
    slabs = lax.axis_size("par")
    rows = jacobian.shape[0]
    total = rows * groups
    scale = 1.0 / math.sqrt(total)
    column_sum = jnp.sum(jacobian, axis=0, dtype=jnp.float32)
    energy_sum = jnp.sum(energies)
    column_total, energy_total = lax.psum((column_sum, energy_sum), "samp")
    centered = ((jacobian.astype(jnp.float32) - (column_total / total)[None, :]) * scale).astype(
        jnp.bfloat16
    )
    centered_energy = (energies - energy_total / total) * scale
    half = groups // 2
    half_rows = rows // 2
    myself = lax.axis_index("samp")
    everyone = None
    everyone = lax.all_gather(centered, "samp", axis=0, tiled=True)
    partners = [
        lax.dynamic_slice_in_dim(everyone, (myself + offset) % groups * rows, rows, 0)
        for offset in range(half + 1)
    ]
    blocks = jnp.stack([row_product(centered, other) for other in partners[:half]])
    far_block = partners[half]
    lower_group = myself < half
    first = jnp.where(lower_group, centered, far_block)
    second = jnp.where(lower_group, far_block, centered)
    start = jnp.where(lower_group, 0, half_rows).astype(jnp.int32)
    row_part = lax.dynamic_slice_in_dim(first, start, half_rows, 0)
    half_block = row_product(row_part, second)[None]
    summed, summed_half = lax.psum((blocks, half_block), "par")
    table, half_table, energy_row = (
        lax.all_gather(summed, "samp", axis=1, tiled=True),
        lax.all_gather(summed_half, "samp", axis=1, tiled=True),
        lax.all_gather(centered_energy[None, :], "samp", axis=1, tiled=True),
    )
    energy_full = energy_row[0]
    layout = [[None] * groups for place in range(groups)]
    for source in range(groups):
        for offset in range(half):
            target = (source + offset) % groups
            piece = table[offset, source * rows : (source + 1) * rows]
            layout[source][target] = piece
            if offset > 0:
                layout[target][source] = piece.T
    for source in range(half):
        target = source + half
        upper_rows = half_table[0, source * half_rows : (source + 1) * half_rows]
        lower_rows = half_table[0, target * half_rows : (target + 1) * half_rows]
        piece = jnp.concatenate([upper_rows, lower_rows], axis=0)
        layout[source][target] = piece
        layout[target][source] = piece.T
    gram = jnp.block(layout) + 0.05 * jnp.eye(total, dtype=jnp.float32)
    factor = jnp.linalg.cholesky(gram)
    solution = chol_solve(factor, energy_full)
    own_coeffs = lax.dynamic_slice_in_dim(solution, myself * rows, rows, 0)
    factor_root = math.sqrt(jacobian.shape[1] * slabs)
    update = (
        jnp.dot(solution, everyone.astype(jnp.float32), precision=lax.Precision.HIGHEST)
        * factor_root
    )
    return (update, own_coeffs)


def solution(mesh):
    return jax.shard_map(
        per_device,
        mesh=mesh,
        in_specs=(P("samp", "par"), P("samp")),
        out_specs=(P("par"), P("samp")),
        check_vma=False,
    )
```

profile of v0, /device:TPU:0, one launch (start us, length us, event | category | flops | bytes accessed | tf_op | source)
XLA Modules:
  0.0 516.8 jit_solution(15226543976860739900)
XLA Ops:
  9.6 11.1 %all-reduce.1 = (f32[2048]{0:T(1024)S(1)}, f32[]{:T(128)}) all-reduce(f32[2048]{0:T(1024)S(1)} %convert_reduce_fusion, f32[]{:T(128)} %reduce_sum.19), channel_id=1, replica_groups=mesh['samp'=4,'par'=32] {'samp'}, use_global_device_ids=true, to_apply=%region_1.0 | all-reduce | flops 2049 | bytes 16392 | tf_op jit(solution)/shard_map/psum | solution.py:32
  20.7 2.0 fusion.13
  23.6 6.5 %all-gather.1 = f32[4,1,128]{2,1,0:T(1,128)S(1)} all-gather(f32[1,1,128]{2,1,0:T(1,128)S(1)} %multiply_bitcast_fusion), channel_id=2, replica_groups=mesh['samp'=4,'par'=32] {'samp'}, dimensions={0}, use_global_device_ids=true | all-gather | bytes 2560 | tf_op jit(solution)/shard_map/all_gather | solution.py:58
  30.1 19.6 %all-gather.4.cloned.1.call-done = bf16[512,2048]{1,0:T(8,128)(2,1)} async-done(((bf16[128,2048]{1,0:T(8,128)(2,1)}), bf16[512,2048]{1,0:T(8,128)(2,1)}) %all-gather.4.cloned.1.call-update) | async-done | bytes 2097168 | tf_op jit(solution)/shard_map/all_gather | solution.py:41
  49.7 1.6 convolution_bitcast_fusion
  51.4 1.5 convolution_bitcast_fusion.1
  53.9 157.3 %psum.30 = f32[1,64,128]{2,1,0:T(8,128)S(1)} all-reduce(f32[1,64,128]{2,1,0:T(8,128)S(1)} %convolution_bitcast_fusion.2), channel_id=1, replica_groups=mesh['samp'=4,'par'=32] {'par'}, use_global_device_ids=true, to_apply=%region_3.0 | all-reduce | flops 8192 | bytes 65536 | tf_op jit(solution)/shard_map/psum | solution.py:54
  211.2 6.9 %all_gather.14 = f32[1,256,128]{2,1,0:T(8,128)S(1)} all-gather(f32[1,64,128]{2,1,0:T(8,128)S(1)} %psum.30), channel_id=1, replica_groups=mesh['samp'=4,'par'=32] {'samp'}, dimensions={1}, use_global_device_ids=true | all-gather | bytes 163840 | tf_op jit(solution)/shard_map/all_gather | solution.py:57
  218.2 113.6 %all-reduce.4.cloned.1.call-done = f32[2,128,128]{1,2,0:T(8,128)} async-done(((f32[2,128,128]{1,2,0:T(8,128)}), f32[2,128,128]{1,2,0:T(8,128)}) %all-reduce.4.cloned.1.call-update) | async-done | bytes 131088 | tf_op jit(solution)/shard_map/psum | solution.py:54
  331.8 8.6 %all_gather.13 = f32[2,512,128]{1,2,0:T(8,128)S(1)} all-gather(f32[2,128,128]{1,2,0:T(8,128)} %all-reduce.4.cloned.1.call-done), channel_id=1, replica_groups=mesh['samp'=4,'par'=32] {'samp'}, dimensions={1}, use_global_device_ids=true | all-gather | bytes 655360 | tf_op jit(solution)/shard_map/all_gather | solution.py:56
  345.2 1.6 copy.33
  349.1 11.7 %cholesky.103 = f32[128,128]{1,0:T(8,128)S(1)} custom-call(f32[128,128]{1,0:T(8,128)S(1)} %cholesky.263), custom_call_target="Cholesky" | custom-call | tf_op jit(solution)/shard_map/jit(cholesky)/cholesky | solution.py:77
  361.5 9.8 %custom-call.32 = f32[1,128,128]{1,2,0:T(8,128)S(1)} custom-call(f32[1,128,128]{2,1,0:T(8,128)S(1)} %get-tuple-element.50), custom_call_target="InvertDiagBlocksLowerTriangular" | custom-call | tf_op jit(solution)/shard_map/jit(cholesky)/cholesky | solution.py:77
  374.0 11.7 %cholesky.215 = f32[128,128]{1,0:T(8,128)S(1)} custom-call(f32[128,128]{1,0:T(8,128)S(1)} %cholesky.267), custom_call_target="Cholesky" | custom-call | tf_op jit(solution)/shard_map/jit(cholesky)/cholesky | solution.py:77
  388.0 11.4 %custom-call.33 = f32[1,128,128]{1,2,0:T(8,128)} custom-call(f32[1,128,128]{2,1,0:T(8,128)} %get-tuple-element.48), custom_call_target="InvertDiagBlocksLowerTriangular" | custom-call | tf_op jit(solution)/shard_map/jit(cholesky)/cholesky | solution.py:77
  402.9 11.7 %cholesky.236 = f32[128,128]{1,0:T(8,128)S(1)} custom-call(f32[128,128]{1,0:T(8,128)S(1)} %cholesky.272), custom_call_target="Cholesky" | custom-call | tf_op jit(solution)/shard_map/jit(cholesky)/cholesky | solution.py:77
  414.8 9.8 %custom-call.34 = f32[1,128,128]{1,2,0:T(8,128)S(1)} custom-call(f32[1,128,128]{2,1,0:T(8,128)S(1)} %get-tuple-element.46), custom_call_target="InvertDiagBlocksLowerTriangular" | custom-call | tf_op jit(solution)/shard_map/jit(cholesky)/cholesky | solution.py:77
  426.2 11.9 %cholesky.253 = f32[128,128]{1,0:T(8,128)S(1)} custom-call(f32[128,128]{1,0:T(8,128)S(1)} %convolution_subtract_fusion.2), custom_call_target="Cholesky" | custom-call | tf_op jit(solution)/shard_map/jit(cholesky)/cholesky | solution.py:77
  444.6 14.9 %while.1 = (s32[]{:T(128)}, f32[512,512]{0,1:T(8,128)}, s32[4,2]{0,1:T(2,128)S(1)}, f32[4,128,128]{2,1,0:T(8,128)}, s32[]{:T(128)}) while((s32[]{:T(128)}, f32[512,512]{0,1:T(8,128)}, s32[4,2]{0,1:T(2,128)S(1)}, f32[4,128,128]{2,1,0:T(8,128)}, s32[]{:T(128)}) %tuple.43), condition=%wide.while_cond, body=%wide.while_body.sunk | while | flops 2 | bytes 393329 | solution.py:12
  445.2 2.3 dynamic-slice.11
  449.0 2.3 dynamic-slice.11
  452.7 2.3 dynamic-slice.11
  456.4 2.3 dynamic-slice.11
  459.4 40.1 %custom-call.35 = f32[4,128,128]{1,2,0:T(8,128)S(1)} custom-call(f32[4,128,128]{2,1,0:T(8,128)} %get-tuple-element.9), custom_call_target="InvertDiagBlocksLowerTriangular" | custom-call | tf_op jit(solution)/shard_map/triangular_solve | solution.py:12
  (110 shorter events, 41.2 us)
Async XLA Ops:
  7.2 16.4 %copy-start.10 = (f32[128]{0:T(128)S(1)}, f32[128]{0:T(128)}, u32[]{:S(2)}) copy-start(f32[128]{0:T(128)} %param.3) | copy-start | bytes 1540
  7.2 42.6 %all-gather.4.cloned.1.call-start = ((), (), s32[]{:S(2)}) async-start(), calls=%async_computation | async-start | bytes 2621440 | tf_op jit(solution)/shard_map/all_gather | solution.py:41
  22.7 30.9 %copy-start = (bf16[128,2048]{1,0:T(8,128)(2,1)S(1)}, bf16[128,2048]{1,0:T(8,128)(2,1)}, u32[]{:S(2)}) copy-start(bf16[128,2048]{1,0:T(8,128)(2,1)} %fusion.13) | copy-start | bytes 1572868
  22.7 309.0 %all-reduce.4.cloned.1.call-start = ((), (), s32[]{:S(2)}) async-start(), calls=%async_computation.1 | async-start | bytes 262144 | tf_op jit(solution)/shard_map/psum | solution.py:54
  49.7 3.9 copy-start.1
  218.1 125.2 %copy-start.8 = (f32[128,128]{0,1:T(8,128)}, f32[128,128]{0,1:T(8,128)S(1)}, u32[]{:S(2)}) copy-start(f32[128,128]{0,1:T(8,128)S(1)} %get-tuple-element.53) | copy-start | bytes 196612
  218.2 125.2 %copy-start.9 = (f32[128,128]{0,1:T(8,128)}, f32[128,128]{0,1:T(8,128)S(1)}, u32[]{:S(2)}) copy-start(f32[128,128]{0,1:T(8,128)S(1)} %get-tuple-element.54) | copy-start | bytes 196612
  340.4 3.0 copy-start.4
  340.4 3.0 copy-start.5
  340.4 3.0 copy-start.6
  340.6 2.9 copy-start.7
  343.4 0.7 copy-start.3
  348.0 1.0 copy-start.2
Sparse Core Ops, SparseCore 0:
  22.8 26.8 all-gather.3
  53.7 278.0 all-reduce.3
where the time goes:
time: 519 us; the launch traced here: 517 us
  blocking collectives  190 us (37%)
  waiting for transfers between devices  133 us (26%)
  other arithmetic  132 us (25%)
  local copies, waits for them, and re-layouts  24.2 us (5%)
  matrix products  19.4 us (4%)
  between operations  17.7 us (3%)
    psum x1, blocking collectives, per_device(): summed, summed_half = lax.psum((blocks, half_block), 'par')  157 us
    psum x1, waiting for transfers between devices, per_device(): summed, summed_half = lax.psum((blocks, half_block), 'par')  114 us
    another operation x15, other arithmetic, per_device(): factor = jnp.linalg.cholesky(gram)  81.4 us
    another operation x4, other arithmetic, chol_solve(): lax.linalg.triangular_solve(factor, lower_sol, left_side=True, lower=True...  41.3 us
    all_gather x1, waiting for transfers between devices, per_device(): everyone = lax.all_gather(centered, 'samp', axis=0, tiled=True)  19.6 us
    another operation x20, local copies, waits for them, and re-layouts  14.8 us
    psum x1, blocking collectives, per_device(): column_total, energy_total = lax.psum((column_sum, energy_sum), 'samp')  11.1 us
  transfers between devices with their start and end apart: 2, of which 2 were waited for; matrix products, arithmetic and copies ran while one was open for 0% of the time, Pallas kernels for 0%

commit v1 on v0

v1 whole, which is shorter than its diff:
```python
import math

import jax
import jax.numpy as jnp
from jax import lax
from jax.experimental import pallas as pl
from jax.experimental.pallas import tpu as pltpu
from jax.sharding import Mesh, PartitionSpec as P

GROUP = 128
ROWS = 8
PANELS = GROUP // ROWS
RIDGE = 0.05


def center_gram_kernel(place_ref, a_ref, b_ref, c_ref, d_ref, cent_ref, out_ref):
    total = 4 * GROUP
    scale = 1.0 / math.sqrt(total)
    parts = (a_ref, b_ref, c_ref, d_ref)
    column_sum = None
    for part in parts:
        piece = jnp.sum(part[...].astype(jnp.float32), axis=0, keepdims=True)
        column_sum = piece if column_sum is None else column_sum + piece
    mean = column_sum / total
    for number, part in enumerate(parts):
        start = pl.multiple_of(place_ref[number] * GROUP, GROUP)
        cent_ref[pl.ds(start, GROUP), :] = (
            (part[...].astype(jnp.float32) - mean) * scale
        ).astype(jnp.bfloat16)
    half = total // 2
    start = pl.multiple_of(place_ref[4] * half, half)
    gram = lax.dot_general(
        cent_ref[pl.ds(start, half), :],
        cent_ref[...],
        (((1,), (1,)), ((), ())),
        preferred_element_type=jnp.float32,
    )
    for strip in range(half // ROWS):
        for side in range(2):
            out_ref[2 * strip + side] = gram[
                ROWS * strip : ROWS * strip + ROWS, half * side : half * side + half
            ]


def lane(value, index):
    return jnp.broadcast_to(value[:, index : index + 1], (ROWS, GROUP))


def row(value, index):
    return jnp.broadcast_to(value[index : index + 1, :], (ROWS, GROUP))


def factor_block(rows):
    rows = list(rows)
    column = lax.broadcasted_iota(jnp.int32, (ROWS, GROUP), 1)
    line = lax.broadcasted_iota(jnp.int32, (ROWS, GROUP), 0)
    inverse, recips = [], []
    for p in range(PANELS):
        first = ROWS * p
        own = (column >= first) & (column < first + ROWS)
        panel = rows[p]
        spread = [lane(panel, first + j) for j in range(ROWS)]
        pivot = {(i, j): row(spread[j], i) for j in range(ROWS) for i in range(j, ROWS)}
        panel = jnp.where(own, (column - first == line).astype(jnp.float32), panel)
        work = [row(panel, i) for i in range(ROWS)]
        recip, lower = [], {}
        for j in range(ROWS):
            recip.append(1.0 / pivot[j, j])
            for i in range(j + 1, ROWS):
                lower[i, j] = pivot[i, j] * recip[j]
            for i in range(j + 1, ROWS):
                for m in range(j + 1, i + 1):
                    pivot[i, m] = pivot[i, m] - lower[i, j] * pivot[m, j]
                work[i] = work[i] - lower[i, j] * work[j]
        done = work[0]
        scale = recip[0]
        for j in range(1, ROWS):
            done = jnp.where(line == j, work[j], done)
            scale = jnp.where(line == j, recip[j], scale)
        inverse.append(jnp.where(column < first + ROWS, done, 0.0))
        recips.append(scale)
        if p == PANELS - 1:
            break
        solved = [work[j] * recip[j] for j in range(ROWS)]
        for j in range(ROWS - 1, -1, -1):
            for i in range(j):
                solved[i] = solved[i] - lower[j, i] * solved[j]
        for i in range(p + 1, PANELS):
            value = jnp.where(own, 0.0, rows[i])
            for j in range(ROWS):
                value = value - lane(rows[i], first + j) * solved[j]
            rows[i] = value
    return inverse, recips


def product(left, right, dims):
    return lax.dot_general(
        left,
        right,
        (dims, ((), ())),
        precision=lax.Precision.HIGHEST,
        preferred_element_type=jnp.float32,
    )


def solve_kernel(
    place_ref, mine_ref, other_ref, rhs_ref, cent_ref, coeff_ref, update_ref, gram, low, rec, z
):
    blocks = 4
    core = place_ref[4]
    for strip in range(2 * PANELS):
        for side in range(2):
            for which, ref in ((core, mine_ref), (1 - core, other_ref)):
                block_row = 2 * which + strip // PANELS
                inner = ROWS * (strip % PANELS)
                for part in range(2):
                    gram[block_row, 2 * side + part, inner : inner + ROWS, :] = ref[
                        2 * strip + side, :, GROUP * part : GROUP * part + GROUP
                    ]
    for k in range(blocks):
        gram[k, blocks] = rhs_ref[GROUP * k : GROUP * k + GROUP, :]
    column = lax.broadcasted_iota(jnp.int32, (ROWS, GROUP), 1)
    line = lax.broadcasted_iota(jnp.int32, (ROWS, GROUP), 0)

    def step(k, carry):
        panels = []
        for p in range(PANELS):
            ridge = jnp.where(column - ROWS * p == line, RIDGE, 0.0)
            panels.append(gram[k, k, ROWS * p : ROWS * p + ROWS, :] + ridge)
        inverse, recips = factor_block(panels)
        for p in range(PANELS):
            low[k, ROWS * p : ROWS * p + ROWS, :] = inverse[p]
            rec[k, ROWS * p : ROWS * p + ROWS, :] = recips[p]
        for now in range(blocks):

            @pl.when(k == now)
            def _():
                tri = low[now]
                rc = rec[now]
                ys = {j: product(tri, gram[now, j], ((1,), (0,))) for j in range(now + 1, blocks + 1)}
                zs = {j: ys[j] * rc for j in ys}
                for j in zs:
                    z[now, j] = zs[j]
                for i in range(now + 1, blocks):
                    for j in range(i, blocks + 1):
                        gram[i, j] = gram[i, j] - product(ys[i], zs[j], ((0,), (0,)))

        return carry

    lax.fori_loop(0, blocks, step, 0)
    xs = [None] * blocks
    for k in range(blocks - 1, -1, -1):
        right = z[k, blocks]
        for j in range(k + 1, blocks):
            right = right - product(z[k, j], xs[j], ((1,), (0,)))
        xs[k] = product(low[k], right, ((0,), (0,)))
        coeff_ref[GROUP * k : GROUP * k + GROUP, :] = xs[k]
    width = cent_ref.shape[1]
    for piece in range(width // GROUP):
        total = jnp.zeros((ROWS, GROUP), jnp.float32)
        for k in range(blocks):
            values = cent_ref[
                GROUP * k : GROUP * k + GROUP, GROUP * piece : GROUP * piece + GROUP
            ].astype(jnp.float32)
            scaled = values * xs[k]
            total = total + jnp.sum(scaled.reshape(PANELS, ROWS, GROUP), axis=0)
        update_ref[:, GROUP * piece : GROUP * piece + GROUP] = jnp.sum(
            total, axis=0, keepdims=True
        )


VMEM = pl.BlockSpec(memory_space=pltpu.VMEM)
SMEM = pl.BlockSpec(memory_space=pltpu.SMEM)


def center_gram(place, parts):
    columns = parts[0].shape[1]
    return pl.pallas_call(
        center_gram_kernel,
        out_shape=(
            jax.ShapeDtypeStruct((4 * GROUP, columns), jnp.bfloat16),
            jax.ShapeDtypeStruct((64, ROWS, 2 * GROUP), jnp.float32),
        ),
        in_specs=[SMEM] + [VMEM] * 4,
        out_specs=(VMEM, VMEM),
        compiler_params=pltpu.CompilerParams(vmem_limit_bytes=32 * 1024 * 1024),
        name="center_gram",
    )(place, *parts)


def solve(place, mine, other, rhs, cent):
    return pl.pallas_call(
        solve_kernel,
        out_shape=(
            jax.ShapeDtypeStruct((4 * GROUP, GROUP), jnp.float32),
            jax.ShapeDtypeStruct((1, cent.shape[1]), jnp.float32),
        ),
        in_specs=[SMEM] + [VMEM] * 4,
        out_specs=(VMEM, VMEM),
        scratch_shapes=[
            pltpu.VMEM((4, 5, GROUP, GROUP), jnp.float32),
            pltpu.VMEM((4, GROUP, GROUP), jnp.float32),
            pltpu.VMEM((4, GROUP, GROUP), jnp.float32),
            pltpu.VMEM((4, 5, GROUP, GROUP), jnp.float32),
        ],
        compiler_params=pltpu.CompilerParams(vmem_limit_bytes=32 * 1024 * 1024),
        name="solve",
    )(place, mine, other, rhs, cent)


SWAP = [(0, 1), (1, 0)]


def per_device(jacobian, energies):
    high = lax.axis_index("high")
    core = lax.axis_index("core")
    total = 4 * GROUP
    half = jacobian.shape[1] // 2
    keep = lax.dynamic_slice_in_dim(jacobian, high * half, half, 1)
    send = lax.dynamic_slice_in_dim(jacobian, (1 - high) * half, half, 1)
    far = lax.ppermute(send, "high", SWAP)
    far_energy = lax.ppermute(energies, "high", SWAP)
    near = lax.ppermute(keep, "core", SWAP)
    both = jnp.stack([energies, far_energy])
    near_both = lax.ppermute(both, "core", SWAP)
    diagonal = lax.ppermute(far, "core", SWAP)
    order = jnp.stack(
        [2 * high + core, 2 * (1 - high) + core, 2 * high + 1 - core, 2 * (1 - high) + 1 - core]
    )
    place = jnp.concatenate([order, core[None]]).astype(jnp.int32)
    pieces = jnp.concatenate([both, near_both])
    table = jnp.stack([pieces[2 * (g % 2 != core) + (g // 2 != high)] for g in range(4)])
    energy = table.reshape(total)
    centered_energy = (energy - jnp.sum(energy) / total) * (1.0 / math.sqrt(total))
    rhs = jnp.broadcast_to(centered_energy[:, None], (total, GROUP))
    cent, partial = center_gram(place, (keep, far, near, diagonal))
    ring = ("high", "par")
    parts = lax.all_to_all(partial, ring, split_axis=0, concat_axis=0, tiled=True)
    summed = jnp.sum(parts, axis=0)
    mine = lax.all_to_all(
        jnp.broadcast_to(summed[None], parts.shape), ring, split_axis=0, concat_axis=0, tiled=True
    )
    other = lax.ppermute(mine, "core", SWAP)
    coeffs, update = solve(place, mine, other, rhs, cent)
    own = lax.dynamic_slice_in_dim(coeffs, (2 * high + core) * GROUP, GROUP, 0)[:, 0]
    update = update[0] * math.sqrt(2 * half * lax.axis_size("par"))
    away = lax.ppermute(update, "high", SWAP)
    lower = jnp.where(high == 0, update, away)
    upper = jnp.where(high == 0, away, update)
    return jnp.concatenate([lower, upper]), own


def solution(mesh):
    shape = mesh.devices.shape
    fine = Mesh(mesh.devices.reshape(2, 2, shape[1]), ("high", "core", "par"))
    return jax.shard_map(
        per_device,
        mesh=fine,
        in_specs=(P(("high", "core"), "par"), P(("high", "core"))),
        out_specs=(P("par"), P(("high", "core"))),
        check_vma=False,
    )
```

time: 519 us -> 94.8 us (0.18)
  blocking collectives: 190 us -> 41.5 us
  other arithmetic: 132 us -> 1.41 us
  waiting for transfers between devices: 133 us -> 15.2 us
  Pallas kernels: 0 us -> 24.5 us
  local copies, waits for them, and re-layouts: 24.2 us -> 1.94 us
  matrix products: 19.4 us -> 0 us
  between operations: 17.7 us -> 3.27 us
  starting transfers between devices: 0.08 us -> 6.63 us
    psum x2 -> x0, blocking collectives: 168 us -> none  [the longest x1 157 us: per_device(): summed, summed_half = lax.psum((blocks, half_block), 'par')]
    another operation x20 -> x1, other arithmetic: 123 us -> 0.01 us  [per_device(): both = jnp.stack([energies, far_energy])]
    psum x1 -> x0, waiting for transfers between devices: 114 us -> none  [per_device(): summed, summed_half = lax.psum((blocks, half_block), 'par')]
    all_to_all x0 -> x2, blocking collectives: none -> 41.5 us  [the longest x1 24.5 us: per_device(): lax.all_to_all(partial, ring, split_axis=0, concat_axis=0, tiled=True)]
    pallas_call x0 -> x2, Pallas kernels: none -> 24.5 us  [the longest x1 22.9 us: solve(): pl.pallas_call(solve_kernel, out_shape=(jax.ShapeDtypeStruct((4 * GROUP,...]
    all_gather x3 -> x0, blocking collectives: 22.1 us -> none  [the longest x1 8.6 us: per_device(): lax.all_gather(summed, 'samp', axis=1, tiled=True)]
    all_gather x1 -> x0, waiting for transfers between devices: 19.6 us -> none  [per_device(): everyone = lax.all_gather(centered, 'samp', axis=0, tiled=True)]
    another operation x34 -> x0, local copies, waits for them, and re-layouts: 18.4 us -> none
  transfers between devices with their start and end apart: 2 -> 7, of which waited for: 2 -> 5; matrix products, arithmetic and copies ran while one was open for 0% -> 2% of each run, Pallas kernels for 0% -> 0%
where the time goes in v1:
time: 94.8 us; the launch traced here: 94.5 us
  blocking collectives  41.5 us (44%)
  Pallas kernels  24.5 us (26%)
  waiting for transfers between devices  15.2 us (16%)
  starting transfers between devices  6.63 us (7%)
  between operations  3.27 us (3%)
  local copies, waits for them, and re-layouts  1.94 us (2%)
  other arithmetic  1.41 us (1%)
    all_to_all x1, blocking collectives, per_device(): lax.all_to_all(partial, ring, split_axis=0, concat_axis=0, tiled=True)  24.5 us
    pallas_call x1, Pallas kernels, solve(): pl.pallas_call(solve_kernel, out_shape=(jax.ShapeDtypeStruct((4 * GROUP,...  22.9 us
    all_to_all x1, blocking collectives, per_device(): lax.all_to_all(jnp.broadcast_to(summed[None], parts.shape), ring, split_a...  17 us
    ppermute x1, waiting for transfers between devices, per_device(): far = lax.ppermute(send, 'high', SWAP)  6.3 us
    ppermute x1, waiting for transfers between devices, per_device(): far_energy = lax.ppermute(energies, 'high', SWAP)  3.45 us
    ppermute x1, starting transfers between devices, per_device(): far = lax.ppermute(send, 'high', SWAP)  3.36 us
    ppermute x1, waiting for transfers between devices, per_device(): away = lax.ppermute(update, 'high', SWAP)  2.89 us
  transfers between devices with their start and end apart: 7, of which 5 were waited for; matrix products, arithmetic and copies ran while one was open for 2% of the time, Pallas kernels for 0%

profile of v1, /device:TPU:0, one launch (start us, length us, event | category | flops | bytes accessed | tf_op | source)
XLA Modules:
  0.0 94.5 jit_solution(12883138257073644229)
XLA Ops:
  0.6 1.1 %constant_dynamic-slice_fusion.4 = (bf16[128,1024]{1,0:T(8,128)(2,1)S(1)}, bf16[128,1024]{1,0:T(8,128)(2,1)S(1)}) fusion(bf16[128,2048]{1,0:T(8,128)(2,1)} %param.2, s32[]{:T(128)S(6)} %select_n.35, s32[]{:T(128)S(6)} %select_n.34), kind=kLoop, calls=%fused_computation.13 | loop fusion | bytes 1048584 | tf_op jit(solution)/shard_map/dynamic_slice | solution.py:220
  1.7 3.4 %collective-permute-start = (bf16[128,1024]{1,0:T(8,128)(2,1)S(1)}, bf16[128,1024]{1,0:T(8,128)(2,1)S(1)}, u32[]{:S(2)}, u32[]{:S(2)}) collective-permute-start(bf16[128,1024]{1,0:T(8,128)(2,1)S(1)} %get-tuple-element.18), channel_id=1, source_target_pairs={{0,64},{64,0},{1,65},{65,1},{2,66},{66,2},{3,67},{67,3},{4,68},{68... | collective-permute-start | bytes 786440 | tf_op jit(solution)/shard_map/ppermute | solution.py:221
  5.1 0.0 collective-permute-start.1
  5.1 6.3 %collective-permute-done.b_ref = bf16[128,1024]{1,0:T(8,128)(2,1)S(1)} collective-permute-done((bf16[128,1024]{1,0:T(8,128)(2,1)S(1)}, bf16[128,1024]{1,0:T(8,128)(2,1)S(1)}, u32[]{:S(2)}, u32[]{:S(2)}) %collective-permute-start) | collective-permute-done | bytes 262176 | tf_op jit(solution)/shard_map/ppermute | solution.py:221
  11.4 0.0 collective-permute-start.2
  11.4 0.1 concatenate.10.place_ref
  11.5 1.4 %collective-permute-done.2.d_ref = bf16[128,1024]{1,0:T(8,128)(2,1)S(1)} collective-permute-done((bf16[128,1024]{1,0:T(8,128)(2,1)S(1)}, bf16[128,1024]{1,0:T(8,128)(2,1)S(1)}, u32[]{:S(2)}, u32[]{:S(2)}) %collective-permute-start.2) | collective-permute-done | bytes 262176 | tf_op jit(solution)/shard_map/ppermute | solution.py:226
  12.9 1.6 %center_gram.1 = (bf16[512,1024]{1,0:T(8,128)(2,1)S(1)}, f32[64,8,256]{2,1,0:T(8,128)S(1)}) custom-call(s32[5]{0:T(128)S(1)} %concatenate.10.place_ref, bf16[128,1024]{1,0:T(8,128)(2,1)S(1)} %get-tuple-element.19.a_ref, bf16[128,1024]{1,0:T(8,128)(2,1)S(1)} %collective-permute-done.b_ref, bf16[128,1024]{1,0:T(8,128)(2,1)S(1)} %collective-permute-done.1.c_ref, ...), custom_call_target="tpu_custom_call" | custom-call | tf_op jit(solution)/shard_map/center_gram/pallas_call | solution.py:178
  14.5 24.5 %all_to_all.10 = f32[64,8,256]{2,1,0:T(8,128)S(1)} all-to-all(f32[64,8,256]{2,1,0:T(8,128)S(1)} %get-tuple-element.6), channel_id=1, replica_groups=mesh['high'=2,'core'=2,'par'=32] {'high','par'}, dimensions={0} | all-to-all | bytes 1048576 | tf_op jit(solution)/shard_map/all_to_all | solution.py:238
  39.0 0.1 reduce_sum.31
  39.1 0.0 copy-start
  39.1 17.0 %all_to_all.11.mine_ref = f32[64,8,256]{2,1,0:T(8,128)S(1)} all-to-all(f32[64,8,256]{2,1,0:T(8,128)S(1)} %broadcast_in_dim.7), channel_id=1, replica_groups=mesh['high'=2,'core'=2,'par'=32] {'high','par'}, dimensions={0} | all-to-all | bytes 1048576 | tf_op jit(solution)/shard_map/all_to_all | solution.py:240
  56.2 0.0 collective-permute-start.3
  56.2 1.6 %collective-permute-start.4 = (f32[128]{0:T(128)S(1)}, f32[128]{0:T(128)S(1)}, u32[]{:S(2)}, u32[]{:S(2)}) collective-permute-start(f32[128]{0:T(128)S(1)} %copy-done), channel_id=1, source_target_pairs={{0,64},{64,0},{1,65},{65,1},{2,66},{66,2},{3,67},{67,3},{4,68},{68... | collective-permute-start | bytes 1544 | tf_op jit(solution)/shard_map/ppermute | solution.py:222
  57.8 3.5 %collective-permute-done.4 = f32[128]{0:T(128)S(1)} collective-permute-done((f32[128]{0:T(128)S(1)}, f32[128]{0:T(128)S(1)}, u32[]{:S(2)}, u32[]{:S(2)}) %collective-permute-start.4) | collective-permute-done | bytes 544 | tf_op jit(solution)/shard_map/ppermute | solution.py:222
  61.2 0.0 collective-permute-start.5
  61.3 1.1 %collective-permute-done.5 = f32[2,128]{1,0:T(2,128)S(1)} collective-permute-done((f32[2,128]{1,0:T(2,128)S(1)}, f32[2,128]{1,0:T(2,128)S(1)}, u32[]{:S(2)}, u32[]{:S(2)}) %collective-permute-start.5) | collective-permute-done | bytes 1056 | tf_op jit(solution)/shard_map/ppermute | solution.py:225
  62.4 0.7 fusion.5
  65.6 0.1 broadcast_in_dim.8.rhs_ref
  65.8 22.9 %solve.1 = (f32[512,128]{1,0:T(8,128)S(1)}, f32[1,1024]{1,0:T(1,128)S(1)}) custom-call(s32[5]{0:T(128)S(1)} %concatenate.10.place_ref, f32[64,8,256]{2,1,0:T(8,128)S(1)} %all_to_all.11.mine_ref, f32[64,8,256]{2,1,0:T(8,128)S(1)} %collective-permute-done.3.other_ref, f32[512,128]{1,0:T(8,128)S(1)} %broadcast_in_dim.8.rhs_ref, ...), custom_call_target="tpu_custom_call" | custom-call | tf_op jit(solution)/shard_map/solve/pallas_call | solution.py:192
  88.7 1.7 %collective-permute-start.6 = (f32[1024]{0:T(1024)S(1)}, f32[1024]{0:T(1024)S(1)}, u32[]{:S(2)}, u32[]{:S(2)}) collective-permute-start(f32[1024]{0:T(1024)S(1)} %bitcast.10), channel_id=1, source_target_pairs={{0,64},{64,0},{1,65},{65,1},{2,66},{66,2},{3,67},{67,3},{4,68},{68... | collective-permute-start | bytes 12296 | tf_op jit(solution)/shard_map/ppermute | solution.py:247
  90.4 0.6 dynamic-slice_reduce_fusion
  91.0 2.9 %collective-permute-done.6 = f32[1024]{0:T(1024)S(1)} collective-permute-done((f32[1024]{0:T(1024)S(1)}, f32[1024]{0:T(1024)S(1)}, u32[]{:S(2)}, u32[]{:S(2)}) %collective-permute-start.6) | collective-permute-done | bytes 4128 | tf_op jit(solution)/shard_map/ppermute | solution.py:247
  93.9 0.6 pad_maximum_fusion
  (9 shorter events, 0.1 us)
Async XLA Ops:
  1.7 9.7 %collective-permute-start = (bf16[128,1024]{1,0:T(8,128)(2,1)S(1)}, bf16[128,1024]{1,0:T(8,128)(2,1)S(1)}, u32[]{:S(2)}, u32[]{:S(2)}) collective-permute-start(bf16[128,1024]{1,0:T(8,128)(2,1)S(1)} %get-tuple-element.18), channel_id=1, source_target_pairs={{0,64},{64,0},{1,65},{65,1},{2,66},{66,2},{3,67},{67,3},{4,68},{68... | collective-permute-start | bytes 786440 | tf_op jit(solution)/shard_map/ppermute | solution.py:221
  5.1 6.4 %collective-permute-start.1 = (bf16[128,1024]{1,0:T(8,128)(2,1)S(1)}, bf16[128,1024]{1,0:T(8,128)(2,1)S(1)}, u32[]{:S(2)}, u32[]{:S(2)}) collective-permute-start(bf16[128,1024]{1,0:T(8,128)(2,1)S(1)} %get-tuple-element.19.a_ref), channel_id=1, source_target_pairs={{0,32},{32,0},{1,33},{33,1},{2,34},{34,2},{3,35},{35,3},{4,36},{36... | collective-permute-start | bytes 786440 | tf_op jit(solution)/shard_map/ppermute | solution.py:223
  11.4 1.5 %collective-permute-start.2 = (bf16[128,1024]{1,0:T(8,128)(2,1)S(1)}, bf16[128,1024]{1,0:T(8,128)(2,1)S(1)}, u32[]{:S(2)}, u32[]{:S(2)}) collective-permute-start(bf16[128,1024]{1,0:T(8,128)(2,1)S(1)} %collective-permute-done.b_ref), channel_id=1, source_target_pairs={{0,32},{32,0},{1,33},{33,1},{2,34},{34,2},{3,35},{35,3},{4,36},{36... | collective-permute-start | bytes 786440 | tf_op jit(solution)/shard_map/ppermute | solution.py:226
  39.1 17.0 %copy-start = (f32[128]{0:T(128)S(1)}, f32[128]{0:T(128)}, u32[]{:S(2)}) copy-start(f32[128]{0:T(128)} %param.3) | copy-start | bytes 1540
  56.2 9.5 %collective-permute-start.3 = (f32[64,8,256]{2,1,0:T(8,128)S(1)}, f32[64,8,256]{2,1,0:T(8,128)S(1)}, u32[]{:S(2)}, u32[]{:S(2)}) collective-permute-start(f32[64,8,256]{2,1,0:T(8,128)S(1)} %all_to_all.11.mine_ref), channel_id=1, source_target_pairs={{0,32},{32,0},{1,33},{33,1},{2,34},{34,2},{3,35},{35,3},{4,36},{36... | collective-permute-start | bytes 1572872 | tf_op jit(solution)/shard_map/ppermute | solution.py:243
  56.2 5.0 %collective-permute-start.4 = (f32[128]{0:T(128)S(1)}, f32[128]{0:T(128)S(1)}, u32[]{:S(2)}, u32[]{:S(2)}) collective-permute-start(f32[128]{0:T(128)S(1)} %copy-done), channel_id=1, source_target_pairs={{0,64},{64,0},{1,65},{65,1},{2,66},{66,2},{3,67},{67,3},{4,68},{68... | collective-permute-start | bytes 1544 | tf_op jit(solution)/shard_map/ppermute | solution.py:222
  61.2 1.1 %collective-permute-start.5 = (f32[2,128]{1,0:T(2,128)S(1)}, f32[2,128]{1,0:T(2,128)S(1)}, u32[]{:S(2)}, u32[]{:S(2)}) collective-permute-start(f32[2,128]{1,0:T(2,128)S(1)} %pad_maximum_fusion.2), channel_id=1, source_target_pairs={{0,32},{32,0},{1,33},{33,1},{2,34},{34,2},{3,35},{35,3},{4,36},{36... | collective-permute-start | bytes 3080 | tf_op jit(solution)/shard_map/ppermute | solution.py:225
  88.7 5.2 %collective-permute-start.6 = (f32[1024]{0:T(1024)S(1)}, f32[1024]{0:T(1024)S(1)}, u32[]{:S(2)}, u32[]{:S(2)}) collective-permute-start(f32[1024]{0:T(1024)S(1)} %bitcast.10), channel_id=1, source_target_pairs={{0,64},{64,0},{1,65},{65,1},{2,66},{66,2},{3,67},{67,3},{4,68},{68... | collective-permute-start | bytes 12296 | tf_op jit(solution)/shard_map/ppermute | solution.py:247

commit v2 on v1

--- a/solution.py
+++ b/solution.py
@@ -13,7 +13,7 @@
 RIDGE = 0.05
 
 
-def center_gram_kernel(place_ref, a_ref, b_ref, c_ref, d_ref, cent_ref, out_ref):
+def center_gram_kernel(place_ref, e_ref, a_ref, b_ref, c_ref, d_ref, cent_ref, out_ref):
     total = 4 * GROUP
     scale = 1.0 / math.sqrt(total)
     parts = (a_ref, b_ref, c_ref, d_ref)
@@ -40,6 +40,11 @@
             out_ref[2 * strip + side] = gram[
                 ROWS * strip : ROWS * strip + ROWS, half * side : half * side + half
             ]
+    column = lax.broadcasted_iota(jnp.int32, (ROWS, GROUP), 1)
+    mine = (column // (GROUP // 2) == place_ref[5]) & (place_ref[6] == 0)
+    for strip in range(PANELS):
+        energies = e_ref[ROWS * strip : ROWS * strip + ROWS, :]
+        out_ref[2 * (PANELS + strip), :, :GROUP] = jnp.where(mine, energies, 0.0)
 
 
 def lane(value, index):
@@ -104,7 +109,7 @@
 
 
 def solve_kernel(
-    place_ref, mine_ref, other_ref, rhs_ref, cent_ref, coeff_ref, update_ref, gram, low, rec, z
+    place_ref, mine_ref, other_ref, cent_ref, coeff_ref, update_ref, gram, low, rec, z
 ):
     blocks = 4
     core = place_ref[4]
@@ -117,8 +122,17 @@
                     gram[block_row, 2 * side + part, inner : inner + ROWS, :] = ref[
                         2 * strip + side, :, GROUP * part : GROUP * part + GROUP
                     ]
+    energy_sum = jnp.zeros((ROWS, GROUP), jnp.float32)
+    for which, ref in ((core, mine_ref), (1 - core, other_ref)):
+        for high in range(2):
+            for p in range(PANELS):
+                value = lane(ref[2 * (PANELS + p), :, :GROUP], high * GROUP // 2)
+                gram[2 * high + which, blocks, ROWS * p : ROWS * p + ROWS, :] = value
+                energy_sum = energy_sum + value
+    energy_mean = jnp.sum(energy_sum, axis=0, keepdims=True) / (blocks * GROUP)
+    scale = 1.0 / math.sqrt(blocks * GROUP)
     for k in range(blocks):
-        gram[k, blocks] = rhs_ref[GROUP * k : GROUP * k + GROUP, :]
+        gram[k, blocks] = (gram[k, blocks] - energy_mean) * scale
     column = lax.broadcasted_iota(jnp.int32, (ROWS, GROUP), 1)
     line = lax.broadcasted_iota(jnp.int32, (ROWS, GROUP), 0)
 
@@ -173,7 +187,7 @@
 SMEM = pl.BlockSpec(memory_space=pltpu.SMEM)
 
 
-def center_gram(place, parts):
+def center_gram(place, energies, parts):
     columns = parts[0].shape[1]
     return pl.pallas_call(
         center_gram_kernel,
@@ -181,21 +195,21 @@
             jax.ShapeDtypeStruct((4 * GROUP, columns), jnp.bfloat16),
             jax.ShapeDtypeStruct((64, ROWS, 2 * GROUP), jnp.float32),
         ),
-        in_specs=[SMEM] + [VMEM] * 4,
+        in_specs=[SMEM] + [VMEM] * 5,
         out_specs=(VMEM, VMEM),
         compiler_params=pltpu.CompilerParams(vmem_limit_bytes=32 * 1024 * 1024),
         name="center_gram",
-    )(place, *parts)
-
-
-def solve(place, mine, other, rhs, cent):
+    )(place, energies, *parts)
+
+
+def solve(place, mine, other, cent):
     return pl.pallas_call(
         solve_kernel,
         out_shape=(
             jax.ShapeDtypeStruct((4 * GROUP, GROUP), jnp.float32),
             jax.ShapeDtypeStruct((1, cent.shape[1]), jnp.float32),
         ),
-        in_specs=[SMEM] + [VMEM] * 4,
+        in_specs=[SMEM] + [VMEM] * 3,
         out_specs=(VMEM, VMEM),
         scratch_shapes=[
             pltpu.VMEM((4, 5, GROUP, GROUP), jnp.float32),
@@ -205,7 +219,7 @@
         ],
         compiler_params=pltpu.CompilerParams(vmem_limit_bytes=32 * 1024 * 1024),
         name="solve",
-    )(place, mine, other, rhs, cent)
+    )(place, mine, other, cent)
 
 
 SWAP = [(0, 1), (1, 0)]
@@ -214,26 +228,25 @@
 def per_device(jacobian, energies):
     high = lax.axis_index("high")
     core = lax.axis_index("core")
-    total = 4 * GROUP
     half = jacobian.shape[1] // 2
     keep = lax.dynamic_slice_in_dim(jacobian, high * half, half, 1)
     send = lax.dynamic_slice_in_dim(jacobian, (1 - high) * half, half, 1)
     far = lax.ppermute(send, "high", SWAP)
-    far_energy = lax.ppermute(energies, "high", SWAP)
     near = lax.ppermute(keep, "core", SWAP)
-    both = jnp.stack([energies, far_energy])
-    near_both = lax.ppermute(both, "core", SWAP)
     diagonal = lax.ppermute(far, "core", SWAP)
-    order = jnp.stack(
-        [2 * high + core, 2 * (1 - high) + core, 2 * high + 1 - core, 2 * (1 - high) + 1 - core]
-    )
-    place = jnp.concatenate([order, core[None]]).astype(jnp.int32)
-    pieces = jnp.concatenate([both, near_both])
-    table = jnp.stack([pieces[2 * (g % 2 != core) + (g // 2 != high)] for g in range(4)])
-    energy = table.reshape(total)
-    centered_energy = (energy - jnp.sum(energy) / total) * (1.0 / math.sqrt(total))
-    rhs = jnp.broadcast_to(centered_energy[:, None], (total, GROUP))
-    cent, partial = center_gram(place, (keep, far, near, diagonal))
+    place = jnp.stack(
+        [
+            2 * high + core,
+            2 * (1 - high) + core,
+            2 * high + 1 - core,
+            2 * (1 - high) + 1 - core,
+            core,
+            high,
+            lax.axis_index("par"),
+        ]
+    ).astype(jnp.int32)
+    spread = jnp.broadcast_to(energies[:, None], (GROUP, GROUP))
+    cent, partial = center_gram(place, spread, (keep, far, near, diagonal))
     ring = ("high", "par")
     parts = lax.all_to_all(partial, ring, split_axis=0, concat_axis=0, tiled=True)
     summed = jnp.sum(parts, axis=0)
@@ -241,7 +254,7 @@
         jnp.broadcast_to(summed[None], parts.shape), ring, split_axis=0, concat_axis=0, tiled=True
     )
     other = lax.ppermute(mine, "core", SWAP)
-    coeffs, update = solve(place, mine, other, rhs, cent)
+    coeffs, update = solve(place, mine, other, cent)
     own = lax.dynamic_slice_in_dim(coeffs, (2 * high + core) * GROUP, GROUP, 0)[:, 0]
     update = update[0] * math.sqrt(2 * half * lax.axis_size("par"))
     away = lax.ppermute(update, "high", SWAP)

time: 94.8 us -> 87.2 us (0.920)
  waiting for transfers between devices: 15.2 us -> 12.6 us
  between operations: 3.27 us -> 0.68 us
  starting transfers between devices: 6.63 us -> 5.03 us
    ppermute x2 -> x0, waiting for transfers between devices: 4.57 us -> none  [the longest x1 3.45 us: per_device(): far_energy = lax.ppermute(energies, 'high', SWAP)]
    ppermute x1, waiting for transfers between devices: 0.01 us -> 1.91 us  [per_device(): other = lax.ppermute(mine, 'core', SWAP)]
    ppermute x2 -> x0, starting transfers between devices: 1.59 us -> none  [the longest x1 1.59 us: per_device(): far_energy = lax.ppermute(energies, 'high', SWAP)]
  transfers between devices with their start and end apart: 7 -> 5, of which waited for: 5 -> 4; matrix products, arithmetic and copies ran while one was open for 2% -> 1% of each run, Pallas kernels for 0% -> 0%
where the time goes in v2:
time: 87.2 us; the launch traced here: 87 us
  blocking collectives  41.5 us (48%)
  Pallas kernels  24.6 us (28%)
  waiting for transfers between devices  12.6 us (14%)
  starting transfers between devices  5.03 us (6%)
  local copies, waits for them, and re-layouts  1.89 us (2%)
    all_to_all x1, blocking collectives, per_device(): lax.all_to_all(partial, ring, split_axis=0, concat_axis=0, tiled=True)  24.5 us
    pallas_call x1, Pallas kernels, solve(): pl.pallas_call(solve_kernel, out_shape=(jax.ShapeDtypeStruct((4 * GROUP,...  23 us
    all_to_all x1, blocking collectives, per_device(): lax.all_to_all(jnp.broadcast_to(summed[None], parts.shape), ring, split_a...  17 us
    ppermute x1, waiting for transfers between devices, per_device(): far = lax.ppermute(send, 'high', SWAP)  6.3 us
    ppermute x1, starting transfers between devices, per_device(): far = lax.ppermute(send, 'high', SWAP)  3.36 us
    ppermute x1, waiting for transfers between devices, per_device(): away = lax.ppermute(update, 'high', SWAP)  2.9 us
    ppermute x1, waiting for transfers between devices, per_device(): other = lax.ppermute(mine, 'core', SWAP)  1.91 us
  transfers between devices with their start and end apart: 5, of which 4 were waited for; matrix products, arithmetic and copies ran while one was open for 1% of the time, Pallas kernels for 0%

profile of v2, /device:TPU:0, one launch (start us, length us, event | category | flops | bytes accessed | tf_op | source)
XLA Modules:
  0.0 87.0 jit_solution(2364820638697257249)
XLA Ops:
  0.6 1.1 %constant_dynamic-slice_fusion = (bf16[128,1024]{1,0:T(8,128)(2,1)S(1)}, bf16[128,1024]{1,0:T(8,128)(2,1)S(1)}) fusion(bf16[128,2048]{1,0:T(8,128)(2,1)} %param.2, s32[]{:T(128)S(6)} %select_n.23, s32[]{:T(128)S(6)} %select_n.22), kind=kLoop, calls=%fused_computation.5 | loop fusion | bytes 1048584 | tf_op jit(solution)/shard_map/dynamic_slice | solution.py:233
  1.7 3.4 %collective-permute-start = (bf16[128,1024]{1,0:T(8,128)(2,1)S(1)}, bf16[128,1024]{1,0:T(8,128)(2,1)S(1)}, u32[]{:S(2)}, u32[]{:S(2)}) collective-permute-start(bf16[128,1024]{1,0:T(8,128)(2,1)S(1)} %get-tuple-element.10), channel_id=1, source_target_pairs={{0,64},{64,0},{1,65},{65,1},{2,66},{66,2},{3,67},{67,3},{4,68},{68... | collective-permute-start | bytes 786440 | tf_op jit(solution)/shard_map/ppermute | solution.py:234
  5.1 0.0 collective-permute-start.1
  5.1 6.3 %collective-permute-done.b_ref = bf16[128,1024]{1,0:T(8,128)(2,1)S(1)} collective-permute-done((bf16[128,1024]{1,0:T(8,128)(2,1)S(1)}, bf16[128,1024]{1,0:T(8,128)(2,1)S(1)}, u32[]{:S(2)}, u32[]{:S(2)}) %collective-permute-start) | collective-permute-done | bytes 262176 | tf_op jit(solution)/shard_map/ppermute | solution.py:234
  11.4 0.0 collective-permute-start.2
  11.4 0.0 copy-start
  11.4 0.1 stack.31.place_ref
  11.5 0.0 collective-permute-done.1.c_ref
  11.5 1.4 %collective-permute-done.2.d_ref = bf16[128,1024]{1,0:T(8,128)(2,1)S(1)} collective-permute-done((bf16[128,1024]{1,0:T(8,128)(2,1)S(1)}, bf16[128,1024]{1,0:T(8,128)(2,1)S(1)}, u32[]{:S(2)}, u32[]{:S(2)}) %collective-permute-start.2) | collective-permute-done | bytes 262176 | tf_op jit(solution)/shard_map/ppermute | solution.py:236
  12.9 0.0 copy-done
  12.9 0.1 broadcast_in_dim.4.e_ref
  13.0 1.6 %center_gram.1 = (bf16[512,1024]{1,0:T(8,128)(2,1)S(1)}, f32[64,8,256]{2,1,0:T(8,128)S(1)}) custom-call(s32[7]{0:T(128)S(1)} %stack.31.place_ref, f32[128,128]{1,0:T(8,128)S(1)} %broadcast_in_dim.4.e_ref, bf16[128,1024]{1,0:T(8,128)(2,1)S(1)} %get-tuple-element.11.a_ref, bf16[128,1024]{1,0:T(8,128)(2,1)S(1)} %collective-permute-done.b_ref, ...), custom_call_target="tpu_custom_call" | custom-call | tf_op jit(solution)/shard_map/center_gram/pallas_call | solution.py:192
  14.6 24.5 %all_to_all.10 = f32[64,8,256]{2,1,0:T(8,128)S(1)} all-to-all(f32[64,8,256]{2,1,0:T(8,128)S(1)} %get-tuple-element.6), channel_id=1, replica_groups=mesh['high'=2,'core'=2,'par'=32] {'high','par'}, dimensions={0} | all-to-all | bytes 1048576 | tf_op jit(solution)/shard_map/all_to_all | solution.py:251
  39.1 0.1 reduce_sum.9
  39.2 17.0 %all_to_all.11.mine_ref = f32[64,8,256]{2,1,0:T(8,128)S(1)} all-to-all(f32[64,8,256]{2,1,0:T(8,128)S(1)} %broadcast_in_dim.5), channel_id=1, replica_groups=mesh['high'=2,'core'=2,'par'=32] {'high','par'}, dimensions={0} | all-to-all | bytes 1048576 | tf_op jit(solution)/shard_map/all_to_all | solution.py:253
  56.2 0.0 collective-permute-start.3
  56.2 1.9 %collective-permute-done.3.other_ref = f32[64,8,256]{2,1,0:T(8,128)S(1)} collective-permute-done((f32[64,8,256]{2,1,0:T(8,128)S(1)}, f32[64,8,256]{2,1,0:T(8,128)S(1)}, u32[]{:S(2)}, u32[]{:S(2)}) %collective-permute-start.3) | collective-permute-done | bytes 524320 | tf_op jit(solution)/shard_map/ppermute | solution.py:256
  58.2 23.0 %solve.1 = (f32[512,128]{1,0:T(8,128)S(1)}, f32[1,1024]{1,0:T(1,128)S(1)}) custom-call(s32[7]{0:T(128)S(1)} %stack.31.place_ref, f32[64,8,256]{2,1,0:T(8,128)S(1)} %all_to_all.11.mine_ref, f32[64,8,256]{2,1,0:T(8,128)S(1)} %collective-permute-done.3.other_ref, bf16[512,1024]{1,0:T(8,128)(2,1)S(1)} %get-tuple-element.7.cent_ref), custom_call_target="tpu_custom_call" | custom-call | tf_op jit(solution)/shard_map/solve/pallas_call | solution.py:206
  81.2 1.7 %collective-permute-start.4 = (f32[1024]{0:T(1024)S(1)}, f32[1024]{0:T(1024)S(1)}, u32[]{:S(2)}, u32[]{:S(2)}) collective-permute-start(f32[1024]{0:T(1024)S(1)} %bitcast.8), channel_id=1, source_target_pairs={{0,64},{64,0},{1,65},{65,1},{2,66},{66,2},{3,67},{67,3},{4,68},{68... | collective-permute-start | bytes 12296 | tf_op jit(solution)/shard_map/ppermute | solution.py:260
  82.9 0.6 dynamic-slice_reduce_fusion
  83.5 2.9 %collective-permute-done.4 = f32[1024]{0:T(1024)S(1)} collective-permute-done((f32[1024]{0:T(1024)S(1)}, f32[1024]{0:T(1024)S(1)}, u32[]{:S(2)}, u32[]{:S(2)}) %collective-permute-start.4) | collective-permute-done | bytes 4128 | tf_op jit(solution)/shard_map/ppermute | solution.py:260
  86.4 0.6 pad_maximum_fusion
  (3 shorter events, 0.0 us)
Async XLA Ops:
  1.7 9.7 %collective-permute-start = (bf16[128,1024]{1,0:T(8,128)(2,1)S(1)}, bf16[128,1024]{1,0:T(8,128)(2,1)S(1)}, u32[]{:S(2)}, u32[]{:S(2)}) collective-permute-start(bf16[128,1024]{1,0:T(8,128)(2,1)S(1)} %get-tuple-element.10), channel_id=1, source_target_pairs={{0,64},{64,0},{1,65},{65,1},{2,66},{66,2},{3,67},{67,3},{4,68},{68... | collective-permute-start | bytes 786440 | tf_op jit(solution)/shard_map/ppermute | solution.py:234
  5.1 6.4 %collective-permute-start.1 = (bf16[128,1024]{1,0:T(8,128)(2,1)S(1)}, bf16[128,1024]{1,0:T(8,128)(2,1)S(1)}, u32[]{:S(2)}, u32[]{:S(2)}) collective-permute-start(bf16[128,1024]{1,0:T(8,128)(2,1)S(1)} %get-tuple-element.11.a_ref), channel_id=1, source_target_pairs={{0,32},{32,0},{1,33},{33,1},{2,34},{34,2},{3,35},{35,3},{4,36},{36... | collective-permute-start | bytes 786440 | tf_op jit(solution)/shard_map/ppermute | solution.py:235
  11.4 1.5 %collective-permute-start.2 = (bf16[128,1024]{1,0:T(8,128)(2,1)S(1)}, bf16[128,1024]{1,0:T(8,128)(2,1)S(1)}, u32[]{:S(2)}, u32[]{:S(2)}) collective-permute-start(bf16[128,1024]{1,0:T(8,128)(2,1)S(1)} %collective-permute-done.b_ref), channel_id=1, source_target_pairs={{0,32},{32,0},{1,33},{33,1},{2,34},{34,2},{3,35},{35,3},{4,36},{36... | collective-permute-start | bytes 786440 | tf_op jit(solution)/shard_map/ppermute | solution.py:236
  11.4 1.5 %copy-start = (f32[128]{0:T(128)S(1)}, f32[128]{0:T(128)}, u32[]{:S(2)}) copy-start(f32[128]{0:T(128)} %param.3) | copy-start | bytes 1540
  56.2 1.9 %collective-permute-start.3 = (f32[64,8,256]{2,1,0:T(8,128)S(1)}, f32[64,8,256]{2,1,0:T(8,128)S(1)}, u32[]{:S(2)}, u32[]{:S(2)}) collective-permute-start(f32[64,8,256]{2,1,0:T(8,128)S(1)} %all_to_all.11.mine_ref), channel_id=1, source_target_pairs={{0,32},{32,0},{1,33},{33,1},{2,34},{34,2},{3,35},{35,3},{4,36},{36... | collective-permute-start | bytes 1572872 | tf_op jit(solution)/shard_map/ppermute | solution.py:256
  81.2 5.2 %collective-permute-start.4 = (f32[1024]{0:T(1024)S(1)}, f32[1024]{0:T(1024)S(1)}, u32[]{:S(2)}, u32[]{:S(2)}) collective-permute-start(f32[1024]{0:T(1024)S(1)} %bitcast.8), channel_id=1, source_target_pairs={{0,64},{64,0},{1,65},{65,1},{2,66},{66,2},{3,67},{67,3},{4,68},{68... | collective-permute-start | bytes 12296 | tf_op jit(solution)/shard_map/ppermute | solution.py:260

commit v3 on v2

--- a/solution.py
+++ b/solution.py
@@ -9,6 +9,7 @@
 
 GROUP = 128
 ROWS = 8
+WIDE = 2
 PANELS = GROUP // ROWS
 RIDGE = 0.05
 
@@ -59,52 +60,79 @@
     rows = list(rows)
     column = lax.broadcasted_iota(jnp.int32, (ROWS, GROUP), 1)
     line = lax.broadcasted_iota(jnp.int32, (ROWS, GROUP), 0)
+    size = WIDE * ROWS
     inverse, recips = [], []
-    for p in range(PANELS):
+    for p in range(0, PANELS, WIDE):
         first = ROWS * p
-        own = (column >= first) & (column < first + ROWS)
-        panel = rows[p]
-        spread = [lane(panel, first + j) for j in range(ROWS)]
-        pivot = {(i, j): row(spread[j], i) for j in range(ROWS) for i in range(j, ROWS)}
-        panel = jnp.where(own, (column - first == line).astype(jnp.float32), panel)
-        work = [row(panel, i) for i in range(ROWS)]
-        recip, lower = [], {}
-        for j in range(ROWS):
-            recip.append(1.0 / pivot[j, j])
-            for i in range(j + 1, ROWS):
-                lower[i, j] = pivot[i, j] * recip[j]
-            for i in range(j + 1, ROWS):
-                for m in range(j + 1, i + 1):
-                    pivot[i, m] = pivot[i, m] - lower[i, j] * pivot[m, j]
-                work[i] = work[i] - lower[i, j] * work[j]
-        done = work[0]
-        scale = recip[0]
-        for j in range(1, ROWS):
-            done = jnp.where(line == j, work[j], done)
-            scale = jnp.where(line == j, recip[j], scale)
-        inverse.append(jnp.where(column < first + ROWS, done, 0.0))
-        recips.append(scale)
-        if p == PANELS - 1:
-            break
-        solved = [work[j] * recip[j] for j in range(ROWS)]
-        for j in range(ROWS - 1, -1, -1):
-            for i in range(j):
-                solved[i] = solved[i] - lower[j, i] * solved[j]
-        for i in range(p + 1, PANELS):
-            value = jnp.where(own, 0.0, rows[i])
-            for j in range(ROWS):
-                value = value - lane(rows[i], first + j) * solved[j]
-            rows[i] = value
+        after = list(range(p + WIDE, min(p + 2 * WIDE, PANELS)))
+        beyond = list(range(p + 2 * WIDE, PANELS))
+        own = (column >= first) & (column < first + size)
+        held = {
+            (m, t): lane(rows[p + t], first + m) for m in range(size) for t in range(m // ROWS, WIDE)
+        }
+        next_held = {(m, i): lane(rows[i], first + m) for m in range(size) for i in after}
+        work = [
+            jnp.where(own, (column - first - ROWS * t == line).astype(jnp.float32), rows[p + t])
+            for t in range(WIDE)
+        ]
+        following = {i: jnp.where(own, 0.0, rows[i]) for i in after}
+        scale = [None] * WIDE
+        for j in range(size):
+            home, at = divmod(j, ROWS)
+            pivot_row = row(work[home], at)
+            spread = {m: row(held[j, m // ROWS], m % ROWS) for m in range(j, size)}
+            recip = 1.0 / spread[j]
+            scale[home] = recip if at == 0 else jnp.where(line == at, recip, scale[home])
+            factor = {t: held[j, t] * recip for t in range(home, WIDE)}
+            for m in range(j + 1, size):
+                for t in range(m // ROWS, WIDE):
+                    if m == j + 1:
+                        held[m, t] = held[m, t] - (held[j, t] * spread[m]) * recip
+                    else:
+                        held[m, t] = held[m, t] - factor[t] * spread[m]
+            for t in range(home, WIDE):
+                part = jnp.where(line > at, factor[t], 0.0) if t == home else factor[t]
+                work[t] = work[t] - part * pivot_row
+            for i in after:
+                part = next_held[j, i] * recip
+                for m in range(j + 1, size):
+                    next_held[m, i] = next_held[m, i] - part * spread[m]
+                following[i] = following[i] - part * pivot_row
+        for t in range(WIDE):
+            inverse.append(jnp.where(column < first + size, work[t], 0.0))
+            recips.append(scale[t])
+        for i in after:
+            rows[i] = following[i]
+        if beyond:
+            panel = jnp.concatenate(work, axis=0)
+            scaled = jnp.concatenate([work[t] * scale[t] for t in range(WIDE)], axis=0)
+            change = contract(stack_left(scaled, 0), stack_right(panel, 0), 0)
+            for i in beyond:
+                change_tile = change[ROWS * i : ROWS * i + ROWS, :]
+                rows[i] = jnp.where(own, 0.0, rows[i]) - change_tile
     return inverse, recips
 
 
-def product(left, right, dims):
+def split(value):
+    high = value.astype(jnp.bfloat16)
+    rest = value - high.astype(jnp.float32)
+    middle = rest.astype(jnp.bfloat16)
+    return high, middle, (rest - middle.astype(jnp.float32)).astype(jnp.bfloat16)
+
+
+def stack_left(value, axis):
+    high, middle, low = split(value)
+    return jnp.concatenate([high, high, middle, middle, high, low], axis=axis)
+
+
+def stack_right(value, axis):
+    high, middle, low = split(value)
+    return jnp.concatenate([high, middle, high, middle, low, high], axis=axis)
+
+
+def contract(left, right, axis):
     return lax.dot_general(
-        left,
-        right,
-        (dims, ((), ())),
-        precision=lax.Precision.HIGHEST,
-        preferred_element_type=jnp.float32,
+        left, right, (((axis,), (0,)), ((), ())), preferred_element_type=jnp.float32
     )
 
 
@@ -136,7 +164,7 @@
     column = lax.broadcasted_iota(jnp.int32, (ROWS, GROUP), 1)
     line = lax.broadcasted_iota(jnp.int32, (ROWS, GROUP), 0)
 
-    def step(k, carry):
+    def step(k):
         panels = []
         for p in range(PANELS):
             ridge = jnp.where(column - ROWS * p == line, RIDGE, 0.0)
@@ -145,29 +173,28 @@
         for p in range(PANELS):
             low[k, ROWS * p : ROWS * p + ROWS, :] = inverse[p]
             rec[k, ROWS * p : ROWS * p + ROWS, :] = recips[p]
-        for now in range(blocks):
-
-            @pl.when(k == now)
-            def _():
-                tri = low[now]
-                rc = rec[now]
-                ys = {j: product(tri, gram[now, j], ((1,), (0,))) for j in range(now + 1, blocks + 1)}
-                zs = {j: ys[j] * rc for j in ys}
-                for j in zs:
-                    z[now, j] = zs[j]
-                for i in range(now + 1, blocks):
-                    for j in range(i, blocks + 1):
-                        gram[i, j] = gram[i, j] - product(ys[i], zs[j], ((0,), (0,)))
-
-        return carry
-
-    lax.fori_loop(0, blocks, step, 0)
+        tri = stack_left(low[k], 1)
+        later = range(k + 1, blocks + 1)
+        ys = {j: contract(tri, stack_right(gram[k, j], 0), 1) for j in later}
+        zs = {j: ys[j] * rec[k] for j in later}
+        for j in later:
+            z[k, j] = zs[j]
+        right = {j: stack_right(zs[j], 0) for j in later}
+        for i in range(k + 1, blocks):
+            left = stack_left(ys[i], 0)
+            for j in range(i, blocks + 1):
+                gram[i, j] = gram[i, j] - contract(left, right[j], 0)
+
+    for k in range(blocks):
+        step(k)
     xs = [None] * blocks
+    spread = [None] * blocks
     for k in range(blocks - 1, -1, -1):
         right = z[k, blocks]
         for j in range(k + 1, blocks):
-            right = right - product(z[k, j], xs[j], ((1,), (0,)))
-        xs[k] = product(low[k], right, ((0,), (0,)))
+            right = right - contract(stack_left(z[k, j], 1), spread[j], 1)
+        xs[k] = contract(stack_left(low[k], 0), stack_right(right, 0), 0)
+        spread[k] = stack_right(xs[k], 0)
         coeff_ref[GROUP * k : GROUP * k + GROUP, :] = xs[k]
     width = cent_ref.shape[1]
     for piece in range(width // GROUP):

time: 87.2 us -> 77.9 us (0.89)
  Pallas kernels: 24.6 us -> 15.4 us
    pallas_call x1, Pallas kernels: 23 us -> 13.8 us  [solve(): pl.pallas_call(solve_kernel, out_shape=(jax.ShapeDtypeStruct((4 * GROUP,...]
where the time goes in v3:
time: 77.9 us; the launch traced here: 77.7 us
  blocking collectives  41.5 us (53%)
  Pallas kernels  15.4 us (20%)
  waiting for transfers between devices  12.5 us (16%)
  starting transfers between devices  5.04 us (6%)
  local copies, waits for them, and re-layouts  1.89 us (2%)
    all_to_all x1, blocking collectives, per_device(): lax.all_to_all(partial, ring, split_axis=0, concat_axis=0, tiled=True)  24.5 us
    all_to_all x1, blocking collectives, per_device(): lax.all_to_all(jnp.broadcast_to(summed[None], parts.shape), ring, split_a...  17 us
    pallas_call x1, Pallas kernels, solve(): pl.pallas_call(solve_kernel, out_shape=(jax.ShapeDtypeStruct((4 * GROUP,...  13.8 us
    ppermute x1, waiting for transfers between devices, per_device(): far = lax.ppermute(send, 'high', SWAP)  6.3 us
    ppermute x1, starting transfers between devices, per_device(): far = lax.ppermute(send, 'high', SWAP)  3.36 us
    ppermute x1, waiting for transfers between devices, per_device(): away = lax.ppermute(update, 'high', SWAP)  2.89 us
    ppermute x1, waiting for transfers between devices, per_device(): other = lax.ppermute(mine, 'core', SWAP)  1.91 us
    ppermute x1, starting transfers between devices, per_device(): away = lax.ppermute(update, 'high', SWAP)  1.68 us
  transfers between devices with their start and end apart: 5, of which 4 were waited for; matrix products, arithmetic and copies ran while one was open for 1% of the time, Pallas kernels for 0%

profile of v3, /device:TPU:0, one launch (start us, length us, event | category | flops | bytes accessed | tf_op | source)
XLA Modules:
  0.0 77.7 jit_solution(16669850365997448425)
XLA Ops:
  0.6 1.1 %constant_dynamic-slice_fusion = (bf16[128,1024]{1,0:T(8,128)(2,1)S(1)}, bf16[128,1024]{1,0:T(8,128)(2,1)S(1)}) fusion(bf16[128,2048]{1,0:T(8,128)(2,1)} %param.2, s32[]{:T(128)S(6)} %select_n.23, s32[]{:T(128)S(6)} %select_n.22), kind=kLoop, calls=%fused_computation.5 | loop fusion | bytes 1048584 | tf_op jit(solution)/shard_map/dynamic_slice | solution.py:260
  1.7 3.4 %collective-permute-start = (bf16[128,1024]{1,0:T(8,128)(2,1)S(1)}, bf16[128,1024]{1,0:T(8,128)(2,1)S(1)}, u32[]{:S(2)}, u32[]{:S(2)}) collective-permute-start(bf16[128,1024]{1,0:T(8,128)(2,1)S(1)} %get-tuple-element.10), channel_id=1, source_target_pairs={{0,64},{64,0},{1,65},{65,1},{2,66},{66,2},{3,67},{67,3},{4,68},{68... | collective-permute-start | bytes 786440 | tf_op jit(solution)/shard_map/ppermute | solution.py:261
  5.1 0.0 collective-permute-start.1
  5.1 6.3 %collective-permute-done.b_ref = bf16[128,1024]{1,0:T(8,128)(2,1)S(1)} collective-permute-done((bf16[128,1024]{1,0:T(8,128)(2,1)S(1)}, bf16[128,1024]{1,0:T(8,128)(2,1)S(1)}, u32[]{:S(2)}, u32[]{:S(2)}) %collective-permute-start) | collective-permute-done | bytes 262176 | tf_op jit(solution)/shard_map/ppermute | solution.py:261
  11.4 0.0 collective-permute-start.2
  11.4 0.0 copy-start
  11.4 0.1 stack.31.place_ref
  11.5 0.0 collective-permute-done.1.c_ref
  11.5 1.4 %collective-permute-done.2.d_ref = bf16[128,1024]{1,0:T(8,128)(2,1)S(1)} collective-permute-done((bf16[128,1024]{1,0:T(8,128)(2,1)S(1)}, bf16[128,1024]{1,0:T(8,128)(2,1)S(1)}, u32[]{:S(2)}, u32[]{:S(2)}) %collective-permute-start.2) | collective-permute-done | bytes 262176 | tf_op jit(solution)/shard_map/ppermute | solution.py:263
  12.9 0.0 copy-done
  12.9 0.1 broadcast_in_dim.4.e_ref
  13.0 1.6 %center_gram.1 = (bf16[512,1024]{1,0:T(8,128)(2,1)S(1)}, f32[64,8,256]{2,1,0:T(8,128)S(1)}) custom-call(s32[7]{0:T(128)S(1)} %stack.31.place_ref, f32[128,128]{1,0:T(8,128)S(1)} %broadcast_in_dim.4.e_ref, bf16[128,1024]{1,0:T(8,128)(2,1)S(1)} %get-tuple-element.11.a_ref, bf16[128,1024]{1,0:T(8,128)(2,1)S(1)} %collective-permute-done.b_ref, ...), custom_call_target="tpu_custom_call" | custom-call | tf_op jit(solution)/shard_map/center_gram/pallas_call | solution.py:219
  14.6 24.5 %all_to_all.10 = f32[64,8,256]{2,1,0:T(8,128)S(1)} all-to-all(f32[64,8,256]{2,1,0:T(8,128)S(1)} %get-tuple-element.6), channel_id=1, replica_groups=mesh['high'=2,'core'=2,'par'=32] {'high','par'}, dimensions={0} | all-to-all | bytes 1048576 | tf_op jit(solution)/shard_map/all_to_all | solution.py:278
  39.1 0.1 reduce_sum.9
  39.2 17.0 %all_to_all.11.mine_ref = f32[64,8,256]{2,1,0:T(8,128)S(1)} all-to-all(f32[64,8,256]{2,1,0:T(8,128)S(1)} %broadcast_in_dim.5), channel_id=1, replica_groups=mesh['high'=2,'core'=2,'par'=32] {'high','par'}, dimensions={0} | all-to-all | bytes 1048576 | tf_op jit(solution)/shard_map/all_to_all | solution.py:280
  56.2 0.0 collective-permute-start.3
  56.2 1.9 %collective-permute-done.3.other_ref = f32[64,8,256]{2,1,0:T(8,128)S(1)} collective-permute-done((f32[64,8,256]{2,1,0:T(8,128)S(1)}, f32[64,8,256]{2,1,0:T(8,128)S(1)}, u32[]{:S(2)}, u32[]{:S(2)}) %collective-permute-start.3) | collective-permute-done | bytes 524320 | tf_op jit(solution)/shard_map/ppermute | solution.py:283
  58.1 13.8 %solve.1 = (f32[512,128]{1,0:T(8,128)S(1)}, f32[1,1024]{1,0:T(1,128)S(1)}) custom-call(s32[7]{0:T(128)S(1)} %stack.31.place_ref, f32[64,8,256]{2,1,0:T(8,128)S(1)} %all_to_all.11.mine_ref, f32[64,8,256]{2,1,0:T(8,128)S(1)} %collective-permute-done.3.other_ref, bf16[512,1024]{1,0:T(8,128)(2,1)S(1)} %get-tuple-element.7.cent_ref), custom_call_target="tpu_custom_call" | custom-call | tf_op jit(solution)/shard_map/solve/pallas_call | solution.py:233
  71.9 1.7 %collective-permute-start.4 = (f32[1024]{0:T(1024)S(1)}, f32[1024]{0:T(1024)S(1)}, u32[]{:S(2)}, u32[]{:S(2)}) collective-permute-start(f32[1024]{0:T(1024)S(1)} %bitcast.8), channel_id=1, source_target_pairs={{0,64},{64,0},{1,65},{65,1},{2,66},{66,2},{3,67},{67,3},{4,68},{68... | collective-permute-start | bytes 12296 | tf_op jit(solution)/shard_map/ppermute | solution.py:287
  73.6 0.6 dynamic-slice_reduce_fusion
  74.2 2.9 %collective-permute-done.4 = f32[1024]{0:T(1024)S(1)} collective-permute-done((f32[1024]{0:T(1024)S(1)}, f32[1024]{0:T(1024)S(1)}, u32[]{:S(2)}, u32[]{:S(2)}) %collective-permute-start.4) | collective-permute-done | bytes 4128 | tf_op jit(solution)/shard_map/ppermute | solution.py:287
  77.1 0.6 pad_maximum_fusion
  (3 shorter events, 0.0 us)
Async XLA Ops:
  1.7 9.7 %collective-permute-start = (bf16[128,1024]{1,0:T(8,128)(2,1)S(1)}, bf16[128,1024]{1,0:T(8,128)(2,1)S(1)}, u32[]{:S(2)}, u32[]{:S(2)}) collective-permute-start(bf16[128,1024]{1,0:T(8,128)(2,1)S(1)} %get-tuple-element.10), channel_id=1, source_target_pairs={{0,64},{64,0},{1,65},{65,1},{2,66},{66,2},{3,67},{67,3},{4,68},{68... | collective-permute-start | bytes 786440 | tf_op jit(solution)/shard_map/ppermute | solution.py:261
  5.1 6.4 %collective-permute-start.1 = (bf16[128,1024]{1,0:T(8,128)(2,1)S(1)}, bf16[128,1024]{1,0:T(8,128)(2,1)S(1)}, u32[]{:S(2)}, u32[]{:S(2)}) collective-permute-start(bf16[128,1024]{1,0:T(8,128)(2,1)S(1)} %get-tuple-element.11.a_ref), channel_id=1, source_target_pairs={{0,32},{32,0},{1,33},{33,1},{2,34},{34,2},{3,35},{35,3},{4,36},{36... | collective-permute-start | bytes 786440 | tf_op jit(solution)/shard_map/ppermute | solution.py:262
  11.4 1.5 %collective-permute-start.2 = (bf16[128,1024]{1,0:T(8,128)(2,1)S(1)}, bf16[128,1024]{1,0:T(8,128)(2,1)S(1)}, u32[]{:S(2)}, u32[]{:S(2)}) collective-permute-start(bf16[128,1024]{1,0:T(8,128)(2,1)S(1)} %collective-permute-done.b_ref), channel_id=1, source_target_pairs={{0,32},{32,0},{1,33},{33,1},{2,34},{34,2},{3,35},{35,3},{4,36},{36... | collective-permute-start | bytes 786440 | tf_op jit(solution)/shard_map/ppermute | solution.py:263
  11.4 1.5 %copy-start = (f32[128]{0:T(128)S(1)}, f32[128]{0:T(128)}, u32[]{:S(2)}) copy-start(f32[128]{0:T(128)} %param.3) | copy-start | bytes 1540
  56.2 1.9 %collective-permute-start.3 = (f32[64,8,256]{2,1,0:T(8,128)S(1)}, f32[64,8,256]{2,1,0:T(8,128)S(1)}, u32[]{:S(2)}, u32[]{:S(2)}) collective-permute-start(f32[64,8,256]{2,1,0:T(8,128)S(1)} %all_to_all.11.mine_ref), channel_id=1, source_target_pairs={{0,32},{32,0},{1,33},{33,1},{2,34},{34,2},{3,35},{35,3},{4,36},{36... | collective-permute-start | bytes 1572872 | tf_op jit(solution)/shard_map/ppermute | solution.py:283
  71.9 5.2 %collective-permute-start.4 = (f32[1024]{0:T(1024)S(1)}, f32[1024]{0:T(1024)S(1)}, u32[]{:S(2)}, u32[]{:S(2)}) collective-permute-start(f32[1024]{0:T(1024)S(1)} %bitcast.8), channel_id=1, source_target_pairs={{0,64},{64,0},{1,65},{65,1},{2,66},{66,2},{3,67},{67,3},{4,68},{68... | collective-permute-start | bytes 12296 | tf_op jit(solution)/shard_map/ppermute | solution.py:287

commit v4 on v3

--- a/solution.py
+++ b/solution.py
@@ -14,8 +14,14 @@
 RIDGE = 0.05
 
 
+BLOCKS = 4
+STRIPS = (((0, 0, 4), (1, 1, 1)), ((1, 2, 2), (2, 2, 2), (3, 3, 1)))
+LISTS = tuple(tuple((r, c + n) for r, c, w in strips for n in range(w)) for strips in STRIPS)
+HELD = len(LISTS[0]) + 1
+
+
 def center_gram_kernel(place_ref, e_ref, a_ref, b_ref, c_ref, d_ref, cent_ref, out_ref):
-    total = 4 * GROUP
+    total = BLOCKS * GROUP
     scale = 1.0 / math.sqrt(total)
     parts = (a_ref, b_ref, c_ref, d_ref)
     column_sum = None
@@ -28,24 +34,25 @@
         cent_ref[pl.ds(start, GROUP), :] = (
             (part[...].astype(jnp.float32) - mean) * scale
         ).astype(jnp.bfloat16)
-    half = total // 2
-    start = pl.multiple_of(place_ref[4] * half, half)
-    gram = lax.dot_general(
-        cent_ref[pl.ds(start, half), :],
-        cent_ref[...],
-        (((1,), (1,)), ((), ())),
-        preferred_element_type=jnp.float32,
-    )
-    for strip in range(half // ROWS):
-        for side in range(2):
-            out_ref[2 * strip + side] = gram[
-                ROWS * strip : ROWS * strip + ROWS, half * side : half * side + half
-            ]
-    column = lax.broadcasted_iota(jnp.int32, (ROWS, GROUP), 1)
+    for core, strips in enumerate(STRIPS):
+
+        @pl.when(place_ref[4] == core)
+        def _():
+            at = 0
+            for r, c, wide in strips:
+                strip = lax.dot_general(
+                    cent_ref[GROUP * r : GROUP * r + GROUP, :],
+                    cent_ref[GROUP * c : GROUP * (c + wide), :],
+                    (((1,), (1,)), ((), ())),
+                    preferred_element_type=jnp.float32,
+                )
+                for n in range(wide):
+                    out_ref[at : at + GROUP, :] = strip[:, GROUP * n : GROUP * n + GROUP]
+                    at += GROUP
+
+    column = lax.broadcasted_iota(jnp.int32, (GROUP, GROUP), 1)
     mine = (column // (GROUP // 2) == place_ref[5]) & (place_ref[6] == 0)
-    for strip in range(PANELS):
-        energies = e_ref[ROWS * strip : ROWS * strip + ROWS, :]
-        out_ref[2 * (PANELS + strip), :, :GROUP] = jnp.where(mine, energies, 0.0)
+    out_ref[GROUP * (HELD - 1) :, :] = jnp.where(mine, e_ref[...], 0.0)
 
 
 def lane(value, index):
@@ -136,26 +143,25 @@
     )
 
 
-def solve_kernel(
-    place_ref, mine_ref, other_ref, cent_ref, coeff_ref, update_ref, gram, low, rec, z
-):
-    blocks = 4
-    core = place_ref[4]
-    for strip in range(2 * PANELS):
-        for side in range(2):
-            for which, ref in ((core, mine_ref), (1 - core, other_ref)):
-                block_row = 2 * which + strip // PANELS
-                inner = ROWS * (strip % PANELS)
-                for part in range(2):
-                    gram[block_row, 2 * side + part, inner : inner + ROWS, :] = ref[
-                        2 * strip + side, :, GROUP * part : GROUP * part + GROUP
-                    ]
+def solve_kernel(place_ref, parts_ref, cent_ref, coeff_ref, update_ref, gram, low, rec, z):
+    blocks = BLOCKS
+    tiles = parts_ref.shape[1] // (2 * ROWS)
+
+    def tile(core, block, p):
+        number = PANELS * block + p
+        start = ROWS * (core * tiles + number % tiles)
+        return parts_ref[number // tiles, start : start + ROWS, :]
+
+    for core, held in enumerate(LISTS):
+        for n, (r, c) in enumerate(held):
+            for p in range(PANELS):
+                gram[r, c, ROWS * p : ROWS * p + ROWS, :] = tile(core, n, p)
     energy_sum = jnp.zeros((ROWS, GROUP), jnp.float32)
-    for which, ref in ((core, mine_ref), (1 - core, other_ref)):
+    for core in range(2):
         for high in range(2):
             for p in range(PANELS):
-                value = lane(ref[2 * (PANELS + p), :, :GROUP], high * GROUP // 2)
-                gram[2 * high + which, blocks, ROWS * p : ROWS * p + ROWS, :] = value
+                value = lane(tile(core, HELD - 1, p), high * GROUP // 2)
+                gram[2 * high + core, blocks, ROWS * p : ROWS * p + ROWS, :] = value
                 energy_sum = energy_sum + value
     energy_mean = jnp.sum(energy_sum, axis=0, keepdims=True) / (blocks * GROUP)
     scale = 1.0 / math.sqrt(blocks * GROUP)
@@ -219,8 +225,8 @@
     return pl.pallas_call(
         center_gram_kernel,
         out_shape=(
-            jax.ShapeDtypeStruct((4 * GROUP, columns), jnp.bfloat16),
-            jax.ShapeDtypeStruct((64, ROWS, 2 * GROUP), jnp.float32),
+            jax.ShapeDtypeStruct((BLOCKS * GROUP, columns), jnp.bfloat16),
+            jax.ShapeDtypeStruct((HELD * GROUP, GROUP), jnp.float32),
         ),
         in_specs=[SMEM] + [VMEM] * 5,
         out_specs=(VMEM, VMEM),
@@ -229,14 +235,14 @@
     )(place, energies, *parts)
 
 
-def solve(place, mine, other, cent):
+def solve(place, parts, cent):
     return pl.pallas_call(
         solve_kernel,
         out_shape=(
-            jax.ShapeDtypeStruct((4 * GROUP, GROUP), jnp.float32),
+            jax.ShapeDtypeStruct((BLOCKS * GROUP, GROUP), jnp.float32),
             jax.ShapeDtypeStruct((1, cent.shape[1]), jnp.float32),
         ),
-        in_specs=[SMEM] + [VMEM] * 3,
+        in_specs=[SMEM] + [VMEM] * 2,
         out_specs=(VMEM, VMEM),
         scratch_shapes=[
             pltpu.VMEM((4, 5, GROUP, GROUP), jnp.float32),
@@ -246,7 +252,7 @@
         ],
         compiler_params=pltpu.CompilerParams(vmem_limit_bytes=32 * 1024 * 1024),
         name="solve",
-    )(place, mine, other, cent)
+    )(place, parts, cent)
 
 
 SWAP = [(0, 1), (1, 0)]
@@ -269,21 +275,37 @@
             2 * (1 - high) + 1 - core,
             core,
             high,
-            lax.axis_index("par"),
+            lax.axis_index(("z", "x", "low")),
         ]
     ).astype(jnp.int32)
     spread = jnp.broadcast_to(energies[:, None], (GROUP, GROUP))
     cent, partial = center_gram(place, spread, (keep, far, near, diagonal))
-    ring = ("high", "par")
-    parts = lax.all_to_all(partial, ring, split_axis=0, concat_axis=0, tiled=True)
-    summed = jnp.sum(parts, axis=0)
-    mine = lax.all_to_all(
-        jnp.broadcast_to(summed[None], parts.shape), ring, split_axis=0, concat_axis=0, tiled=True
-    )
-    other = lax.ppermute(mine, "core", SWAP)
-    coeffs, update = solve(place, mine, other, cent)
+    plane = ("high", "x", "low")
+    peers = lax.axis_size(plane)
+    parts = lax.all_to_all(
+        partial.reshape(peers, -1, GROUP), plane, split_axis=0, concat_axis=0, tiled=True
+    )
+    chunk = jnp.sum(parts, axis=0)
+    ring = lax.axis_size("z")
+    one, two, three = (
+        lax.ppermute(chunk, "z", [(n, (n + step) % ring) for n in range(ring)])
+        for step in range(1, ring)
+    )
+    chunk = (chunk + two) + (one + three)
+    other = lax.ppermute(chunk, "core", SWAP)
+    pair = jnp.concatenate(
+        [jnp.where(core == 0, chunk, other), jnp.where(core == 0, other, chunk)], axis=0
+    )
+    blocks = lax.all_to_all(
+        jnp.broadcast_to(pair[None], (peers, *pair.shape)),
+        plane,
+        split_axis=0,
+        concat_axis=0,
+        tiled=True,
+    )
+    coeffs, update = solve(place, blocks, cent)
     own = lax.dynamic_slice_in_dim(coeffs, (2 * high + core) * GROUP, GROUP, 0)[:, 0]
-    update = update[0] * math.sqrt(2 * half * lax.axis_size("par"))
+    update = update[0] * math.sqrt(2 * half * lax.axis_size(("z", "x", "low")))
     away = lax.ppermute(update, "high", SWAP)
     lower = jnp.where(high == 0, update, away)
     upper = jnp.where(high == 0, away, update)
@@ -291,12 +313,12 @@
 
 
 def solution(mesh):
-    shape = mesh.devices.shape
-    fine = Mesh(mesh.devices.reshape(2, 2, shape[1]), ("high", "core", "par"))
+    fine = Mesh(mesh.devices.reshape(2, 2, 4, 4, 2), ("high", "core", "z", "x", "low"))
+    samples, params = ("high", "core"), ("z", "x", "low")
     return jax.shard_map(
         per_device,
         mesh=fine,
-        in_specs=(P(("high", "core"), "par"), P(("high", "core"))),
-        out_specs=(P("par"), P(("high", "core"))),
+        in_specs=(P(samples, params), P(samples)),
+        out_specs=(P(params), P(samples)),
         check_vma=False,
     )

time: 77.9 us -> 80.1 us (1.028)
  blocking collectives: 41.5 us -> 35 us
  starting transfers between devices: 5.04 us -> 11 us
  waiting for transfers between devices: 12.5 us -> 15.4 us
    all_to_all x2, blocking collectives: 41.5 us -> 35 us  [the longest x1 18 us: per_device(): lax.all_to_all(jnp.broadcast_to(pair[None], (peers, *pair.shape)), plane,...]
    ppermute x1 -> x4, starting transfers between devices: 0.01 us -> 6.05 us  [the longest x3 5.97 us: per_device(): lax.ppermute(chunk, 'z', [(n, (n + step) % ring) for n in range(ring)])]
    ppermute x1 -> x4, waiting for transfers between devices: 1.91 us -> 4.65 us  [the longest x3 3.47 us: per_device(): lax.ppermute(chunk, 'z', [(n, (n + step) % ring) for n in range(ring)])]
  transfers between devices with their start and end apart: 5 -> 8, of which waited for: 4 -> 6; matrix products, arithmetic and copies ran while one was open for 1% -> 1% of each run, Pallas kernels for 0% -> 0%
where the time goes in v4:
time: 80.1 us; the launch traced here: 79.9 us
  blocking collectives  35 us (44%)
  waiting for transfers between devices  15.4 us (19%)
  Pallas kernels  15.2 us (19%)
  starting transfers between devices  11 us (14%)
  local copies, waits for them, and re-layouts  1.92 us (2%)
    all_to_all x1, blocking collectives, per_device(): lax.all_to_all(jnp.broadcast_to(pair[None], (peers, *pair.shape)), plane,...  18 us
    all_to_all x1, blocking collectives, per_device(): lax.all_to_all(partial.reshape(peers, -1, GROUP), plane, split_axis=0, co...  17 us
    pallas_call x1, Pallas kernels, solve(): pl.pallas_call(solve_kernel, out_shape=(jax.ShapeDtypeStruct((BLOCKS * GR...  13.6 us
    ppermute x1, waiting for transfers between devices, per_device(): far = lax.ppermute(send, 'high', SWAP)  6.3 us
    ppermute x3, starting transfers between devices, per_device(): lax.ppermute(chunk, 'z', [(n, (n + step) % ring) for n in range(ring)])  5.97 us
    ppermute x3, waiting for transfers between devices, per_device(): lax.ppermute(chunk, 'z', [(n, (n + step) % ring) for n in range(ring)])  3.47 us
    ppermute x1, starting transfers between devices, per_device(): far = lax.ppermute(send, 'high', SWAP)  3.36 us
    ppermute x1, waiting for transfers between devices, per_device(): away = lax.ppermute(update, 'high', SWAP)  3.02 us
  transfers between devices with their start and end apart: 8, of which 6 were waited for; matrix products, arithmetic and copies ran while one was open for 1% of the time, Pallas kernels for 0%

profile of v4, /device:TPU:0, one launch (start us, length us, event | category | flops | bytes accessed | tf_op | source)
XLA Modules:
  0.0 79.9 jit_solution(1085883304458589900)
XLA Ops:
  0.6 1.1 %constant_dynamic-slice_fusion = (bf16[128,1024]{1,0:T(8,128)(2,1)S(1)}, bf16[128,1024]{1,0:T(8,128)(2,1)S(1)}) fusion(bf16[128,2048]{1,0:T(8,128)(2,1)} %param.2, s32[]{:T(128)S(6)} %select_n.36, s32[]{:T(128)S(6)} %select_n.35), kind=kLoop, calls=%fused_computation.9 | loop fusion | bytes 1048584 | tf_op jit(solution)/shard_map/dynamic_slice | solution.py:266
  1.7 3.4 %collective-permute-start = (bf16[128,1024]{1,0:T(8,128)(2,1)S(1)}, bf16[128,1024]{1,0:T(8,128)(2,1)S(1)}, u32[]{:S(2)}, u32[]{:S(2)}) collective-permute-start(bf16[128,1024]{1,0:T(8,128)(2,1)S(1)} %get-tuple-element.10), channel_id=1, source_target_pairs={{0,64},{64,0},{1,65},{65,1},{2,66},{66,2},{3,67},{67,3},{4,68},{68... | collective-permute-start | bytes 786440 | tf_op jit(solution)/shard_map/ppermute | solution.py:267
  5.1 6.3 %collective-permute-done.b_ref = bf16[128,1024]{1,0:T(8,128)(2,1)S(1)} collective-permute-done((bf16[128,1024]{1,0:T(8,128)(2,1)S(1)}, bf16[128,1024]{1,0:T(8,128)(2,1)S(1)}, u32[]{:S(2)}, u32[]{:S(2)}) %collective-permute-start) | collective-permute-done | bytes 262176 | tf_op jit(solution)/shard_map/ppermute | solution.py:267
  11.4 0.0 collective-permute-start.2
  11.4 0.1 stack.31.place_ref
  11.5 0.0 collective-permute-done.1.c_ref
  11.5 1.4 %collective-permute-done.2.d_ref = bf16[128,1024]{1,0:T(8,128)(2,1)S(1)} collective-permute-done((bf16[128,1024]{1,0:T(8,128)(2,1)S(1)}, bf16[128,1024]{1,0:T(8,128)(2,1)S(1)}, u32[]{:S(2)}, u32[]{:S(2)}) %collective-permute-start.2) | collective-permute-done | bytes 262176 | tf_op jit(solution)/shard_map/ppermute | solution.py:269
  12.9 0.1 broadcast_in_dim.4.e_ref
  13.0 1.6 %center_gram.1 = (bf16[512,1024]{1,0:T(8,128)(2,1)S(1)}, f32[768,128]{1,0:T(8,128)S(1)}) custom-call(s32[7]{0:T(128)S(1)} %stack.31.place_ref, f32[128,128]{1,0:T(8,128)S(1)} %broadcast_in_dim.4.e_ref, bf16[128,1024]{1,0:T(8,128)(2,1)S(1)} %get-tuple-element.11.a_ref, bf16[128,1024]{1,0:T(8,128)(2,1)S(1)} %collective-permute-done.b_ref, ...), custom_call_target="tpu_custom_call" | custom-call | tf_op jit(solution)/shard_map/center_gram/pallas_call | solution.py:225
  14.6 17.0 %all_to_all.10 = f32[16,48,128]{2,1,0:T(8,128)S(1)} all-to-all(f32[16,48,128]{2,1,0:T(8,128)S(1)} %bitcast.9), channel_id=1, replica_groups=mesh['high'=2,'core'=2,'z'=4,'x'=4,'low'=2] {'high','x','low'}, dimensions={0} | all-to-all | bytes 786432 | tf_op jit(solution)/shard_map/all_to_all | solution.py:285
  31.6 4.1 %collective-permute-start.5 = (f32[48,128]{1,0:T(8,128)S(1)}, f32[48,128]{1,0:T(8,128)S(1)}, u32[]{:S(2)}, u32[]{:S(2)}) collective-permute-start(f32[48,128]{1,0:T(8,128)S(1)} %reduce_sum.9), channel_id=1, source_target_pairs={{0,24},{8,0},{16,8},{24,16},{1,25},{9,1},{17,9},{25,17},{2,26},{10... | collective-permute-start | bytes 73736 | tf_op jit(solution)/shard_map/ppermute | solution.py:291
  35.7 0.0 collective-permute-start.4
  35.7 1.9 %collective-permute-start.3 = (f32[48,128]{1,0:T(8,128)S(1)}, f32[48,128]{1,0:T(8,128)S(1)}, u32[]{:S(2)}, u32[]{:S(2)}) collective-permute-start(f32[48,128]{1,0:T(8,128)S(1)} %reduce_sum.9), channel_id=1, source_target_pairs={{0,16},{8,24},{16,0},{24,8},{1,17},{9,25},{17,1},{25,9},{2,18},{10... | collective-permute-start | bytes 73736 | tf_op jit(solution)/shard_map/ppermute | solution.py:291
  37.6 3.2 %collective-permute-done.4 = f32[48,128]{1,0:T(8,128)S(1)} collective-permute-done((f32[48,128]{1,0:T(8,128)S(1)}, f32[48,128]{1,0:T(8,128)S(1)}, u32[]{:S(2)}, u32[]{:S(2)}) %collective-permute-start.4) | collective-permute-done | bytes 24608 | tf_op jit(solution)/shard_map/ppermute | solution.py:291
  40.8 0.3 collective-permute-done.3
  41.1 0.1 collective-permute-start.6
  41.2 1.2 %collective-permute-done.6 = f32[48,128]{1,0:T(8,128)S(1)} collective-permute-done((f32[48,128]{1,0:T(8,128)S(1)}, f32[48,128]{1,0:T(8,128)S(1)}, u32[]{:S(2)}, u32[]{:S(2)}) %collective-permute-start.6) | collective-permute-done | bytes 24608 | tf_op jit(solution)/shard_map/ppermute | solution.py:295
  42.3 0.1 broadcast_in_dim.5
  42.4 18.0 %all_to_all.11.parts_ref = f32[16,96,128]{2,1,0:T(8,128)S(1)} all-to-all(f32[16,96,128]{2,1,0:T(8,128)S(1)} %broadcast_in_dim.5), channel_id=1, replica_groups=mesh['high'=2,'core'=2,'z'=4,'x'=4,'low'=2] {'high','x','low'}, dimensions={0} | all-to-all | bytes 1572864 | tf_op jit(solution)/shard_map/all_to_all | solution.py:299
  60.4 13.6 %solve.1 = (f32[512,128]{1,0:T(8,128)S(1)}, f32[1,1024]{1,0:T(1,128)S(1)}) custom-call(s32[7]{0:T(128)S(1)} %stack.31.place_ref, f32[16,96,128]{2,1,0:T(8,128)S(1)} %all_to_all.11.parts_ref, bf16[512,1024]{1,0:T(8,128)(2,1)S(1)} %get-tuple-element.7.cent_ref), custom_call_target="tpu_custom_call" | custom-call | tf_op jit(solution)/shard_map/solve/pallas_call | solution.py:239
  74.1 1.5 %collective-permute-start.7 = (f32[1024]{0:T(1024)S(1)}, f32[1024]{0:T(1024)S(1)}, u32[]{:S(2)}, u32[]{:S(2)}) collective-permute-start(f32[1024]{0:T(1024)S(1)} %bitcast.10), channel_id=1, source_target_pairs={{0,64},{64,0},{1,65},{65,1},{2,66},{66,2},{3,67},{67,3},{4,68},{68... | collective-permute-start | bytes 12296 | tf_op jit(solution)/shard_map/ppermute | solution.py:309
  75.6 0.6 dynamic-slice_reduce_fusion
  76.2 3.0 %collective-permute-done.7 = f32[1024]{0:T(1024)S(1)} collective-permute-done((f32[1024]{0:T(1024)S(1)}, f32[1024]{0:T(1024)S(1)}, u32[]{:S(2)}, u32[]{:S(2)}) %collective-permute-start.7) | collective-permute-done | bytes 4128 | tf_op jit(solution)/shard_map/ppermute | solution.py:309
  79.3 0.6 pad_maximum_fusion.1
  (10 shorter events, 0.1 us)
Async XLA Ops:
  1.7 9.7 %collective-permute-start = (bf16[128,1024]{1,0:T(8,128)(2,1)S(1)}, bf16[128,1024]{1,0:T(8,128)(2,1)S(1)}, u32[]{:S(2)}, u32[]{:S(2)}) collective-permute-start(bf16[128,1024]{1,0:T(8,128)(2,1)S(1)} %get-tuple-element.10), channel_id=1, source_target_pairs={{0,64},{64,0},{1,65},{65,1},{2,66},{66,2},{3,67},{67,3},{4,68},{68... | collective-permute-start | bytes 786440 | tf_op jit(solution)/shard_map/ppermute | solution.py:267
  5.1 6.4 %collective-permute-start.1 = (bf16[128,1024]{1,0:T(8,128)(2,1)S(1)}, bf16[128,1024]{1,0:T(8,128)(2,1)S(1)}, u32[]{:S(2)}, u32[]{:S(2)}) collective-permute-start(bf16[128,1024]{1,0:T(8,128)(2,1)S(1)} %get-tuple-element.11.a_ref), channel_id=1, source_target_pairs={{0,32},{32,0},{1,33},{33,1},{2,34},{34,2},{3,35},{35,3},{4,36},{36... | collective-permute-start | bytes 786440 | tf_op jit(solution)/shard_map/ppermute | solution.py:268
  11.4 1.5 %collective-permute-start.2 = (bf16[128,1024]{1,0:T(8,128)(2,1)S(1)}, bf16[128,1024]{1,0:T(8,128)(2,1)S(1)}, u32[]{:S(2)}, u32[]{:S(2)}) collective-permute-start(bf16[128,1024]{1,0:T(8,128)(2,1)S(1)} %collective-permute-done.b_ref), channel_id=1, source_target_pairs={{0,32},{32,0},{1,33},{33,1},{2,34},{34,2},{3,35},{35,3},{4,36},{36... | collective-permute-start | bytes 786440 | tf_op jit(solution)/shard_map/ppermute | solution.py:269
  11.4 1.5 %copy-start = (f32[128]{0:T(128)S(1)}, f32[128]{0:T(128)}, u32[]{:S(2)}) copy-start(f32[128]{0:T(128)} %param.3) | copy-start | bytes 1540
  31.6 6.0 %collective-permute-start.5 = (f32[48,128]{1,0:T(8,128)S(1)}, f32[48,128]{1,0:T(8,128)S(1)}, u32[]{:S(2)}, u32[]{:S(2)}) collective-permute-start(f32[48,128]{1,0:T(8,128)S(1)} %reduce_sum.9), channel_id=1, source_target_pairs={{0,24},{8,0},{16,8},{24,16},{1,25},{9,1},{17,9},{25,17},{2,26},{10... | collective-permute-start | bytes 73736 | tf_op jit(solution)/shard_map/ppermute | solution.py:291
  35.7 5.0 %collective-permute-start.4 = (f32[48,128]{1,0:T(8,128)S(1)}, f32[48,128]{1,0:T(8,128)S(1)}, u32[]{:S(2)}, u32[]{:S(2)}) collective-permute-start(f32[48,128]{1,0:T(8,128)S(1)} %reduce_sum.9), channel_id=1, source_target_pairs={{0,8},{8,16},{16,24},{24,0},{1,9},{9,17},{17,25},{25,1},{2,10},{10... | collective-permute-start | bytes 73736 | tf_op jit(solution)/shard_map/ppermute | solution.py:291
  35.7 5.3 %collective-permute-start.3 = (f32[48,128]{1,0:T(8,128)S(1)}, f32[48,128]{1,0:T(8,128)S(1)}, u32[]{:S(2)}, u32[]{:S(2)}) collective-permute-start(f32[48,128]{1,0:T(8,128)S(1)} %reduce_sum.9), channel_id=1, source_target_pairs={{0,16},{8,24},{16,0},{24,8},{1,17},{9,25},{17,1},{25,9},{2,18},{10... | collective-permute-start | bytes 73736 | tf_op jit(solution)/shard_map/ppermute | solution.py:291
  41.1 1.3 %collective-permute-start.6 = (f32[48,128]{1,0:T(8,128)S(1)}, f32[48,128]{1,0:T(8,128)S(1)}, u32[]{:S(2)}, u32[]{:S(2)}) collective-permute-start(f32[48,128]{1,0:T(8,128)S(1)} %add_add_fusion), channel_id=1, source_target_pairs={{0,32},{32,0},{1,33},{33,1},{2,34},{34,2},{3,35},{35,3},{4,36},{36... | collective-permute-start | bytes 73736 | tf_op jit(solution)/shard_map/ppermute | solution.py:295
  74.1 5.2 %collective-permute-start.7 = (f32[1024]{0:T(1024)S(1)}, f32[1024]{0:T(1024)S(1)}, u32[]{:S(2)}, u32[]{:S(2)}) collective-permute-start(f32[1024]{0:T(1024)S(1)} %bitcast.10), channel_id=1, source_target_pairs={{0,64},{64,0},{1,65},{65,1},{2,66},{66,2},{3,67},{67,3},{4,68},{68... | collective-permute-start | bytes 12296 | tf_op jit(solution)/shard_map/ppermute | solution.py:309

commit v5 on v4

--- a/solution.py
+++ b/solution.py
@@ -17,7 +17,8 @@
 BLOCKS = 4
 STRIPS = (((0, 0, 4), (1, 1, 1)), ((1, 2, 2), (2, 2, 2), (3, 3, 1)))
 LISTS = tuple(tuple((r, c + n) for r, c, w in strips for n in range(w)) for strips in STRIPS)
-HELD = len(LISTS[0]) + 1
+HELD = len(LISTS[0])
+SPARE, SPAN = GROUP // 2, 16
 
 
 def center_gram_kernel(place_ref, e_ref, a_ref, b_ref, c_ref, d_ref, cent_ref, out_ref):
@@ -50,9 +51,15 @@
                     out_ref[at : at + GROUP, :] = strip[:, GROUP * n : GROUP * n + GROUP]
                     at += GROUP
 
-    column = lax.broadcasted_iota(jnp.int32, (GROUP, GROUP), 1)
-    mine = (column // (GROUP // 2) == place_ref[5]) & (place_ref[6] == 0)
-    out_ref[GROUP * (HELD - 1) :, :] = jnp.where(mine, e_ref[...], 0.0)
+            column = lax.broadcasted_iota(jnp.int32, (SPARE, GROUP), 1)
+            pair = jnp.where(column < SPAN, e_ref[:SPARE, :], e_ref[SPARE:, :])
+            diagonals = [n for n, (r, c) in enumerate(LISTS[core]) if r == c]
+            for high, n in enumerate(diagonals):
+                mine = (place_ref[5] == high) & (place_ref[6] == 0)
+                rows = slice(GROUP * n + SPARE, GROUP * (n + 1))
+                out_ref[rows, :] = jnp.where(
+                    column < 2 * SPAN, jnp.where(mine, pair, 0.0), out_ref[rows, :]
+                )
 
 
 def lane(value, index):
@@ -143,24 +150,25 @@
     )
 
 
-def solve_kernel(place_ref, parts_ref, cent_ref, coeff_ref, update_ref, gram, low, rec, z):
+def solve_kernel(
+    place_ref, mine_ref, other_ref, cent_ref, coeff_ref, update_ref, gram, low, rec, z
+):
     blocks = BLOCKS
-    tiles = parts_ref.shape[1] // (2 * ROWS)
-
-    def tile(core, block, p):
-        number = PANELS * block + p
-        start = ROWS * (core * tiles + number % tiles)
-        return parts_ref[number // tiles, start : start + ROWS, :]
-
     for core, held in enumerate(LISTS):
-        for n, (r, c) in enumerate(held):
+        for mine, ref in ((core, mine_ref), (1 - core, other_ref)):
+
+            @pl.when(place_ref[4] == mine)
+            def _():
+                for n, (r, c) in enumerate(held):
+                    gram[r, c] = ref[GROUP * n : GROUP * n + GROUP, :]
+
+    energy_sum = jnp.zeros((ROWS, GROUP), jnp.float32)
+    for core, held in enumerate(LISTS):
+        for high, k in enumerate(r for r, c in held if r == c):
             for p in range(PANELS):
-                gram[r, c, ROWS * p : ROWS * p + ROWS, :] = tile(core, n, p)
-    energy_sum = jnp.zeros((ROWS, GROUP), jnp.float32)
-    for core in range(2):
-        for high in range(2):
-            for p in range(PANELS):
-                value = lane(tile(core, HELD - 1, p), high * GROUP // 2)
+                which, start = divmod(ROWS * p, SPARE)
+                tile = gram[k, k, SPARE + start : SPARE + start + ROWS, :]
+                value = lane(tile, SPAN * which)
                 gram[2 * high + core, blocks, ROWS * p : ROWS * p + ROWS, :] = value
                 energy_sum = energy_sum + value
     energy_mean = jnp.sum(energy_sum, axis=0, keepdims=True) / (blocks * GROUP)
@@ -235,14 +243,14 @@
     )(place, energies, *parts)
 
 
-def solve(place, parts, cent):
+def solve(place, mine, other, cent):
     return pl.pallas_call(
         solve_kernel,
         out_shape=(
             jax.ShapeDtypeStruct((BLOCKS * GROUP, GROUP), jnp.float32),
             jax.ShapeDtypeStruct((1, cent.shape[1]), jnp.float32),
         ),
-        in_specs=[SMEM] + [VMEM] * 2,
+        in_specs=[SMEM] + [VMEM] * 3,
         out_specs=(VMEM, VMEM),
         scratch_shapes=[
             pltpu.VMEM((4, 5, GROUP, GROUP), jnp.float32),
@@ -252,7 +260,7 @@
         ],
         compiler_params=pltpu.CompilerParams(vmem_limit_bytes=32 * 1024 * 1024),
         name="solve",
-    )(place, parts, cent)
+    )(place, mine, other, cent)
 
 
 SWAP = [(0, 1), (1, 0)]
@@ -262,8 +270,9 @@
     high = lax.axis_index("high")
     core = lax.axis_index("core")
     half = jacobian.shape[1] // 2
+    send = lax.dynamic_slice_in_dim(jacobian, (1 - high) * half, half, 1)
+    send, jacobian = lax.optimization_barrier((send, jacobian))
     keep = lax.dynamic_slice_in_dim(jacobian, high * half, half, 1)
-    send = lax.dynamic_slice_in_dim(jacobian, (1 - high) * half, half, 1)
     far = lax.ppermute(send, "high", SWAP)
     near = lax.ppermute(keep, "core", SWAP)
     diagonal = lax.ppermute(far, "core", SWAP)
@@ -292,18 +301,15 @@
         for step in range(1, ring)
     )
     chunk = (chunk + two) + (one + three)
-    other = lax.ppermute(chunk, "core", SWAP)
-    pair = jnp.concatenate(
-        [jnp.where(core == 0, chunk, other), jnp.where(core == 0, other, chunk)], axis=0
-    )
-    blocks = lax.all_to_all(
-        jnp.broadcast_to(pair[None], (peers, *pair.shape)),
+    mine = lax.all_to_all(
+        jnp.broadcast_to(chunk[None], (peers, *chunk.shape)),
         plane,
         split_axis=0,
         concat_axis=0,
         tiled=True,
-    )
-    coeffs, update = solve(place, blocks, cent)
+    ).reshape(HELD * GROUP, GROUP)
+    other = lax.ppermute(mine, "core", SWAP)
+    coeffs, update = solve(place, mine, other, cent)
     own = lax.dynamic_slice_in_dim(coeffs, (2 * high + core) * GROUP, GROUP, 0)[:, 0]
     update = update[0] * math.sqrt(2 * half * lax.axis_size(("z", "x", "low")))
     away = lax.ppermute(update, "high", SWAP)

time: 80.1 us -> 74.2 us (0.926)
  blocking collectives: 35 us -> 28.6 us
    all_to_all x1, blocking collectives: 18 us -> 12.3 us  [per_device(): lax.all_to_all(jnp.broadcast_to(chunk[None], (peers, *chunk.shape)), plan...]
    dynamic_slice x1, local copies, waits for them, and re-layouts: 1.07 us -> 0.02 us  [per_device(): send = lax.dynamic_slice_in_dim(jacobian, (1 - high) * half, half, 1)]
    unnamed x2 -> x4, local copies, waits for them, and re-layouts: 0.01 us -> 1.04 us
where the time goes in v5:
time: 74.2 us; the launch traced here: 74 us
  blocking collectives  28.6 us (39%)
  waiting for transfers between devices  15.7 us (21%)
  Pallas kernels  15.4 us (21%)
  starting transfers between devices  11 us (15%)
  local copies, waits for them, and re-layouts  1.88 us (3%)
    all_to_all x1, blocking collectives, per_device(): lax.all_to_all(partial.reshape(peers, -1, GROUP), plane, split_axis=0, co...  16.3 us
    pallas_call x1, Pallas kernels, solve(): pl.pallas_call(solve_kernel, out_shape=(jax.ShapeDtypeStruct((BLOCKS * GR...  13.9 us
    all_to_all x1, blocking collectives, per_device(): lax.all_to_all(jnp.broadcast_to(chunk[None], (peers, *chunk.shape)), plan...  12.3 us
    ppermute x1, waiting for transfers between devices, per_device(): far = lax.ppermute(send, 'high', SWAP)  6.19 us
    ppermute x3, starting transfers between devices, per_device(): lax.ppermute(chunk, 'z', [(n, (n + step) % ring) for n in range(ring)])  5.97 us
    ppermute x3, waiting for transfers between devices, per_device(): lax.ppermute(chunk, 'z', [(n, (n + step) % ring) for n in range(ring)])  3.43 us
    ppermute x1, starting transfers between devices, per_device(): far = lax.ppermute(send, 'high', SWAP)  3.36 us
    ppermute x1, waiting for transfers between devices, per_device(): away = lax.ppermute(update, 'high', SWAP)  3.02 us
  transfers between devices with their start and end apart: 8, of which 6 were waited for; matrix products, arithmetic and copies ran while one was open for 1% of the time, Pallas kernels for 0%

profile of v5, /device:TPU:0, one launch (start us, length us, event | category | flops | bytes accessed | tf_op | source)
XLA Modules:
  0.0 74.0 jit_solution(17841464272623484572)
XLA Ops:
  0.6 0.0 copy-start
  0.7 1.0 %copy-done = bf16[128,2048]{1,0:T(8,128)(2,1)S(1)} copy-done((bf16[128,2048]{1,0:T(8,128)(2,1)S(1)}, bf16[128,2048]{1,0:T(8,128)(2,1)}, u32[]{:S(2)}) %copy-start) | copy-done | bytes 524312
  1.7 3.4 %collective-permute-start = (bf16[128,1024]{1,0:T(8,128)(2,1)S(1)}, bf16[128,1024]{1,0:T(8,128)(2,1)S(1)}, u32[]{:S(2)}, u32[]{:S(2)}) collective-permute-start(bf16[128,1024]{1,0:T(8,128)(2,1)S(1)} %constant_dynamic-slice_fusion.1), channel_id=1, source_target_pairs={{0,64},{64,0},{1,65},{65,1},{2,66},{66,2},{3,67},{67,3},{4,68},{68... | collective-permute-start | bytes 786440 | tf_op jit(solution)/shard_map/ppermute | solution.py:276
  5.1 0.1 collective-permute-start.1
  5.2 6.2 %collective-permute-done.b_ref = bf16[128,1024]{1,0:T(8,128)(2,1)S(1)} collective-permute-done((bf16[128,1024]{1,0:T(8,128)(2,1)S(1)}, bf16[128,1024]{1,0:T(8,128)(2,1)S(1)}, u32[]{:S(2)}, u32[]{:S(2)}) %collective-permute-start) | collective-permute-done | bytes 262176 | tf_op jit(solution)/shard_map/ppermute | solution.py:276
  11.4 0.0 collective-permute-start.2
  11.4 0.1 stack.31.place_ref
  11.5 0.0 collective-permute-done.1.c_ref
  11.5 1.4 %collective-permute-done.2.d_ref = bf16[128,1024]{1,0:T(8,128)(2,1)S(1)} collective-permute-done((bf16[128,1024]{1,0:T(8,128)(2,1)S(1)}, bf16[128,1024]{1,0:T(8,128)(2,1)S(1)}, u32[]{:S(2)}, u32[]{:S(2)}) %collective-permute-start.2) | collective-permute-done | bytes 262176 | tf_op jit(solution)/shard_map/ppermute | solution.py:278
  12.9 0.1 broadcast_in_dim.4.e_ref
  13.0 1.6 %center_gram.1 = (bf16[512,1024]{1,0:T(8,128)(2,1)S(1)}, f32[640,128]{1,0:T(8,128)S(1)}) custom-call(s32[7]{0:T(128)S(1)} %stack.31.place_ref, f32[128,128]{1,0:T(8,128)S(1)} %broadcast_in_dim.4.e_ref, bf16[128,1024]{1,0:T(8,128)(2,1)S(1)} %constant_dynamic-slice_fusion.a_ref, bf16[128,1024]{1,0:T(8,128)(2,1)S(1)} %collective-permute-done.b_ref, ...), custom_call_target="tpu_custom_call" | custom-call | tf_op jit(solution)/shard_map/center_gram/pallas_call | solution.py:233
  14.6 16.3 %all_to_all.10 = f32[16,40,128]{2,1,0:T(8,128)S(1)} all-to-all(f32[16,40,128]{2,1,0:T(8,128)S(1)} %bitcast.12), channel_id=1, replica_groups=mesh['high'=2,'core'=2,'z'=4,'x'=4,'low'=2] {'high','x','low'}, dimensions={0} | all-to-all | bytes 655360 | tf_op jit(solution)/shard_map/all_to_all | solution.py:294
  30.9 4.1 %collective-permute-start.5 = (f32[40,128]{1,0:T(8,128)S(1)}, f32[40,128]{1,0:T(8,128)S(1)}, u32[]{:S(2)}, u32[]{:S(2)}) collective-permute-start(f32[40,128]{1,0:T(8,128)S(1)} %reduce_sum.9), channel_id=1, source_target_pairs={{0,24},{8,0},{16,8},{24,16},{1,25},{9,1},{17,9},{25,17},{2,26},{10... | collective-permute-start | bytes 61448 | tf_op jit(solution)/shard_map/ppermute | solution.py:300
  35.0 1.9 %collective-permute-start.3 = (f32[40,128]{1,0:T(8,128)S(1)}, f32[40,128]{1,0:T(8,128)S(1)}, u32[]{:S(2)}, u32[]{:S(2)}) collective-permute-start(f32[40,128]{1,0:T(8,128)S(1)} %reduce_sum.9), channel_id=1, source_target_pairs={{0,16},{8,24},{16,0},{24,8},{1,17},{9,25},{17,1},{25,9},{2,18},{10... | collective-permute-start | bytes 61448 | tf_op jit(solution)/shard_map/ppermute | solution.py:300
  36.9 0.0 collective-permute-done.5
  36.9 3.1 %collective-permute-done.4 = f32[40,128]{1,0:T(8,128)S(1)} collective-permute-done((f32[40,128]{1,0:T(8,128)S(1)}, f32[40,128]{1,0:T(8,128)S(1)}, u32[]{:S(2)}, u32[]{:S(2)}) %collective-permute-start.4) | collective-permute-done | bytes 20512 | tf_op jit(solution)/shard_map/ppermute | solution.py:300
  40.0 0.3 collective-permute-done.3
  40.4 12.3 %all_to_all.11 = f32[16,40,128]{2,1,0:T(8,128)S(1)} all-to-all(f32[16,40,128]{2,1,0:T(8,128)S(1)} %broadcast_in_dim.5), channel_id=1, replica_groups=mesh['high'=2,'core'=2,'z'=4,'x'=4,'low'=2] {'high','x','low'}, dimensions={0} | all-to-all | bytes 655360 | tf_op jit(solution)/shard_map/all_to_all | solution.py:304
  52.7 1.6 %collective-permute-done.6.other_ref = f32[640,128]{1,0:T(8,128)S(1)} collective-permute-done((f32[640,128]{1,0:T(8,128)S(1)}, f32[640,128]{1,0:T(8,128)S(1)}, u32[]{:S(2)}, u32[]{:S(2)}) %collective-permute-start.6) | collective-permute-done | bytes 327712 | tf_op jit(solution)/shard_map/ppermute | solution.py:311
  54.3 13.9 %solve.1 = (f32[512,128]{1,0:T(8,128)S(1)}, f32[1,1024]{1,0:T(1,128)S(1)}) custom-call(s32[7]{0:T(128)S(1)} %stack.31.place_ref, f32[640,128]{1,0:T(8,128)S(1)} %bitcast.11, f32[640,128]{1,0:T(8,128)S(1)} %collective-permute-done.6.other_ref, bf16[512,1024]{1,0:T(8,128)(2,1)S(1)} %get-tuple-element.11.cent_ref), custom_call_target="tpu_custom_call" | custom-call | tf_op jit(solution)/shard_map/solve/pallas_call | solution.py:247
  68.2 1.5 %collective-permute-start.7 = (f32[1024]{0:T(1024)S(1)}, f32[1024]{0:T(1024)S(1)}, u32[]{:S(2)}, u32[]{:S(2)}) collective-permute-start(f32[1024]{0:T(1024)S(1)} %bitcast.13), channel_id=1, source_target_pairs={{0,64},{64,0},{1,65},{65,1},{2,66},{66,2},{3,67},{67,3},{4,68},{68... | collective-permute-start | bytes 12296 | tf_op jit(solution)/shard_map/ppermute | solution.py:315
  69.7 0.6 dynamic-slice_reduce_fusion
  70.3 3.0 %collective-permute-done.7 = f32[1024]{0:T(1024)S(1)} collective-permute-done((f32[1024]{0:T(1024)S(1)}, f32[1024]{0:T(1024)S(1)}, u32[]{:S(2)}, u32[]{:S(2)}) %collective-permute-start.7) | collective-permute-done | bytes 4128 | tf_op jit(solution)/shard_map/ppermute | solution.py:315
  73.4 0.6 pad_maximum_fusion
  (11 shorter events, 0.1 us)
Async XLA Ops:
  0.6 1.0 %copy-start = (bf16[128,2048]{1,0:T(8,128)(2,1)S(1)}, bf16[128,2048]{1,0:T(8,128)(2,1)}, u32[]{:S(2)}) copy-start(bf16[128,2048]{1,0:T(8,128)(2,1)} %param.2) | copy-start | bytes 1572868
  1.7 9.7 %collective-permute-start = (bf16[128,1024]{1,0:T(8,128)(2,1)S(1)}, bf16[128,1024]{1,0:T(8,128)(2,1)S(1)}, u32[]{:S(2)}, u32[]{:S(2)}) collective-permute-start(bf16[128,1024]{1,0:T(8,128)(2,1)S(1)} %constant_dynamic-slice_fusion.1), channel_id=1, source_target_pairs={{0,64},{64,0},{1,65},{65,1},{2,66},{66,2},{3,67},{67,3},{4,68},{68... | collective-permute-start | bytes 786440 | tf_op jit(solution)/shard_map/ppermute | solution.py:276
  5.1 6.4 %collective-permute-start.1 = (bf16[128,1024]{1,0:T(8,128)(2,1)S(1)}, bf16[128,1024]{1,0:T(8,128)(2,1)S(1)}, u32[]{:S(2)}, u32[]{:S(2)}) collective-permute-start(bf16[128,1024]{1,0:T(8,128)(2,1)S(1)} %constant_dynamic-slice_fusion.a_ref), channel_id=1, source_target_pairs={{0,32},{32,0},{1,33},{33,1},{2,34},{34,2},{3,35},{35,3},{4,36},{36... | collective-permute-start | bytes 786440 | tf_op jit(solution)/shard_map/ppermute | solution.py:277
  11.4 1.5 %collective-permute-start.2 = (bf16[128,1024]{1,0:T(8,128)(2,1)S(1)}, bf16[128,1024]{1,0:T(8,128)(2,1)S(1)}, u32[]{:S(2)}, u32[]{:S(2)}) collective-permute-start(bf16[128,1024]{1,0:T(8,128)(2,1)S(1)} %collective-permute-done.b_ref), channel_id=1, source_target_pairs={{0,32},{32,0},{1,33},{33,1},{2,34},{34,2},{3,35},{35,3},{4,36},{36... | collective-permute-start | bytes 786440 | tf_op jit(solution)/shard_map/ppermute | solution.py:278
  11.4 1.5 %copy-start.1 = (f32[128]{0:T(128)S(1)}, f32[128]{0:T(128)}, u32[]{:S(2)}) copy-start(f32[128]{0:T(128)} %param.3) | copy-start | bytes 1540
  30.9 6.0 %collective-permute-start.5 = (f32[40,128]{1,0:T(8,128)S(1)}, f32[40,128]{1,0:T(8,128)S(1)}, u32[]{:S(2)}, u32[]{:S(2)}) collective-permute-start(f32[40,128]{1,0:T(8,128)S(1)} %reduce_sum.9), channel_id=1, source_target_pairs={{0,24},{8,0},{16,8},{24,16},{1,25},{9,1},{17,9},{25,17},{2,26},{10... | collective-permute-start | bytes 61448 | tf_op jit(solution)/shard_map/ppermute | solution.py:300
  35.0 5.0 %collective-permute-start.4 = (f32[40,128]{1,0:T(8,128)S(1)}, f32[40,128]{1,0:T(8,128)S(1)}, u32[]{:S(2)}, u32[]{:S(2)}) collective-permute-start(f32[40,128]{1,0:T(8,128)S(1)} %reduce_sum.9), channel_id=1, source_target_pairs={{0,8},{8,16},{16,24},{24,0},{1,9},{9,17},{17,25},{25,1},{2,10},{10... | collective-permute-start | bytes 61448 | tf_op jit(solution)/shard_map/ppermute | solution.py:300
  35.0 5.3 %collective-permute-start.3 = (f32[40,128]{1,0:T(8,128)S(1)}, f32[40,128]{1,0:T(8,128)S(1)}, u32[]{:S(2)}, u32[]{:S(2)}) collective-permute-start(f32[40,128]{1,0:T(8,128)S(1)} %reduce_sum.9), channel_id=1, source_target_pairs={{0,16},{8,24},{16,0},{24,8},{1,17},{9,25},{17,1},{25,9},{2,18},{10... | collective-permute-start | bytes 61448 | tf_op jit(solution)/shard_map/ppermute | solution.py:300
  52.6 1.6 %collective-permute-start.6 = (f32[640,128]{1,0:T(8,128)S(1)}, f32[640,128]{1,0:T(8,128)S(1)}, u32[]{:S(2)}, u32[]{:S(2)}) collective-permute-start(f32[640,128]{1,0:T(8,128)S(1)} %bitcast.10), channel_id=1, source_target_pairs={{0,32},{32,0},{1,33},{33,1},{2,34},{34,2},{3,35},{35,3},{4,36},{36... | collective-permute-start | bytes 983048 | tf_op jit(solution)/shard_map/ppermute | solution.py:311
  68.2 5.2 %collective-permute-start.7 = (f32[1024]{0:T(1024)S(1)}, f32[1024]{0:T(1024)S(1)}, u32[]{:S(2)}, u32[]{:S(2)}) collective-permute-start(f32[1024]{0:T(1024)S(1)} %bitcast.13), channel_id=1, source_target_pairs={{0,64},{64,0},{1,65},{65,1},{2,66},{66,2},{3,67},{67,3},{4,68},{68... | collective-permute-start | bytes 12296 | tf_op jit(solution)/shard_map/ppermute | solution.py:315

commit v6 on v5

--- a/solution.py
+++ b/solution.py
@@ -100,10 +100,7 @@
             factor = {t: held[j, t] * recip for t in range(home, WIDE)}
             for m in range(j + 1, size):
                 for t in range(m // ROWS, WIDE):
-                    if m == j + 1:
-                        held[m, t] = held[m, t] - (held[j, t] * spread[m]) * recip
-                    else:
-                        held[m, t] = held[m, t] - factor[t] * spread[m]
+                    held[m, t] = held[m, t] - factor[t] * spread[m]
             for t in range(home, WIDE):
                 part = jnp.where(line > at, factor[t], 0.0) if t == home else factor[t]
                 work[t] = work[t] - part * pivot_row
@@ -151,7 +148,7 @@
 
 
 def solve_kernel(
-    place_ref, mine_ref, other_ref, cent_ref, coeff_ref, update_ref, gram, low, rec, z
+    place_ref, mine_ref, other_ref, cent_ref, coeff_ref, update_ref, gram, rest
 ):
     blocks = BLOCKS
     for core, held in enumerate(LISTS):
@@ -160,21 +157,25 @@
             @pl.when(place_ref[4] == mine)
             def _():
                 for n, (r, c) in enumerate(held):
-                    gram[r, c] = ref[GROUP * n : GROUP * n + GROUP, :]
+                    gram[r, :, GROUP * c : GROUP * c + GROUP] = ref[
+                        GROUP * n : GROUP * n + GROUP, :
+                    ]
 
     energy_sum = jnp.zeros((ROWS, GROUP), jnp.float32)
     for core, held in enumerate(LISTS):
         for high, k in enumerate(r for r, c in held if r == c):
             for p in range(PANELS):
                 which, start = divmod(ROWS * p, SPARE)
-                tile = gram[k, k, SPARE + start : SPARE + start + ROWS, :]
+                tile = gram[
+                    k, SPARE + start : SPARE + start + ROWS, GROUP * k : GROUP * k + GROUP
+                ]
                 value = lane(tile, SPAN * which)
-                gram[2 * high + core, blocks, ROWS * p : ROWS * p + ROWS, :] = value
+                gram[2 * high + core, ROWS * p : ROWS * p + ROWS, GROUP * blocks :] = value
                 energy_sum = energy_sum + value
     energy_mean = jnp.sum(energy_sum, axis=0, keepdims=True) / (blocks * GROUP)
     scale = 1.0 / math.sqrt(blocks * GROUP)
     for k in range(blocks):
-        gram[k, blocks] = (gram[k, blocks] - energy_mean) * scale
+        gram[k, :, GROUP * blocks :] = (gram[k, :, GROUP * blocks :] - energy_mean) * scale
     column = lax.broadcasted_iota(jnp.int32, (ROWS, GROUP), 1)
     line = lax.broadcasted_iota(jnp.int32, (ROWS, GROUP), 0)
 
@@ -182,33 +183,32 @@
         panels = []
         for p in range(PANELS):
             ridge = jnp.where(column - ROWS * p == line, RIDGE, 0.0)
-            panels.append(gram[k, k, ROWS * p : ROWS * p + ROWS, :] + ridge)
+            tile = gram[k, ROWS * p : ROWS * p + ROWS, GROUP * k : GROUP * k + GROUP]
+            panels.append(tile + ridge)
         inverse, recips = factor_block(panels)
-        for p in range(PANELS):
-            low[k, ROWS * p : ROWS * p + ROWS, :] = inverse[p]
-            rec[k, ROWS * p : ROWS * p + ROWS, :] = recips[p]
-        tri = stack_left(low[k], 1)
-        later = range(k + 1, blocks + 1)
-        ys = {j: contract(tri, stack_right(gram[k, j], 0), 1) for j in later}
-        zs = {j: ys[j] * rec[k] for j in later}
-        for j in later:
-            z[k, j] = zs[j]
-        right = {j: stack_right(zs[j], 0) for j in later}
+        triangle = jnp.concatenate(inverse, axis=0)
+        tri = stack_left(triangle, 1)
+        tri_turned = stack_left(triangle, 0)
+        wide = slice(GROUP * (k + 1), GROUP * (blocks + 1))
+        y = contract(tri, stack_right(gram[k, :, wide], 0), 1)
+        inverse_d = jnp.concatenate(recips, axis=0)
+        right = stack_right(y * jnp.concatenate([inverse_d] * (blocks - k), axis=1), 0)
         for i in range(k + 1, blocks):
-            left = stack_left(ys[i], 0)
-            for j in range(i, blocks + 1):
-                gram[i, j] = gram[i, j] - contract(left, right[j], 0)
+            skip = GROUP * (i - k - 1)
+            left = stack_left(y[:, skip : skip + GROUP], 0)
+            place = slice(GROUP * i, GROUP * (blocks + 1))
+            gram[i, :, place] = gram[i, :, place] - contract(left, right[:, skip:], 0)
+        rest[k, :, wide] = contract(tri_turned, right, 0)
+        if k:
+            found = stack_right(rest[k, :, wide], 0)
+        for i in range(k):
+            left = stack_left(rest[i, :, GROUP * k : GROUP * k + GROUP], 1)
+            rest[i, :, wide] = rest[i, :, wide] - contract(left, found, 1)
 
     for k in range(blocks):
         step(k)
-    xs = [None] * blocks
-    spread = [None] * blocks
-    for k in range(blocks - 1, -1, -1):
-        right = z[k, blocks]
-        for j in range(k + 1, blocks):
-            right = right - contract(stack_left(z[k, j], 1), spread[j], 1)
-        xs[k] = contract(stack_left(low[k], 0), stack_right(right, 0), 0)
-        spread[k] = stack_right(xs[k], 0)
+    xs = [rest[k, :, GROUP * blocks :] for k in range(blocks)]
+    for k in range(blocks):
         coeff_ref[GROUP * k : GROUP * k + GROUP, :] = xs[k]
     width = cent_ref.shape[1]
     for piece in range(width // GROUP):
@@ -253,10 +253,8 @@
         in_specs=[SMEM] + [VMEM] * 3,
         out_specs=(VMEM, VMEM),
         scratch_shapes=[
-            pltpu.VMEM((4, 5, GROUP, GROUP), jnp.float32),
-            pltpu.VMEM((4, GROUP, GROUP), jnp.float32),
-            pltpu.VMEM((4, GROUP, GROUP), jnp.float32),
-            pltpu.VMEM((4, 5, GROUP, GROUP), jnp.float32),
+            pltpu.VMEM((BLOCKS, GROUP, (BLOCKS + 1) * GROUP), jnp.float32),
+            pltpu.VMEM((BLOCKS, GROUP, (BLOCKS + 1) * GROUP), jnp.float32),
         ],
         compiler_params=pltpu.CompilerParams(vmem_limit_bytes=32 * 1024 * 1024),
         name="solve",

time: 74.2 us -> 73.4 us (0.989)
  Pallas kernels: 15.4 us -> 14.6 us
    pallas_call x1, Pallas kernels: 13.9 us -> 13 us  [solve(): pl.pallas_call(solve_kernel, out_shape=(jax.ShapeDtypeStruct((BLOCKS * GR...]
where the time goes in v6:
time: 73.4 us; the launch traced here: 73.1 us
  blocking collectives  28.6 us (39%)
  waiting for transfers between devices  15.7 us (21%)
  Pallas kernels  14.6 us (20%)
  starting transfers between devices  11 us (15%)
  local copies, waits for them, and re-layouts  1.88 us (3%)
    all_to_all x1, blocking collectives, per_device(): lax.all_to_all(partial.reshape(peers, -1, GROUP), plane, split_axis=0, co...  16.3 us
    pallas_call x1, Pallas kernels, solve(): pl.pallas_call(solve_kernel, out_shape=(jax.ShapeDtypeStruct((BLOCKS * GR...  13 us
    all_to_all x1, blocking collectives, per_device(): lax.all_to_all(jnp.broadcast_to(chunk[None], (peers, *chunk.shape)), plan...  12.3 us
    ppermute x1, waiting for transfers between devices, per_device(): far = lax.ppermute(send, 'high', SWAP)  6.19 us
    ppermute x3, starting transfers between devices, per_device(): lax.ppermute(chunk, 'z', [(n, (n + step) % ring) for n in range(ring)])  5.97 us
    ppermute x3, waiting for transfers between devices, per_device(): lax.ppermute(chunk, 'z', [(n, (n + step) % ring) for n in range(ring)])  3.43 us
    ppermute x1, starting transfers between devices, per_device(): far = lax.ppermute(send, 'high', SWAP)  3.36 us
    ppermute x1, waiting for transfers between devices, per_device(): away = lax.ppermute(update, 'high', SWAP)  3.02 us
  transfers between devices with their start and end apart: 8, of which 6 were waited for; matrix products, arithmetic and copies ran while one was open for 1% of the time, Pallas kernels for 0%

profile of v6, /device:TPU:0, one launch (start us, length us, event | category | flops | bytes accessed | tf_op | source)
XLA Modules:
  0.0 73.1 jit_solution(14437460653125986227)
XLA Ops:
  0.6 0.0 copy-start
  0.7 1.0 %copy-done = bf16[128,2048]{1,0:T(8,128)(2,1)S(1)} copy-done((bf16[128,2048]{1,0:T(8,128)(2,1)S(1)}, bf16[128,2048]{1,0:T(8,128)(2,1)}, u32[]{:S(2)}) %copy-start) | copy-done | bytes 524312
  1.7 3.4 %collective-permute-start = (bf16[128,1024]{1,0:T(8,128)(2,1)S(1)}, bf16[128,1024]{1,0:T(8,128)(2,1)S(1)}, u32[]{:S(2)}, u32[]{:S(2)}) collective-permute-start(bf16[128,1024]{1,0:T(8,128)(2,1)S(1)} %constant_dynamic-slice_fusion.1), channel_id=1, source_target_pairs={{0,64},{64,0},{1,65},{65,1},{2,66},{66,2},{3,67},{67,3},{4,68},{68... | collective-permute-start | bytes 786440 | tf_op jit(solution)/shard_map/ppermute | solution.py:274
  5.1 0.1 collective-permute-start.1
  5.2 6.2 %collective-permute-done.b_ref = bf16[128,1024]{1,0:T(8,128)(2,1)S(1)} collective-permute-done((bf16[128,1024]{1,0:T(8,128)(2,1)S(1)}, bf16[128,1024]{1,0:T(8,128)(2,1)S(1)}, u32[]{:S(2)}, u32[]{:S(2)}) %collective-permute-start) | collective-permute-done | bytes 262176 | tf_op jit(solution)/shard_map/ppermute | solution.py:274
  11.4 0.0 collective-permute-start.2
  11.4 0.1 stack.31.place_ref
  11.5 1.4 %collective-permute-done.2.d_ref = bf16[128,1024]{1,0:T(8,128)(2,1)S(1)} collective-permute-done((bf16[128,1024]{1,0:T(8,128)(2,1)S(1)}, bf16[128,1024]{1,0:T(8,128)(2,1)S(1)}, u32[]{:S(2)}, u32[]{:S(2)}) %collective-permute-start.2) | collective-permute-done | bytes 262176 | tf_op jit(solution)/shard_map/ppermute | solution.py:276
  12.9 0.1 broadcast_in_dim.4.e_ref
  13.0 1.6 %center_gram.1 = (bf16[512,1024]{1,0:T(8,128)(2,1)S(1)}, f32[640,128]{1,0:T(8,128)S(1)}) custom-call(s32[7]{0:T(128)S(1)} %stack.31.place_ref, f32[128,128]{1,0:T(8,128)S(1)} %broadcast_in_dim.4.e_ref, bf16[128,1024]{1,0:T(8,128)(2,1)S(1)} %constant_dynamic-slice_fusion.a_ref, bf16[128,1024]{1,0:T(8,128)(2,1)S(1)} %collective-permute-done.b_ref, ...), custom_call_target="tpu_custom_call" | custom-call | tf_op jit(solution)/shard_map/center_gram/pallas_call | solution.py:233
  14.6 16.3 %all_to_all.10 = f32[16,40,128]{2,1,0:T(8,128)S(1)} all-to-all(f32[16,40,128]{2,1,0:T(8,128)S(1)} %bitcast.12), channel_id=1, replica_groups=mesh['high'=2,'core'=2,'z'=4,'x'=4,'low'=2] {'high','x','low'}, dimensions={0} | all-to-all | bytes 655360 | tf_op jit(solution)/shard_map/all_to_all | solution.py:292
  30.9 4.1 %collective-permute-start.5 = (f32[40,128]{1,0:T(8,128)S(1)}, f32[40,128]{1,0:T(8,128)S(1)}, u32[]{:S(2)}, u32[]{:S(2)}) collective-permute-start(f32[40,128]{1,0:T(8,128)S(1)} %reduce_sum.9), channel_id=1, source_target_pairs={{0,24},{8,0},{16,8},{24,16},{1,25},{9,1},{17,9},{25,17},{2,26},{10... | collective-permute-start | bytes 61448 | tf_op jit(solution)/shard_map/ppermute | solution.py:298
  35.0 0.0 collective-permute-start.4
  35.0 1.9 %collective-permute-start.3 = (f32[40,128]{1,0:T(8,128)S(1)}, f32[40,128]{1,0:T(8,128)S(1)}, u32[]{:S(2)}, u32[]{:S(2)}) collective-permute-start(f32[40,128]{1,0:T(8,128)S(1)} %reduce_sum.9), channel_id=1, source_target_pairs={{0,16},{8,24},{16,0},{24,8},{1,17},{9,25},{17,1},{25,9},{2,18},{10... | collective-permute-start | bytes 61448 | tf_op jit(solution)/shard_map/ppermute | solution.py:298
  36.9 3.1 %collective-permute-done.4 = f32[40,128]{1,0:T(8,128)S(1)} collective-permute-done((f32[40,128]{1,0:T(8,128)S(1)}, f32[40,128]{1,0:T(8,128)S(1)}, u32[]{:S(2)}, u32[]{:S(2)}) %collective-permute-start.4) | collective-permute-done | bytes 20512 | tf_op jit(solution)/shard_map/ppermute | solution.py:298
  40.0 0.3 collective-permute-done.3
  40.4 12.3 %all_to_all.11 = f32[16,40,128]{2,1,0:T(8,128)S(1)} all-to-all(f32[16,40,128]{2,1,0:T(8,128)S(1)} %broadcast_in_dim.5), channel_id=1, replica_groups=mesh['high'=2,'core'=2,'z'=4,'x'=4,'low'=2] {'high','x','low'}, dimensions={0} | all-to-all | bytes 655360 | tf_op jit(solution)/shard_map/all_to_all | solution.py:302
  52.6 0.0 collective-permute-start.6
  52.7 1.6 %collective-permute-done.6.other_ref = f32[640,128]{1,0:T(8,128)S(1)} collective-permute-done((f32[640,128]{1,0:T(8,128)S(1)}, f32[640,128]{1,0:T(8,128)S(1)}, u32[]{:S(2)}, u32[]{:S(2)}) %collective-permute-start.6) | collective-permute-done | bytes 327712 | tf_op jit(solution)/shard_map/ppermute | solution.py:309
  54.3 13.0 %solve.1 = (f32[512,128]{1,0:T(8,128)S(1)}, f32[1,1024]{1,0:T(1,128)S(1)}) custom-call(s32[7]{0:T(128)S(1)} %stack.31.place_ref, f32[640,128]{1,0:T(8,128)S(1)} %bitcast.11, f32[640,128]{1,0:T(8,128)S(1)} %collective-permute-done.6.other_ref, bf16[512,1024]{1,0:T(8,128)(2,1)S(1)} %get-tuple-element.11.cent_ref), custom_call_target="tpu_custom_call" | custom-call | tf_op jit(solution)/shard_map/solve/pallas_call | solution.py:247
  67.3 1.5 %collective-permute-start.7 = (f32[1024]{0:T(1024)S(1)}, f32[1024]{0:T(1024)S(1)}, u32[]{:S(2)}, u32[]{:S(2)}) collective-permute-start(f32[1024]{0:T(1024)S(1)} %bitcast.13), channel_id=1, source_target_pairs={{0,64},{64,0},{1,65},{65,1},{2,66},{66,2},{3,67},{67,3},{4,68},{68... | collective-permute-start | bytes 12296 | tf_op jit(solution)/shard_map/ppermute | solution.py:313
  68.9 0.6 dynamic-slice_reduce_fusion
  69.5 3.0 %collective-permute-done.7 = f32[1024]{0:T(1024)S(1)} collective-permute-done((f32[1024]{0:T(1024)S(1)}, f32[1024]{0:T(1024)S(1)}, u32[]{:S(2)}, u32[]{:S(2)}) %collective-permute-start.7) | collective-permute-done | bytes 4128 | tf_op jit(solution)/shard_map/ppermute | solution.py:313
  72.5 0.6 pad_maximum_fusion
  (11 shorter events, 0.1 us)
Async XLA Ops:
  0.6 1.0 %copy-start = (bf16[128,2048]{1,0:T(8,128)(2,1)S(1)}, bf16[128,2048]{1,0:T(8,128)(2,1)}, u32[]{:S(2)}) copy-start(bf16[128,2048]{1,0:T(8,128)(2,1)} %param.2) | copy-start | bytes 1572868
  1.7 9.7 %collective-permute-start = (bf16[128,1024]{1,0:T(8,128)(2,1)S(1)}, bf16[128,1024]{1,0:T(8,128)(2,1)S(1)}, u32[]{:S(2)}, u32[]{:S(2)}) collective-permute-start(bf16[128,1024]{1,0:T(8,128)(2,1)S(1)} %constant_dynamic-slice_fusion.1), channel_id=1, source_target_pairs={{0,64},{64,0},{1,65},{65,1},{2,66},{66,2},{3,67},{67,3},{4,68},{68... | collective-permute-start | bytes 786440 | tf_op jit(solution)/shard_map/ppermute | solution.py:274
  5.1 6.4 %collective-permute-start.1 = (bf16[128,1024]{1,0:T(8,128)(2,1)S(1)}, bf16[128,1024]{1,0:T(8,128)(2,1)S(1)}, u32[]{:S(2)}, u32[]{:S(2)}) collective-permute-start(bf16[128,1024]{1,0:T(8,128)(2,1)S(1)} %constant_dynamic-slice_fusion.a_ref), channel_id=1, source_target_pairs={{0,32},{32,0},{1,33},{33,1},{2,34},{34,2},{3,35},{35,3},{4,36},{36... | collective-permute-start | bytes 786440 | tf_op jit(solution)/shard_map/ppermute | solution.py:275
  11.4 1.5 %collective-permute-start.2 = (bf16[128,1024]{1,0:T(8,128)(2,1)S(1)}, bf16[128,1024]{1,0:T(8,128)(2,1)S(1)}, u32[]{:S(2)}, u32[]{:S(2)}) collective-permute-start(bf16[128,1024]{1,0:T(8,128)(2,1)S(1)} %collective-permute-done.b_ref), channel_id=1, source_target_pairs={{0,32},{32,0},{1,33},{33,1},{2,34},{34,2},{3,35},{35,3},{4,36},{36... | collective-permute-start | bytes 786440 | tf_op jit(solution)/shard_map/ppermute | solution.py:276
  11.4 1.5 %copy-start.1 = (f32[128]{0:T(128)S(1)}, f32[128]{0:T(128)}, u32[]{:S(2)}) copy-start(f32[128]{0:T(128)} %param.3) | copy-start | bytes 1540
  30.9 6.0 %collective-permute-start.5 = (f32[40,128]{1,0:T(8,128)S(1)}, f32[40,128]{1,0:T(8,128)S(1)}, u32[]{:S(2)}, u32[]{:S(2)}) collective-permute-start(f32[40,128]{1,0:T(8,128)S(1)} %reduce_sum.9), channel_id=1, source_target_pairs={{0,24},{8,0},{16,8},{24,16},{1,25},{9,1},{17,9},{25,17},{2,26},{10... | collective-permute-start | bytes 61448 | tf_op jit(solution)/shard_map/ppermute | solution.py:298
  35.0 5.0 %collective-permute-start.4 = (f32[40,128]{1,0:T(8,128)S(1)}, f32[40,128]{1,0:T(8,128)S(1)}, u32[]{:S(2)}, u32[]{:S(2)}) collective-permute-start(f32[40,128]{1,0:T(8,128)S(1)} %reduce_sum.9), channel_id=1, source_target_pairs={{0,8},{8,16},{16,24},{24,0},{1,9},{9,17},{17,25},{25,1},{2,10},{10... | collective-permute-start | bytes 61448 | tf_op jit(solution)/shard_map/ppermute | solution.py:298
  35.0 5.3 %collective-permute-start.3 = (f32[40,128]{1,0:T(8,128)S(1)}, f32[40,128]{1,0:T(8,128)S(1)}, u32[]{:S(2)}, u32[]{:S(2)}) collective-permute-start(f32[40,128]{1,0:T(8,128)S(1)} %reduce_sum.9), channel_id=1, source_target_pairs={{0,16},{8,24},{16,0},{24,8},{1,17},{9,25},{17,1},{25,9},{2,18},{10... | collective-permute-start | bytes 61448 | tf_op jit(solution)/shard_map/ppermute | solution.py:298
  52.6 1.6 %collective-permute-start.6 = (f32[640,128]{1,0:T(8,128)S(1)}, f32[640,128]{1,0:T(8,128)S(1)}, u32[]{:S(2)}, u32[]{:S(2)}) collective-permute-start(f32[640,128]{1,0:T(8,128)S(1)} %bitcast.10), channel_id=1, source_target_pairs={{0,32},{32,0},{1,33},{33,1},{2,34},{34,2},{3,35},{35,3},{4,36},{36... | collective-permute-start | bytes 983048 | tf_op jit(solution)/shard_map/ppermute | solution.py:309
  67.3 5.2 %collective-permute-start.7 = (f32[1024]{0:T(1024)S(1)}, f32[1024]{0:T(1024)S(1)}, u32[]{:S(2)}, u32[]{:S(2)}) collective-permute-start(f32[1024]{0:T(1024)S(1)} %bitcast.13), channel_id=1, source_target_pairs={{0,64},{64,0},{1,65},{65,1},{2,66},{66,2},{3,67},{67,3},{4,68},{68... | collective-permute-start | bytes 12296 | tf_op jit(solution)/shard_map/ppermute | solution.py:313

commit v7 on v6

--- a/solution.py
+++ b/solution.py
@@ -11,6 +11,7 @@
 ROWS = 8
 WIDE = 2
 PANELS = GROUP // ROWS
+COPIES = 4
 RIDGE = 0.05
 
 
@@ -224,8 +225,38 @@
         )
 
 
+def half_kernel(source_ref, half_ref, sems):
+    columns = half_ref.shape[1]
+    start = pl.multiple_of((1 - lax.axis_index("high")) * columns, columns)
+    copies = []
+    for n in range(COPIES):
+        rows = pl.ds(n * (GROUP // COPIES), GROUP // COPIES)
+        copies.append(
+            pltpu.make_async_copy(
+                source_ref.at[rows, pl.ds(start, columns)], half_ref.at[rows, :], sems.at[n]
+            )
+        )
+    for copy in copies:
+        copy.start()
+    for copy in copies:
+        copy.wait()
+
+
 VMEM = pl.BlockSpec(memory_space=pltpu.VMEM)
 SMEM = pl.BlockSpec(memory_space=pltpu.SMEM)
+
+
+def other_half(jacobian):
+    rows, columns = jacobian.shape
+    return pl.pallas_call(
+        half_kernel,
+        out_shape=jax.ShapeDtypeStruct((rows, columns // 2), jacobian.dtype),
+        in_specs=[pl.BlockSpec(memory_space=pl.ANY)],
+        out_specs=pl.BlockSpec(memory_space=pl.ANY),
+        scratch_shapes=[pltpu.SemaphoreType.DMA((COPIES,))],
+        compiler_params=pltpu.CompilerParams(vmem_limit_bytes=60 * 1024 * 1024),
+        name="other_half",
+    )(jacobian)
 
 
 def center_gram(place, energies, parts):
@@ -268,8 +299,7 @@
     high = lax.axis_index("high")
     core = lax.axis_index("core")
     half = jacobian.shape[1] // 2
-    send = lax.dynamic_slice_in_dim(jacobian, (1 - high) * half, half, 1)
-    send, jacobian = lax.optimization_barrier((send, jacobian))
+    send = other_half(jacobian)
     keep = lax.dynamic_slice_in_dim(jacobian, high * half, half, 1)
     far = lax.ppermute(send, "high", SWAP)
     near = lax.ppermute(keep, "core", SWAP)
@@ -294,9 +324,9 @@
     )
     chunk = jnp.sum(parts, axis=0)
     ring = lax.axis_size("z")
-    one, two, three = (
+    one, three, two = (
         lax.ppermute(chunk, "z", [(n, (n + step) % ring) for n in range(ring)])
-        for step in range(1, ring)
+        for step in (1, 3, 2)
     )
     chunk = (chunk + two) + (one + three)
     mine = lax.all_to_all(

time: 73.4 us -> 81.6 us (1.11)
  Pallas kernels: 14.6 us -> 23.7 us
  local copies, waits for them, and re-layouts: 1.88 us -> 0.83 us
    pallas_call x0 -> x1, Pallas kernels: none -> 9.09 us  [other_half(): pl.pallas_call(half_kernel, out_shape=jax.ShapeDtypeStruct((rows, columns...]
    unnamed x4, local copies, waits for them, and re-layouts: 1.04 us -> 0.01 us
where the time goes in v7:
time: 81.6 us; the launch traced here: 81.4 us
  blocking collectives  28.6 us (35%)
  Pallas kernels  23.7 us (29%)
  waiting for transfers between devices  15.9 us (19%)
  starting transfers between devices  11 us (13%)
  local copies, waits for them, and re-layouts  0.83 us (1%)
    all_to_all x1, blocking collectives, per_device(): lax.all_to_all(partial.reshape(peers, -1, GROUP), plane, split_axis=0, co...  16.3 us
    pallas_call x1, Pallas kernels, solve(): pl.pallas_call(solve_kernel, out_shape=(jax.ShapeDtypeStruct((BLOCKS * GR...  13 us
    all_to_all x1, blocking collectives, per_device(): lax.all_to_all(jnp.broadcast_to(chunk[None], (peers, *chunk.shape)), plan...  12.3 us
    pallas_call x1, Pallas kernels, other_half(): pl.pallas_call(half_kernel, out_shape=jax.ShapeDtypeStruct((rows, columns...  9.09 us
    ppermute x1, waiting for transfers between devices, per_device(): far = lax.ppermute(send, 'high', SWAP)  6.4 us
    ppermute x3, starting transfers between devices, per_device(): lax.ppermute(chunk, 'z', [(n, (n + step) % ring) for n in range(ring)])  5.97 us
    ppermute x3, waiting for transfers between devices, per_device(): lax.ppermute(chunk, 'z', [(n, (n + step) % ring) for n in range(ring)])  3.42 us
    ppermute x1, starting transfers between devices, per_device(): far = lax.ppermute(send, 'high', SWAP)  3.36 us
  transfers between devices with their start and end apart: 8, of which 6 were waited for; matrix products, arithmetic and copies ran while one was open for 1% of the time, Pallas kernels for 0%

profile of v7, /device:TPU:0, one launch (start us, length us, event | category | flops | bytes accessed | tf_op | source)
XLA Modules:
  0.0 81.4 jit_solution(3205044809970545392)
XLA Ops:
  0.6 9.1 %other_half.1 = bf16[128,1024]{1,0:T(8,128)(2,1)} custom-call(bf16[128,2048]{1,0:T(8,128)(2,1)} %source_ref.1), custom_call_target="tpu_custom_call" | custom-call | tf_op jit(solution)/shard_map/other_half/pallas_call | solution.py:251
  9.7 3.4 %collective-permute-start = (bf16[128,1024]{1,0:T(8,128)(2,1)}, bf16[128,1024]{1,0:T(8,128)(2,1)S(1)}, u32[]{:S(2)}, u32[]{:S(2)}) collective-permute-start(bf16[128,1024]{1,0:T(8,128)(2,1)} %other_half.1), channel_id=1, source_target_pairs={{0,64},{64,0},{1,65},{65,1},{2,66},{66,2},{3,67},{67,3},{4,68},{68... | collective-permute-start | bytes 786440 | tf_op jit(solution)/shard_map/ppermute | solution.py:304
  13.1 0.1 collective-permute-start.1
  13.2 6.4 %collective-permute-done.b_ref = bf16[128,1024]{1,0:T(8,128)(2,1)S(1)} collective-permute-done((bf16[128,1024]{1,0:T(8,128)(2,1)}, bf16[128,1024]{1,0:T(8,128)(2,1)S(1)}, u32[]{:S(2)}, u32[]{:S(2)}) %collective-permute-start) | collective-permute-done | bytes 262176 | tf_op jit(solution)/shard_map/ppermute | solution.py:304
  19.6 0.0 collective-permute-start.2
  19.6 0.1 stack.31.place_ref
  19.7 0.0 collective-permute-done.1.c_ref
  19.7 1.4 %collective-permute-done.2.d_ref = bf16[128,1024]{1,0:T(8,128)(2,1)S(1)} collective-permute-done((bf16[128,1024]{1,0:T(8,128)(2,1)S(1)}, bf16[128,1024]{1,0:T(8,128)(2,1)S(1)}, u32[]{:S(2)}, u32[]{:S(2)}) %collective-permute-start.2) | collective-permute-done | bytes 262176 | tf_op jit(solution)/shard_map/ppermute | solution.py:306
  21.1 0.1 broadcast_in_dim.4.e_ref
  21.2 1.6 %center_gram.1 = (bf16[512,1024]{1,0:T(8,128)(2,1)S(1)}, f32[640,128]{1,0:T(8,128)S(1)}) custom-call(s32[7]{0:T(128)S(1)} %stack.31.place_ref, f32[128,128]{1,0:T(8,128)S(1)} %broadcast_in_dim.4.e_ref, bf16[128,1024]{1,0:T(8,128)(2,1)S(1)} %constant_dynamic-slice_fusion.a_ref, bf16[128,1024]{1,0:T(8,128)(2,1)S(1)} %collective-permute-done.b_ref, ...), custom_call_target="tpu_custom_call" | custom-call | tf_op jit(solution)/shard_map/center_gram/pallas_call | solution.py:264
  22.8 16.3 %all_to_all.10 = f32[16,40,128]{2,1,0:T(8,128)S(1)} all-to-all(f32[16,40,128]{2,1,0:T(8,128)S(1)} %bitcast.12), channel_id=1, replica_groups=mesh['high'=2,'core'=2,'z'=4,'x'=4,'low'=2] {'high','x','low'}, dimensions={0} | all-to-all | bytes 655360 | tf_op jit(solution)/shard_map/all_to_all | solution.py:322
  39.2 4.1 %collective-permute-start.5 = (f32[40,128]{1,0:T(8,128)S(1)}, f32[40,128]{1,0:T(8,128)S(1)}, u32[]{:S(2)}, u32[]{:S(2)}) collective-permute-start(f32[40,128]{1,0:T(8,128)S(1)} %reduce_sum.9), channel_id=1, source_target_pairs={{0,24},{8,0},{16,8},{24,16},{1,25},{9,1},{17,9},{25,17},{2,26},{10... | collective-permute-start | bytes 61448 | tf_op jit(solution)/shard_map/ppermute | solution.py:328
  43.3 0.0 collective-permute-start.4
  43.3 1.9 %collective-permute-start.3 = (f32[40,128]{1,0:T(8,128)S(1)}, f32[40,128]{1,0:T(8,128)S(1)}, u32[]{:S(2)}, u32[]{:S(2)}) collective-permute-start(f32[40,128]{1,0:T(8,128)S(1)} %reduce_sum.9), channel_id=1, source_target_pairs={{0,16},{8,24},{16,0},{24,8},{1,17},{9,25},{17,1},{25,9},{2,18},{10... | collective-permute-start | bytes 61448 | tf_op jit(solution)/shard_map/ppermute | solution.py:328
  45.1 0.0 collective-permute-done.5
  45.1 3.1 %collective-permute-done.4 = f32[40,128]{1,0:T(8,128)S(1)} collective-permute-done((f32[40,128]{1,0:T(8,128)S(1)}, f32[40,128]{1,0:T(8,128)S(1)}, u32[]{:S(2)}, u32[]{:S(2)}) %collective-permute-start.4) | collective-permute-done | bytes 20512 | tf_op jit(solution)/shard_map/ppermute | solution.py:328
  48.3 0.3 collective-permute-done.3
  48.6 12.3 %all_to_all.11 = f32[16,40,128]{2,1,0:T(8,128)S(1)} all-to-all(f32[16,40,128]{2,1,0:T(8,128)S(1)} %broadcast_in_dim.5), channel_id=1, replica_groups=mesh['high'=2,'core'=2,'z'=4,'x'=4,'low'=2] {'high','x','low'}, dimensions={0} | all-to-all | bytes 655360 | tf_op jit(solution)/shard_map/all_to_all | solution.py:332
  60.9 1.6 %collective-permute-done.6.other_ref = f32[640,128]{1,0:T(8,128)S(1)} collective-permute-done((f32[640,128]{1,0:T(8,128)S(1)}, f32[640,128]{1,0:T(8,128)S(1)}, u32[]{:S(2)}, u32[]{:S(2)}) %collective-permute-start.6) | collective-permute-done | bytes 327712 | tf_op jit(solution)/shard_map/ppermute | solution.py:339
  62.5 13.0 %solve.1 = (f32[512,128]{1,0:T(8,128)S(1)}, f32[1,1024]{1,0:T(1,128)S(1)}) custom-call(s32[7]{0:T(128)S(1)} %stack.31.place_ref, f32[640,128]{1,0:T(8,128)S(1)} %bitcast.11, f32[640,128]{1,0:T(8,128)S(1)} %collective-permute-done.6.other_ref, bf16[512,1024]{1,0:T(8,128)(2,1)S(1)} %get-tuple-element.7.cent_ref), custom_call_target="tpu_custom_call" | custom-call | tf_op jit(solution)/shard_map/solve/pallas_call | solution.py:278
  75.6 1.5 %collective-permute-start.7 = (f32[1024]{0:T(1024)S(1)}, f32[1024]{0:T(1024)S(1)}, u32[]{:S(2)}, u32[]{:S(2)}) collective-permute-start(f32[1024]{0:T(1024)S(1)} %bitcast.13), channel_id=1, source_target_pairs={{0,64},{64,0},{1,65},{65,1},{2,66},{66,2},{3,67},{67,3},{4,68},{68... | collective-permute-start | bytes 12296 | tf_op jit(solution)/shard_map/ppermute | solution.py:343
  77.1 0.6 dynamic-slice_reduce_fusion
  77.8 3.0 %collective-permute-done.7 = f32[1024]{0:T(1024)S(1)} collective-permute-done((f32[1024]{0:T(1024)S(1)}, f32[1024]{0:T(1024)S(1)}, u32[]{:S(2)}, u32[]{:S(2)}) %collective-permute-start.7) | collective-permute-done | bytes 4128 | tf_op jit(solution)/shard_map/ppermute | solution.py:343
  80.8 0.6 pad_maximum_fusion
  (11 shorter events, 0.1 us)
Async XLA Ops:
  0.6 12.5 %copy-start = (bf16[128,2048]{1,0:T(8,128)(2,1)S(1)}, bf16[128,2048]{1,0:T(8,128)(2,1)}, u32[]{:S(2)}) copy-start(bf16[128,2048]{1,0:T(8,128)(2,1)} %source_ref.1) | copy-start | bytes 1572868
  9.7 9.9 %collective-permute-start = (bf16[128,1024]{1,0:T(8,128)(2,1)}, bf16[128,1024]{1,0:T(8,128)(2,1)S(1)}, u32[]{:S(2)}, u32[]{:S(2)}) collective-permute-start(bf16[128,1024]{1,0:T(8,128)(2,1)} %other_half.1), channel_id=1, source_target_pairs={{0,64},{64,0},{1,65},{65,1},{2,66},{66,2},{3,67},{67,3},{4,68},{68... | collective-permute-start | bytes 786440 | tf_op jit(solution)/shard_map/ppermute | solution.py:304
  13.1 6.6 %collective-permute-start.1 = (bf16[128,1024]{1,0:T(8,128)(2,1)S(1)}, bf16[128,1024]{1,0:T(8,128)(2,1)S(1)}, u32[]{:S(2)}, u32[]{:S(2)}) collective-permute-start(bf16[128,1024]{1,0:T(8,128)(2,1)S(1)} %constant_dynamic-slice_fusion.a_ref), channel_id=1, source_target_pairs={{0,32},{32,0},{1,33},{33,1},{2,34},{34,2},{3,35},{35,3},{4,36},{36... | collective-permute-start | bytes 786440 | tf_op jit(solution)/shard_map/ppermute | solution.py:305
  19.6 1.5 %collective-permute-start.2 = (bf16[128,1024]{1,0:T(8,128)(2,1)S(1)}, bf16[128,1024]{1,0:T(8,128)(2,1)S(1)}, u32[]{:S(2)}, u32[]{:S(2)}) collective-permute-start(bf16[128,1024]{1,0:T(8,128)(2,1)S(1)} %collective-permute-done.b_ref), channel_id=1, source_target_pairs={{0,32},{32,0},{1,33},{33,1},{2,34},{34,2},{3,35},{35,3},{4,36},{36... | collective-permute-start | bytes 786440 | tf_op jit(solution)/shard_map/ppermute | solution.py:306
  19.6 1.5 %copy-start.1 = (f32[128]{0:T(128)S(1)}, f32[128]{0:T(128)}, u32[]{:S(2)}) copy-start(f32[128]{0:T(128)} %param.3) | copy-start | bytes 1540
  39.2 6.0 %collective-permute-start.5 = (f32[40,128]{1,0:T(8,128)S(1)}, f32[40,128]{1,0:T(8,128)S(1)}, u32[]{:S(2)}, u32[]{:S(2)}) collective-permute-start(f32[40,128]{1,0:T(8,128)S(1)} %reduce_sum.9), channel_id=1, source_target_pairs={{0,24},{8,0},{16,8},{24,16},{1,25},{9,1},{17,9},{25,17},{2,26},{10... | collective-permute-start | bytes 61448 | tf_op jit(solution)/shard_map/ppermute | solution.py:328
  43.3 5.0 %collective-permute-start.4 = (f32[40,128]{1,0:T(8,128)S(1)}, f32[40,128]{1,0:T(8,128)S(1)}, u32[]{:S(2)}, u32[]{:S(2)}) collective-permute-start(f32[40,128]{1,0:T(8,128)S(1)} %reduce_sum.9), channel_id=1, source_target_pairs={{0,8},{8,16},{16,24},{24,0},{1,9},{9,17},{17,25},{25,1},{2,10},{10... | collective-permute-start | bytes 61448 | tf_op jit(solution)/shard_map/ppermute | solution.py:328
  43.3 5.3 %collective-permute-start.3 = (f32[40,128]{1,0:T(8,128)S(1)}, f32[40,128]{1,0:T(8,128)S(1)}, u32[]{:S(2)}, u32[]{:S(2)}) collective-permute-start(f32[40,128]{1,0:T(8,128)S(1)} %reduce_sum.9), channel_id=1, source_target_pairs={{0,16},{8,24},{16,0},{24,8},{1,17},{9,25},{17,1},{25,9},{2,18},{10... | collective-permute-start | bytes 61448 | tf_op jit(solution)/shard_map/ppermute | solution.py:328
  60.9 1.6 %collective-permute-start.6 = (f32[640,128]{1,0:T(8,128)S(1)}, f32[640,128]{1,0:T(8,128)S(1)}, u32[]{:S(2)}, u32[]{:S(2)}) collective-permute-start(f32[640,128]{1,0:T(8,128)S(1)} %bitcast.10), channel_id=1, source_target_pairs={{0,32},{32,0},{1,33},{33,1},{2,34},{34,2},{3,35},{35,3},{4,36},{36... | collective-permute-start | bytes 983048 | tf_op jit(solution)/shard_map/ppermute | solution.py:339
  75.6 5.2 %collective-permute-start.7 = (f32[1024]{0:T(1024)S(1)}, f32[1024]{0:T(1024)S(1)}, u32[]{:S(2)}, u32[]{:S(2)}) collective-permute-start(f32[1024]{0:T(1024)S(1)} %bitcast.13), channel_id=1, source_target_pairs={{0,64},{64,0},{1,65},{65,1},{2,66},{66,2},{3,67},{67,3},{4,68},{68... | collective-permute-start | bytes 12296 | tf_op jit(solution)/shard_map/ppermute | solution.py:343

commit v8 on v6

--- a/solution.py
+++ b/solution.py
@@ -147,20 +147,12 @@
     )
 
 
-def solve_kernel(
-    place_ref, mine_ref, other_ref, cent_ref, coeff_ref, update_ref, gram, rest
-):
+def solve_kernel(parts_ref, cent_ref, coeff_ref, update_ref, gram, rest):
     blocks = BLOCKS
     for core, held in enumerate(LISTS):
-        for mine, ref in ((core, mine_ref), (1 - core, other_ref)):
-
-            @pl.when(place_ref[4] == mine)
-            def _():
-                for n, (r, c) in enumerate(held):
-                    gram[r, :, GROUP * c : GROUP * c + GROUP] = ref[
-                        GROUP * n : GROUP * n + GROUP, :
-                    ]
-
+        for n, (r, c) in enumerate(held):
+            start = GROUP * (HELD * core + n)
+            gram[r, :, GROUP * c : GROUP * c + GROUP] = parts_ref[start : start + GROUP, :]
     energy_sum = jnp.zeros((ROWS, GROUP), jnp.float32)
     for core, held in enumerate(LISTS):
         for high, k in enumerate(r for r, c in held if r == c):
@@ -243,14 +235,14 @@
     )(place, energies, *parts)
 
 
-def solve(place, mine, other, cent):
+def solve(blocks, cent):
     return pl.pallas_call(
         solve_kernel,
         out_shape=(
             jax.ShapeDtypeStruct((BLOCKS * GROUP, GROUP), jnp.float32),
             jax.ShapeDtypeStruct((1, cent.shape[1]), jnp.float32),
         ),
-        in_specs=[SMEM] + [VMEM] * 3,
+        in_specs=[VMEM] * 2,
         out_specs=(VMEM, VMEM),
         scratch_shapes=[
             pltpu.VMEM((BLOCKS, GROUP, (BLOCKS + 1) * GROUP), jnp.float32),
@@ -258,7 +250,7 @@
         ],
         compiler_params=pltpu.CompilerParams(vmem_limit_bytes=32 * 1024 * 1024),
         name="solve",
-    )(place, mine, other, cent)
+    )(blocks, cent)
 
 
 SWAP = [(0, 1), (1, 0)]
@@ -299,15 +291,15 @@
         for step in range(1, ring)
     )
     chunk = (chunk + two) + (one + three)
-    mine = lax.all_to_all(
-        jnp.broadcast_to(chunk[None], (peers, *chunk.shape)),
-        plane,
+    everyone = ("core",) + plane
+    blocks = lax.all_to_all(
+        jnp.broadcast_to(chunk[None], (lax.axis_size(everyone), *chunk.shape)),
+        everyone,
         split_axis=0,
         concat_axis=0,
         tiled=True,
-    ).reshape(HELD * GROUP, GROUP)
-    other = lax.ppermute(mine, "core", SWAP)
-    coeffs, update = solve(place, mine, other, cent)
+    ).reshape(2 * HELD * GROUP, GROUP)
+    coeffs, update = solve(blocks, cent)
     own = lax.dynamic_slice_in_dim(coeffs, (2 * high + core) * GROUP, GROUP, 0)[:, 0]
     update = update[0] * math.sqrt(2 * half * lax.axis_size(("z", "x", "low")))
     away = lax.ppermute(update, "high", SWAP)

time: 73.4 us -> 75.6 us (1.030)
  blocking collectives: 28.6 us -> 33.2 us
  waiting for transfers between devices: 15.7 us -> 14.3 us
  Pallas kernels: 14.6 us -> 13.8 us
    all_to_all x1, blocking collectives: 12.3 us -> 16.9 us  [per_device(): lax.all_to_all(jnp.broadcast_to(chunk[None], (lax.axis_size(everyone), *c...]
    ppermute x1 -> x0, waiting for transfers between devices: 1.63 us -> none  [per_device(): other = lax.ppermute(mine, 'core', SWAP)]
    pallas_call x1, Pallas kernels: 13 us -> 12.2 us  [solve(): pl.pallas_call(solve_kernel, out_shape=(jax.ShapeDtypeStruct((BLOCKS * GR...]
  transfers between devices with their start and end apart: 8 -> 7, of which waited for: 6 -> 5; matrix products, arithmetic and copies ran while one was open for 1% -> 1% of each run, Pallas kernels for 0% -> 0%
where the time goes in v8:
time: 75.6 us; the launch traced here: 75.3 us
  blocking collectives  33.2 us (44%)
  waiting for transfers between devices  14.3 us (19%)
  Pallas kernels  13.8 us (18%)
  starting transfers between devices  10.7 us (14%)
  local copies, waits for them, and re-layouts  1.9 us (3%)
    all_to_all x1, blocking collectives, per_device(): lax.all_to_all(jnp.broadcast_to(chunk[None], (lax.axis_size(everyone), *c...  16.9 us
    all_to_all x1, blocking collectives, per_device(): lax.all_to_all(partial.reshape(peers, -1, GROUP), plane, split_axis=0, co...  16.3 us
    pallas_call x1, Pallas kernels, solve(): pl.pallas_call(solve_kernel, out_shape=(jax.ShapeDtypeStruct((BLOCKS * GR...  12.2 us
    ppermute x1, waiting for transfers between devices, per_device(): far = lax.ppermute(send, 'high', SWAP)  6.19 us
    ppermute x3, starting transfers between devices, per_device(): lax.ppermute(chunk, 'z', [(n, (n + step) % ring) for n in range(ring)])  5.97 us
    ppermute x3, waiting for transfers between devices, per_device(): lax.ppermute(chunk, 'z', [(n, (n + step) % ring) for n in range(ring)])  3.43 us
    ppermute x1, starting transfers between devices, per_device(): far = lax.ppermute(send, 'high', SWAP)  3.36 us
    ppermute x1, waiting for transfers between devices, per_device(): away = lax.ppermute(update, 'high', SWAP)  3.23 us
  transfers between devices with their start and end apart: 7, of which 5 were waited for; matrix products, arithmetic and copies ran while one was open for 1% of the time, Pallas kernels for 0%

profile of v8, /device:TPU:0, one launch (start us, length us, event | category | flops | bytes accessed | tf_op | source)
XLA Modules:
  0.0 75.3 jit_solution(4126128560099026663)
XLA Ops:
  0.6 0.0 copy-start
  0.7 1.0 %copy-done = bf16[128,2048]{1,0:T(8,128)(2,1)S(1)} copy-done((bf16[128,2048]{1,0:T(8,128)(2,1)S(1)}, bf16[128,2048]{1,0:T(8,128)(2,1)}, u32[]{:S(2)}) %copy-start) | copy-done | bytes 524312
  1.7 3.4 %collective-permute-start = (bf16[128,1024]{1,0:T(8,128)(2,1)S(1)}, bf16[128,1024]{1,0:T(8,128)(2,1)S(1)}, u32[]{:S(2)}, u32[]{:S(2)}) collective-permute-start(bf16[128,1024]{1,0:T(8,128)(2,1)S(1)} %constant_dynamic-slice_fusion.1), channel_id=1, source_target_pairs={{0,64},{64,0},{1,65},{65,1},{2,66},{66,2},{3,67},{67,3},{4,68},{68... | collective-permute-start | bytes 786440 | tf_op jit(solution)/shard_map/ppermute | solution.py:266
  5.1 0.1 collective-permute-start.1
  5.2 6.2 %collective-permute-done.b_ref = bf16[128,1024]{1,0:T(8,128)(2,1)S(1)} collective-permute-done((bf16[128,1024]{1,0:T(8,128)(2,1)S(1)}, bf16[128,1024]{1,0:T(8,128)(2,1)S(1)}, u32[]{:S(2)}, u32[]{:S(2)}) %collective-permute-start) | collective-permute-done | bytes 262176 | tf_op jit(solution)/shard_map/ppermute | solution.py:266
  11.4 0.0 collective-permute-start.2
  11.4 0.1 stack.31.place_ref
  11.5 0.0 collective-permute-done.1.c_ref
  11.5 1.4 %collective-permute-done.2.d_ref = bf16[128,1024]{1,0:T(8,128)(2,1)S(1)} collective-permute-done((bf16[128,1024]{1,0:T(8,128)(2,1)S(1)}, bf16[128,1024]{1,0:T(8,128)(2,1)S(1)}, u32[]{:S(2)}, u32[]{:S(2)}) %collective-permute-start.2) | collective-permute-done | bytes 262176 | tf_op jit(solution)/shard_map/ppermute | solution.py:268
  12.9 0.1 broadcast_in_dim.4.e_ref
  13.0 1.6 %center_gram.1 = (bf16[512,1024]{1,0:T(8,128)(2,1)S(1)}, f32[640,128]{1,0:T(8,128)S(1)}) custom-call(s32[7]{0:T(128)S(1)} %stack.31.place_ref, f32[128,128]{1,0:T(8,128)S(1)} %broadcast_in_dim.4.e_ref, bf16[128,1024]{1,0:T(8,128)(2,1)S(1)} %constant_dynamic-slice_fusion.a_ref, bf16[128,1024]{1,0:T(8,128)(2,1)S(1)} %collective-permute-done.b_ref, ...), custom_call_target="tpu_custom_call" | custom-call | tf_op jit(solution)/shard_map/center_gram/pallas_call | solution.py:225
  14.6 16.3 %all_to_all.10 = f32[16,40,128]{2,1,0:T(8,128)S(1)} all-to-all(f32[16,40,128]{2,1,0:T(8,128)S(1)} %bitcast.11), channel_id=1, replica_groups=mesh['high'=2,'core'=2,'z'=4,'x'=4,'low'=2] {'high','x','low'}, dimensions={0} | all-to-all | bytes 655360 | tf_op jit(solution)/shard_map/all_to_all | solution.py:284
  30.9 4.1 %collective-permute-start.5 = (f32[40,128]{1,0:T(8,128)S(1)}, f32[40,128]{1,0:T(8,128)S(1)}, u32[]{:S(2)}, u32[]{:S(2)}) collective-permute-start(f32[40,128]{1,0:T(8,128)S(1)} %reduce_sum.9), channel_id=1, source_target_pairs={{0,24},{8,0},{16,8},{24,16},{1,25},{9,1},{17,9},{25,17},{2,26},{10... | collective-permute-start | bytes 61448 | tf_op jit(solution)/shard_map/ppermute | solution.py:290
  35.0 0.0 collective-permute-start.4
  35.0 1.9 %collective-permute-start.3 = (f32[40,128]{1,0:T(8,128)S(1)}, f32[40,128]{1,0:T(8,128)S(1)}, u32[]{:S(2)}, u32[]{:S(2)}) collective-permute-start(f32[40,128]{1,0:T(8,128)S(1)} %reduce_sum.9), channel_id=1, source_target_pairs={{0,16},{8,24},{16,0},{24,8},{1,17},{9,25},{17,1},{25,9},{2,18},{10... | collective-permute-start | bytes 61448 | tf_op jit(solution)/shard_map/ppermute | solution.py:290
  36.9 0.0 collective-permute-done.5
  36.9 3.1 %collective-permute-done.4 = f32[40,128]{1,0:T(8,128)S(1)} collective-permute-done((f32[40,128]{1,0:T(8,128)S(1)}, f32[40,128]{1,0:T(8,128)S(1)}, u32[]{:S(2)}, u32[]{:S(2)}) %collective-permute-start.4) | collective-permute-done | bytes 20512 | tf_op jit(solution)/shard_map/ppermute | solution.py:290
  40.0 0.3 collective-permute-done.3
  40.4 16.9 %all_to_all.11 = f32[32,40,128]{2,1,0:T(8,128)S(1)} all-to-all(f32[32,40,128]{2,1,0:T(8,128)S(1)} %broadcast_in_dim.5), channel_id=1, replica_groups=mesh['high'=2,'core'=2,'z'=4,'x'=4,'low'=2] {'core','high','x','low'}, dimensions={0} | all-to-all | bytes 1310720 | tf_op jit(solution)/shard_map/all_to_all | solution.py:295
  57.3 12.2 %solve.1 = (f32[512,128]{1,0:T(8,128)S(1)}, f32[1,1024]{1,0:T(1,128)S(1)}) custom-call(f32[1280,128]{1,0:T(8,128)S(1)} %bitcast.10, bf16[512,1024]{1,0:T(8,128)(2,1)S(1)} %get-tuple-element.11.cent_ref), custom_call_target="tpu_custom_call" | custom-call | tf_op jit(solution)/shard_map/solve/pallas_call | solution.py:239
  69.5 1.3 %collective-permute-start.6 = (f32[1024]{0:T(1024)S(1)}, f32[1024]{0:T(1024)S(1)}, u32[]{:S(2)}, u32[]{:S(2)}) collective-permute-start(f32[1024]{0:T(1024)S(1)} %bitcast.12), channel_id=1, source_target_pairs={{0,64},{64,0},{1,65},{65,1},{2,66},{66,2},{3,67},{67,3},{4,68},{68... | collective-permute-start | bytes 12296 | tf_op jit(solution)/shard_map/ppermute | solution.py:305
  70.8 0.6 dynamic-slice_reduce_fusion
  71.5 3.2 %collective-permute-done.6 = f32[1024]{0:T(1024)S(1)} collective-permute-done((f32[1024]{0:T(1024)S(1)}, f32[1024]{0:T(1024)S(1)}, u32[]{:S(2)}, u32[]{:S(2)}) %collective-permute-start.6) | collective-permute-done | bytes 4128 | tf_op jit(solution)/shard_map/ppermute | solution.py:305
  74.7 0.6 pad_maximum_fusion
  (9 shorter events, 0.1 us)
Async XLA Ops:
  0.6 1.0 %copy-start = (bf16[128,2048]{1,0:T(8,128)(2,1)S(1)}, bf16[128,2048]{1,0:T(8,128)(2,1)}, u32[]{:S(2)}) copy-start(bf16[128,2048]{1,0:T(8,128)(2,1)} %param.2) | copy-start | bytes 1572868
  1.7 9.7 %collective-permute-start = (bf16[128,1024]{1,0:T(8,128)(2,1)S(1)}, bf16[128,1024]{1,0:T(8,128)(2,1)S(1)}, u32[]{:S(2)}, u32[]{:S(2)}) collective-permute-start(bf16[128,1024]{1,0:T(8,128)(2,1)S(1)} %constant_dynamic-slice_fusion.1), channel_id=1, source_target_pairs={{0,64},{64,0},{1,65},{65,1},{2,66},{66,2},{3,67},{67,3},{4,68},{68... | collective-permute-start | bytes 786440 | tf_op jit(solution)/shard_map/ppermute | solution.py:266
  5.1 6.4 %collective-permute-start.1 = (bf16[128,1024]{1,0:T(8,128)(2,1)S(1)}, bf16[128,1024]{1,0:T(8,128)(2,1)S(1)}, u32[]{:S(2)}, u32[]{:S(2)}) collective-permute-start(bf16[128,1024]{1,0:T(8,128)(2,1)S(1)} %constant_dynamic-slice_fusion.a_ref), channel_id=1, source_target_pairs={{0,32},{32,0},{1,33},{33,1},{2,34},{34,2},{3,35},{35,3},{4,36},{36... | collective-permute-start | bytes 786440 | tf_op jit(solution)/shard_map/ppermute | solution.py:267
  11.4 1.5 %collective-permute-start.2 = (bf16[128,1024]{1,0:T(8,128)(2,1)S(1)}, bf16[128,1024]{1,0:T(8,128)(2,1)S(1)}, u32[]{:S(2)}, u32[]{:S(2)}) collective-permute-start(bf16[128,1024]{1,0:T(8,128)(2,1)S(1)} %collective-permute-done.b_ref), channel_id=1, source_target_pairs={{0,32},{32,0},{1,33},{33,1},{2,34},{34,2},{3,35},{35,3},{4,36},{36... | collective-permute-start | bytes 786440 | tf_op jit(solution)/shard_map/ppermute | solution.py:268
  11.4 1.5 %copy-start.1 = (f32[128]{0:T(128)S(1)}, f32[128]{0:T(128)}, u32[]{:S(2)}) copy-start(f32[128]{0:T(128)} %param.3) | copy-start | bytes 1540
  30.9 6.0 %collective-permute-start.5 = (f32[40,128]{1,0:T(8,128)S(1)}, f32[40,128]{1,0:T(8,128)S(1)}, u32[]{:S(2)}, u32[]{:S(2)}) collective-permute-start(f32[40,128]{1,0:T(8,128)S(1)} %reduce_sum.9), channel_id=1, source_target_pairs={{0,24},{8,0},{16,8},{24,16},{1,25},{9,1},{17,9},{25,17},{2,26},{10... | collective-permute-start | bytes 61448 | tf_op jit(solution)/shard_map/ppermute | solution.py:290
  35.0 5.0 %collective-permute-start.4 = (f32[40,128]{1,0:T(8,128)S(1)}, f32[40,128]{1,0:T(8,128)S(1)}, u32[]{:S(2)}, u32[]{:S(2)}) collective-permute-start(f32[40,128]{1,0:T(8,128)S(1)} %reduce_sum.9), channel_id=1, source_target_pairs={{0,8},{8,16},{16,24},{24,0},{1,9},{9,17},{17,25},{25,1},{2,10},{10... | collective-permute-start | bytes 61448 | tf_op jit(solution)/shard_map/ppermute | solution.py:290
  35.0 5.3 %collective-permute-start.3 = (f32[40,128]{1,0:T(8,128)S(1)}, f32[40,128]{1,0:T(8,128)S(1)}, u32[]{:S(2)}, u32[]{:S(2)}) collective-permute-start(f32[40,128]{1,0:T(8,128)S(1)} %reduce_sum.9), channel_id=1, source_target_pairs={{0,16},{8,24},{16,0},{24,8},{1,17},{9,25},{17,1},{25,9},{2,18},{10... | collective-permute-start | bytes 61448 | tf_op jit(solution)/shard_map/ppermute | solution.py:290
  69.5 5.2 %collective-permute-start.6 = (f32[1024]{0:T(1024)S(1)}, f32[1024]{0:T(1024)S(1)}, u32[]{:S(2)}, u32[]{:S(2)}) collective-permute-start(f32[1024]{0:T(1024)S(1)} %bitcast.12), channel_id=1, source_target_pairs={{0,64},{64,0},{1,65},{65,1},{2,66},{66,2},{3,67},{67,3},{4,68},{68... | collective-permute-start | bytes 12296 | tf_op jit(solution)/shard_map/ppermute | solution.py:305

commit v9 on v6

--- a/solution.py
+++ b/solution.py
@@ -21,23 +21,28 @@
 SPARE, SPAN = GROUP // 2, 16
 
 
-def center_gram_kernel(place_ref, e_ref, a_ref, b_ref, c_ref, d_ref, cent_ref, out_ref):
+def center_gram_kernel(e_ref, a_ref, b_ref, c_ref, d_ref, cent_ref, out_ref):
     total = BLOCKS * GROUP
     scale = 1.0 / math.sqrt(total)
     parts = (a_ref, b_ref, c_ref, d_ref)
-    column_sum = None
-    for part in parts:
-        piece = jnp.sum(part[...].astype(jnp.float32), axis=0, keepdims=True)
-        column_sum = piece if column_sum is None else column_sum + piece
-    mean = column_sum / total
+    high, core = lax.axis_index("high"), lax.axis_index("core")
+    groups = (
+        2 * high + core,
+        2 * (1 - high) + core,
+        2 * high + 1 - core,
+        2 * (1 - high) + 1 - core,
+    )
+    sums = [jnp.sum(part[...].astype(jnp.float32), axis=0, keepdims=True) for part in parts]
+    mean = ((sums[0] + sums[2]) + (sums[1] + sums[3])) / total
     for number, part in enumerate(parts):
-        start = pl.multiple_of(place_ref[number] * GROUP, GROUP)
+        start = pl.multiple_of(groups[number] * GROUP, GROUP)
         cent_ref[pl.ds(start, GROUP), :] = (
             (part[...].astype(jnp.float32) - mean) * scale
         ).astype(jnp.bfloat16)
-    for core, strips in enumerate(STRIPS):
-
-        @pl.when(place_ref[4] == core)
+    first_slab = lax.axis_index(("z", "x", "low")) == 0
+    for half, strips in enumerate(STRIPS):
+
+        @pl.when(core == half)
         def _():
             at = 0
             for r, c, wide in strips:
@@ -53,9 +58,9 @@
 
             column = lax.broadcasted_iota(jnp.int32, (SPARE, GROUP), 1)
             pair = jnp.where(column < SPAN, e_ref[:SPARE, :], e_ref[SPARE:, :])
-            diagonals = [n for n, (r, c) in enumerate(LISTS[core]) if r == c]
-            for high, n in enumerate(diagonals):
-                mine = (place_ref[5] == high) & (place_ref[6] == 0)
+            diagonals = [n for n, (r, c) in enumerate(LISTS[half]) if r == c]
+            for group, n in enumerate(diagonals):
+                mine = (high == group) & first_slab
                 rows = slice(GROUP * n + SPARE, GROUP * (n + 1))
                 out_ref[rows, :] = jnp.where(
                     column < 2 * SPAN, jnp.where(mine, pair, 0.0), out_ref[rows, :]
@@ -102,8 +107,8 @@
                 for t in range(m // ROWS, WIDE):
                     held[m, t] = held[m, t] - factor[t] * spread[m]
             for t in range(home, WIDE):
-                part = jnp.where(line > at, factor[t], 0.0) if t == home else factor[t]
-                work[t] = work[t] - part * pivot_row
+                change = work[t] - factor[t] * pivot_row
+                work[t] = jnp.where(line > at, change, work[t]) if t == home else change
             for i in after:
                 part = next_held[j, i] * recip
                 for m in range(j + 1, size):
@@ -148,19 +153,17 @@
 
 
 def solve_kernel(
-    place_ref, mine_ref, other_ref, cent_ref, coeff_ref, update_ref, gram, rest
+    mine_ref, other_ref, cent_ref, coeff_ref, update_ref, parts, gram, rest
 ):
     blocks = BLOCKS
+    core = lax.axis_index("core")
+    parts[core] = mine_ref[...]
+    parts[1 - core] = other_ref[...]
     for core, held in enumerate(LISTS):
-        for mine, ref in ((core, mine_ref), (1 - core, other_ref)):
-
-            @pl.when(place_ref[4] == mine)
-            def _():
-                for n, (r, c) in enumerate(held):
-                    gram[r, :, GROUP * c : GROUP * c + GROUP] = ref[
-                        GROUP * n : GROUP * n + GROUP, :
-                    ]
-
+        for n, (r, c) in enumerate(held):
+            gram[r, :, GROUP * c : GROUP * c + GROUP] = parts[
+                core, GROUP * n : GROUP * n + GROUP, :
+            ]
     energy_sum = jnp.zeros((ROWS, GROUP), jnp.float32)
     for core, held in enumerate(LISTS):
         for high, k in enumerate(r for r, c in held if r == c):
@@ -225,10 +228,9 @@
 
 
 VMEM = pl.BlockSpec(memory_space=pltpu.VMEM)
-SMEM = pl.BlockSpec(memory_space=pltpu.SMEM)
-
-
-def center_gram(place, energies, parts):
+
+
+def center_gram(energies, parts):
     columns = parts[0].shape[1]
     return pl.pallas_call(
         center_gram_kernel,
@@ -236,29 +238,30 @@
             jax.ShapeDtypeStruct((BLOCKS * GROUP, columns), jnp.bfloat16),
             jax.ShapeDtypeStruct((HELD * GROUP, GROUP), jnp.float32),
         ),
-        in_specs=[SMEM] + [VMEM] * 5,
+        in_specs=[VMEM] * 5,
         out_specs=(VMEM, VMEM),
         compiler_params=pltpu.CompilerParams(vmem_limit_bytes=32 * 1024 * 1024),
         name="center_gram",
-    )(place, energies, *parts)
-
-
-def solve(place, mine, other, cent):
+    )(energies, *parts)
+
+
+def solve(mine, other, cent):
     return pl.pallas_call(
         solve_kernel,
         out_shape=(
             jax.ShapeDtypeStruct((BLOCKS * GROUP, GROUP), jnp.float32),
             jax.ShapeDtypeStruct((1, cent.shape[1]), jnp.float32),
         ),
-        in_specs=[SMEM] + [VMEM] * 3,
+        in_specs=[VMEM] * 3,
         out_specs=(VMEM, VMEM),
         scratch_shapes=[
+            pltpu.VMEM((2, HELD * GROUP, GROUP), jnp.float32),
             pltpu.VMEM((BLOCKS, GROUP, (BLOCKS + 1) * GROUP), jnp.float32),
             pltpu.VMEM((BLOCKS, GROUP, (BLOCKS + 1) * GROUP), jnp.float32),
         ],
         compiler_params=pltpu.CompilerParams(vmem_limit_bytes=32 * 1024 * 1024),
         name="solve",
-    )(place, mine, other, cent)
+    )(mine, other, cent)
 
 
 SWAP = [(0, 1), (1, 0)]
@@ -274,19 +277,8 @@
     far = lax.ppermute(send, "high", SWAP)
     near = lax.ppermute(keep, "core", SWAP)
     diagonal = lax.ppermute(far, "core", SWAP)
-    place = jnp.stack(
-        [
-            2 * high + core,
-            2 * (1 - high) + core,
-            2 * high + 1 - core,
-            2 * (1 - high) + 1 - core,
-            core,
-            high,
-            lax.axis_index(("z", "x", "low")),
-        ]
-    ).astype(jnp.int32)
     spread = jnp.broadcast_to(energies[:, None], (GROUP, GROUP))
-    cent, partial = center_gram(place, spread, (keep, far, near, diagonal))
+    cent, partial = center_gram(spread, (keep, far, near, diagonal))
     plane = ("high", "x", "low")
     peers = lax.axis_size(plane)
     parts = lax.all_to_all(
@@ -307,7 +299,7 @@
         tiled=True,
     ).reshape(HELD * GROUP, GROUP)
     other = lax.ppermute(mine, "core", SWAP)
-    coeffs, update = solve(place, mine, other, cent)
+    coeffs, update = solve(mine, other, cent)
     own = lax.dynamic_slice_in_dim(coeffs, (2 * high + core) * GROUP, GROUP, 0)[:, 0]
     update = update[0] * math.sqrt(2 * half * lax.axis_size(("z", "x", "low")))
     away = lax.ppermute(update, "high", SWAP)

time: 73.4 us -> 72 us (0.981)
  Pallas kernels: 14.6 us -> 13.2 us
    pallas_call x1, Pallas kernels: 13 us -> 12.2 us  [solve(): pl.pallas_call(solve_kernel, out_shape=(jax.ShapeDtypeStruct((BLOCKS * GR...]
where the time goes in v9:
time: 72 us; the launch traced here: 71.8 us
  blocking collectives  28.6 us (40%)
  waiting for transfers between devices  15.8 us (22%)
  Pallas kernels  13.2 us (18%)
  starting transfers between devices  11 us (15%)
  local copies, waits for them, and re-layouts  1.8 us (2%)
    all_to_all x1, blocking collectives, per_device(): lax.all_to_all(partial.reshape(peers, -1, GROUP), plane, split_axis=0, co...  16.3 us
    all_to_all x1, blocking collectives, per_device(): lax.all_to_all(jnp.broadcast_to(chunk[None], (peers, *chunk.shape)), plan...  12.3 us
    pallas_call x1, Pallas kernels, solve(): pl.pallas_call(solve_kernel, out_shape=(jax.ShapeDtypeStruct((BLOCKS * GR...  12.2 us
    ppermute x1, waiting for transfers between devices, per_device(): far = lax.ppermute(send, 'high', SWAP)  6.19 us
    ppermute x3, starting transfers between devices, per_device(): lax.ppermute(chunk, 'z', [(n, (n + step) % ring) for n in range(ring)])  5.97 us
    ppermute x3, waiting for transfers between devices, per_device(): lax.ppermute(chunk, 'z', [(n, (n + step) % ring) for n in range(ring)])  3.42 us
    ppermute x1, starting transfers between devices, per_device(): far = lax.ppermute(send, 'high', SWAP)  3.36 us
    ppermute x1, waiting for transfers between devices, per_device(): away = lax.ppermute(update, 'high', SWAP)  3.02 us
  transfers between devices with their start and end apart: 8, of which 6 were waited for; matrix products, arithmetic and copies ran while one was open for 1% of the time, Pallas kernels for 0%

profile of v9, /device:TPU:0, one launch (start us, length us, event | category | flops | bytes accessed | tf_op | source)
XLA Modules:
  0.0 71.8 jit_solution(6428139951091381308)
XLA Ops:
  0.6 0.0 copy-start
  0.7 1.0 %copy-done = bf16[128,2048]{1,0:T(8,128)(2,1)S(1)} copy-done((bf16[128,2048]{1,0:T(8,128)(2,1)S(1)}, bf16[128,2048]{1,0:T(8,128)(2,1)}, u32[]{:S(2)}) %copy-start) | copy-done | bytes 524312
  1.7 3.4 %collective-permute-start = (bf16[128,1024]{1,0:T(8,128)(2,1)S(1)}, bf16[128,1024]{1,0:T(8,128)(2,1)S(1)}, u32[]{:S(2)}, u32[]{:S(2)}) collective-permute-start(bf16[128,1024]{1,0:T(8,128)(2,1)S(1)} %constant_dynamic-slice_fusion.1), channel_id=1, source_target_pairs={{0,64},{64,0},{1,65},{65,1},{2,66},{66,2},{3,67},{67,3},{4,68},{68... | collective-permute-start | bytes 786440 | tf_op jit(solution)/shard_map/ppermute | solution.py:277
  5.1 0.1 collective-permute-start.1
  5.2 6.2 %collective-permute-done.b_ref = bf16[128,1024]{1,0:T(8,128)(2,1)S(1)} collective-permute-done((bf16[128,1024]{1,0:T(8,128)(2,1)S(1)}, bf16[128,1024]{1,0:T(8,128)(2,1)S(1)}, u32[]{:S(2)}, u32[]{:S(2)}) %collective-permute-start) | collective-permute-done | bytes 262176 | tf_op jit(solution)/shard_map/ppermute | solution.py:277
  11.4 0.0 collective-permute-start.2
  11.4 0.0 collective-permute-done.1.c_ref
  11.4 1.5 %collective-permute-done.2.d_ref = bf16[128,1024]{1,0:T(8,128)(2,1)S(1)} collective-permute-done((bf16[128,1024]{1,0:T(8,128)(2,1)S(1)}, bf16[128,1024]{1,0:T(8,128)(2,1)S(1)}, u32[]{:S(2)}, u32[]{:S(2)}) %collective-permute-start.2) | collective-permute-done | bytes 262176 | tf_op jit(solution)/shard_map/ppermute | solution.py:279
  12.9 0.1 broadcast_in_dim.4.e_ref
  13.0 1.0 %center_gram.1 = (bf16[512,1024]{1,0:T(8,128)(2,1)S(1)}, f32[640,128]{1,0:T(8,128)S(1)}) custom-call(f32[128,128]{1,0:T(8,128)S(1)} %broadcast_in_dim.4.e_ref, bf16[128,1024]{1,0:T(8,128)(2,1)S(1)} %constant_dynamic-slice_fusion.a_ref, bf16[128,1024]{1,0:T(8,128)(2,1)S(1)} %collective-permute-done.b_ref, bf16[128,1024]{1,0:T(8,128)(2,1)S(1)} %collective-permute-done.1.c_ref, ...), custom_call_target="tpu_custom_call" | custom-call | tf_op jit(solution)/shard_map/center_gram/pallas_call | solution.py:235
  14.0 16.3 %all_to_all.10 = f32[16,40,128]{2,1,0:T(8,128)S(1)} all-to-all(f32[16,40,128]{2,1,0:T(8,128)S(1)} %bitcast.5), channel_id=1, replica_groups=mesh['high'=2,'core'=2,'z'=4,'x'=4,'low'=2] {'high','x','low'}, dimensions={0} | all-to-all | bytes 655360 | tf_op jit(solution)/shard_map/all_to_all | solution.py:284
  30.4 4.1 %collective-permute-start.5 = (f32[40,128]{1,0:T(8,128)S(1)}, f32[40,128]{1,0:T(8,128)S(1)}, u32[]{:S(2)}, u32[]{:S(2)}) collective-permute-start(f32[40,128]{1,0:T(8,128)S(1)} %reduce_sum.9), channel_id=1, source_target_pairs={{0,24},{8,0},{16,8},{24,16},{1,25},{9,1},{17,9},{25,17},{2,26},{10... | collective-permute-start | bytes 61448 | tf_op jit(solution)/shard_map/ppermute | solution.py:290
  34.5 1.9 %collective-permute-start.3 = (f32[40,128]{1,0:T(8,128)S(1)}, f32[40,128]{1,0:T(8,128)S(1)}, u32[]{:S(2)}, u32[]{:S(2)}) collective-permute-start(f32[40,128]{1,0:T(8,128)S(1)} %reduce_sum.9), channel_id=1, source_target_pairs={{0,16},{8,24},{16,0},{24,8},{1,17},{9,25},{17,1},{25,9},{2,18},{10... | collective-permute-start | bytes 61448 | tf_op jit(solution)/shard_map/ppermute | solution.py:290
  36.4 0.0 collective-permute-done.5
  36.4 3.1 %collective-permute-done.4 = f32[40,128]{1,0:T(8,128)S(1)} collective-permute-done((f32[40,128]{1,0:T(8,128)S(1)}, f32[40,128]{1,0:T(8,128)S(1)}, u32[]{:S(2)}, u32[]{:S(2)}) %collective-permute-start.4) | collective-permute-done | bytes 20512 | tf_op jit(solution)/shard_map/ppermute | solution.py:290
  39.5 0.3 collective-permute-done.3
  39.8 12.3 %all_to_all.11 = f32[16,40,128]{2,1,0:T(8,128)S(1)} all-to-all(f32[16,40,128]{2,1,0:T(8,128)S(1)} %broadcast_in_dim.5), channel_id=1, replica_groups=mesh['high'=2,'core'=2,'z'=4,'x'=4,'low'=2] {'high','x','low'}, dimensions={0} | all-to-all | bytes 655360 | tf_op jit(solution)/shard_map/all_to_all | solution.py:294
  52.1 0.0 collective-permute-start.6
  52.1 1.6 %collective-permute-done.6.other_ref = f32[640,128]{1,0:T(8,128)S(1)} collective-permute-done((f32[640,128]{1,0:T(8,128)S(1)}, f32[640,128]{1,0:T(8,128)S(1)}, u32[]{:S(2)}, u32[]{:S(2)}) %collective-permute-start.6) | collective-permute-done | bytes 327712 | tf_op jit(solution)/shard_map/ppermute | solution.py:301
  53.7 12.2 %solve.1 = (f32[512,128]{1,0:T(8,128)S(1)}, f32[1,1024]{1,0:T(1,128)S(1)}) custom-call(f32[640,128]{1,0:T(8,128)S(1)} %bitcast.4, f32[640,128]{1,0:T(8,128)S(1)} %collective-permute-done.6.other_ref, bf16[512,1024]{1,0:T(8,128)(2,1)S(1)} %get-tuple-element.11.cent_ref), custom_call_target="tpu_custom_call" | custom-call | tf_op jit(solution)/shard_map/solve/pallas_call | solution.py:249
  66.0 1.5 %collective-permute-start.7 = (f32[1024]{0:T(1024)S(1)}, f32[1024]{0:T(1024)S(1)}, u32[]{:S(2)}, u32[]{:S(2)}) collective-permute-start(f32[1024]{0:T(1024)S(1)} %bitcast.6), channel_id=1, source_target_pairs={{0,64},{64,0},{1,65},{65,1},{2,66},{66,2},{3,67},{67,3},{4,68},{68... | collective-permute-start | bytes 12296 | tf_op jit(solution)/shard_map/ppermute | solution.py:305
  67.5 0.6 dynamic-slice_reduce_fusion
  68.1 3.0 %collective-permute-done.7 = f32[1024]{0:T(1024)S(1)} collective-permute-done((f32[1024]{0:T(1024)S(1)}, f32[1024]{0:T(1024)S(1)}, u32[]{:S(2)}, u32[]{:S(2)}) %collective-permute-start.7) | collective-permute-done | bytes 4128 | tf_op jit(solution)/shard_map/ppermute | solution.py:305
  71.2 0.6 pad_maximum_fusion
  (10 shorter events, 0.1 us)
Async XLA Ops:
  0.6 1.0 %copy-start = (bf16[128,2048]{1,0:T(8,128)(2,1)S(1)}, bf16[128,2048]{1,0:T(8,128)(2,1)}, u32[]{:S(2)}) copy-start(bf16[128,2048]{1,0:T(8,128)(2,1)} %param.2) | copy-start | bytes 1572868
  1.7 9.7 %collective-permute-start = (bf16[128,1024]{1,0:T(8,128)(2,1)S(1)}, bf16[128,1024]{1,0:T(8,128)(2,1)S(1)}, u32[]{:S(2)}, u32[]{:S(2)}) collective-permute-start(bf16[128,1024]{1,0:T(8,128)(2,1)S(1)} %constant_dynamic-slice_fusion.1), channel_id=1, source_target_pairs={{0,64},{64,0},{1,65},{65,1},{2,66},{66,2},{3,67},{67,3},{4,68},{68... | collective-permute-start | bytes 786440 | tf_op jit(solution)/shard_map/ppermute | solution.py:277
  5.1 7.8 %copy-start.1 = (f32[128]{0:T(128)S(1)}, f32[128]{0:T(128)}, u32[]{:S(2)}) copy-start(f32[128]{0:T(128)} %param.3) | copy-start | bytes 1540
  5.1 6.3 %collective-permute-start.1 = (bf16[128,1024]{1,0:T(8,128)(2,1)S(1)}, bf16[128,1024]{1,0:T(8,128)(2,1)S(1)}, u32[]{:S(2)}, u32[]{:S(2)}) collective-permute-start(bf16[128,1024]{1,0:T(8,128)(2,1)S(1)} %constant_dynamic-slice_fusion.a_ref), channel_id=1, source_target_pairs={{0,32},{32,0},{1,33},{33,1},{2,34},{34,2},{3,35},{35,3},{4,36},{36... | collective-permute-start | bytes 786440 | tf_op jit(solution)/shard_map/ppermute | solution.py:278
  11.4 1.5 %collective-permute-start.2 = (bf16[128,1024]{1,0:T(8,128)(2,1)S(1)}, bf16[128,1024]{1,0:T(8,128)(2,1)S(1)}, u32[]{:S(2)}, u32[]{:S(2)}) collective-permute-start(bf16[128,1024]{1,0:T(8,128)(2,1)S(1)} %collective-permute-done.b_ref), channel_id=1, source_target_pairs={{0,32},{32,0},{1,33},{33,1},{2,34},{34,2},{3,35},{35,3},{4,36},{36... | collective-permute-start | bytes 786440 | tf_op jit(solution)/shard_map/ppermute | solution.py:279
  30.4 6.0 %collective-permute-start.5 = (f32[40,128]{1,0:T(8,128)S(1)}, f32[40,128]{1,0:T(8,128)S(1)}, u32[]{:S(2)}, u32[]{:S(2)}) collective-permute-start(f32[40,128]{1,0:T(8,128)S(1)} %reduce_sum.9), channel_id=1, source_target_pairs={{0,24},{8,0},{16,8},{24,16},{1,25},{9,1},{17,9},{25,17},{2,26},{10... | collective-permute-start | bytes 61448 | tf_op jit(solution)/shard_map/ppermute | solution.py:290
  34.5 5.0 %collective-permute-start.4 = (f32[40,128]{1,0:T(8,128)S(1)}, f32[40,128]{1,0:T(8,128)S(1)}, u32[]{:S(2)}, u32[]{:S(2)}) collective-permute-start(f32[40,128]{1,0:T(8,128)S(1)} %reduce_sum.9), channel_id=1, source_target_pairs={{0,8},{8,16},{16,24},{24,0},{1,9},{9,17},{17,25},{25,1},{2,10},{10... | collective-permute-start | bytes 61448 | tf_op jit(solution)/shard_map/ppermute | solution.py:290
  34.5 5.3 %collective-permute-start.3 = (f32[40,128]{1,0:T(8,128)S(1)}, f32[40,128]{1,0:T(8,128)S(1)}, u32[]{:S(2)}, u32[]{:S(2)}) collective-permute-start(f32[40,128]{1,0:T(8,128)S(1)} %reduce_sum.9), channel_id=1, source_target_pairs={{0,16},{8,24},{16,0},{24,8},{1,17},{9,25},{17,1},{25,9},{2,18},{10... | collective-permute-start | bytes 61448 | tf_op jit(solution)/shard_map/ppermute | solution.py:290
  52.1 1.6 %collective-permute-start.6 = (f32[640,128]{1,0:T(8,128)S(1)}, f32[640,128]{1,0:T(8,128)S(1)}, u32[]{:S(2)}, u32[]{:S(2)}) collective-permute-start(f32[640,128]{1,0:T(8,128)S(1)} %bitcast.3), channel_id=1, source_target_pairs={{0,32},{32,0},{1,33},{33,1},{2,34},{34,2},{3,35},{35,3},{4,36},{36... | collective-permute-start | bytes 983048 | tf_op jit(solution)/shard_map/ppermute | solution.py:301
  66.0 5.2 %collective-permute-start.7 = (f32[1024]{0:T(1024)S(1)}, f32[1024]{0:T(1024)S(1)}, u32[]{:S(2)}, u32[]{:S(2)}) collective-permute-start(f32[1024]{0:T(1024)S(1)} %bitcast.6), channel_id=1, source_target_pairs={{0,64},{64,0},{1,65},{65,1},{2,66},{66,2},{3,67},{67,3},{4,68},{68... | collective-permute-start | bytes 12296 | tf_op jit(solution)/shard_map/ppermute | solution.py:305

commit v10 on v9

--- a/solution.py
+++ b/solution.py
@@ -156,9 +156,9 @@
     mine_ref, other_ref, cent_ref, coeff_ref, update_ref, parts, gram, rest
 ):
     blocks = BLOCKS
-    core = lax.axis_index("core")
-    parts[core] = mine_ref[...]
-    parts[1 - core] = other_ref[...]
+    core_index = lax.axis_index("core")
+    parts[core_index] = mine_ref[...]
+    parts[1 - core_index] = other_ref[...]
     for core, held in enumerate(LISTS):
         for n, (r, c) in enumerate(held):
             gram[r, :, GROUP * c : GROUP * c + GROUP] = parts[
@@ -211,8 +211,8 @@
     for k in range(blocks):
         step(k)
     xs = [rest[k, :, GROUP * blocks :] for k in range(blocks)]
-    for k in range(blocks):
-        coeff_ref[GROUP * k : GROUP * k + GROUP, :] = xs[k]
+    mine = 2 * lax.axis_index("high") + core_index
+    coeff_ref[...] = rest[mine, :, GROUP * blocks :]
     width = cent_ref.shape[1]
     for piece in range(width // GROUP):
         total = jnp.zeros((ROWS, GROUP), jnp.float32)
@@ -249,7 +249,7 @@
     return pl.pallas_call(
         solve_kernel,
         out_shape=(
-            jax.ShapeDtypeStruct((BLOCKS * GROUP, GROUP), jnp.float32),
+            jax.ShapeDtypeStruct((GROUP, GROUP), jnp.float32),
             jax.ShapeDtypeStruct((1, cent.shape[1]), jnp.float32),
         ),
         in_specs=[VMEM] * 3,
@@ -300,12 +300,11 @@
     ).reshape(HELD * GROUP, GROUP)
     other = lax.ppermute(mine, "core", SWAP)
     coeffs, update = solve(mine, other, cent)
-    own = lax.dynamic_slice_in_dim(coeffs, (2 * high + core) * GROUP, GROUP, 0)[:, 0]
+    own = coeffs[:, 0]
     update = update[0] * math.sqrt(2 * half * lax.axis_size(("z", "x", "low")))
     away = lax.ppermute(update, "high", SWAP)
-    lower = jnp.where(high == 0, update, away)
-    upper = jnp.where(high == 0, away, update)
-    return jnp.concatenate([lower, upper]), own
+    whole = lax.dynamic_update_slice(jnp.zeros((2 * half,), jnp.float32), update, (high * half,))
+    return lax.dynamic_update_slice(whole, away, ((1 - high) * half,)), own
 
 
 def solution(mesh):

time: 72 us -> 71.8 us (level)
  waiting for transfers between devices: 15.8 us -> 13.9 us
  starting transfers between devices: 11 us -> 12.2 us
  local copies, waits for them, and re-layouts: 1.8 us -> 2.72 us
    ppermute x3, waiting for transfers between devices: 3.42 us -> 1.76 us  [per_device(): lax.ppermute(chunk, 'z', [(n, (n + step) % ring) for n in range(ring)])]
    ppermute x3, starting transfers between devices: 5.97 us -> 7.19 us  [per_device(): lax.ppermute(chunk, 'z', [(n, (n + step) % ring) for n in range(ring)])]
    unnamed x4 -> x6, local copies, waits for them, and re-layouts: 1.04 us -> 1.64 us
  transfers between devices with their start and end apart: 8 -> 8, of which waited for: 6 -> 5; matrix products, arithmetic and copies ran while one was open for 1% -> 1% of each run, Pallas kernels for 0% -> 0%
where the time goes in v10:
time: 71.8 us; the launch traced here: 71.5 us
  blocking collectives  28.6 us (40%)
  waiting for transfers between devices  13.9 us (19%)
  Pallas kernels  13.3 us (19%)
  starting transfers between devices  12.2 us (17%)
  local copies, waits for them, and re-layouts  2.72 us (4%)
    all_to_all x1, blocking collectives, per_device(): lax.all_to_all(partial.reshape(peers, -1, GROUP), plane, split_axis=0, co...  16.3 us
    all_to_all x1, blocking collectives, per_device(): lax.all_to_all(jnp.broadcast_to(chunk[None], (peers, *chunk.shape)), plan...  12.3 us
    pallas_call x1, Pallas kernels, solve(): pl.pallas_call(solve_kernel, out_shape=(jax.ShapeDtypeStruct((GROUP, GROU...  12.3 us
    ppermute x3, starting transfers between devices, per_device(): lax.ppermute(chunk, 'z', [(n, (n + step) % ring) for n in range(ring)])  7.19 us
    ppermute x1, waiting for transfers between devices, per_device(): far = lax.ppermute(send, 'high', SWAP)  6.19 us
    ppermute x1, starting transfers between devices, per_device(): far = lax.ppermute(send, 'high', SWAP)  3.36 us
    ppermute x1, waiting for transfers between devices, per_device(): away = lax.ppermute(update, 'high', SWAP)  2.84 us
    ppermute x3, waiting for transfers between devices, per_device(): lax.ppermute(chunk, 'z', [(n, (n + step) % ring) for n in range(ring)])  1.76 us
  transfers between devices with their start and end apart: 8, of which 5 were waited for; matrix products, arithmetic and copies ran while one was open for 1% of the time, Pallas kernels for 0%

profile of v10, /device:TPU:0, one launch (start us, length us, event | category | flops | bytes accessed | tf_op | source)
XLA Modules:
  0.0 71.5 jit_solution(14174067813293257655)
XLA Ops:
  0.6 0.0 copy-start
  0.7 1.0 %copy-done = bf16[128,2048]{1,0:T(8,128)(2,1)S(1)} copy-done((bf16[128,2048]{1,0:T(8,128)(2,1)S(1)}, bf16[128,2048]{1,0:T(8,128)(2,1)}, u32[]{:S(2)}) %copy-start) | copy-done | bytes 524312
  1.7 3.4 %collective-permute-start = (bf16[128,1024]{1,0:T(8,128)(2,1)S(1)}, bf16[128,1024]{1,0:T(8,128)(2,1)S(1)}, u32[]{:S(2)}, u32[]{:S(2)}) collective-permute-start(bf16[128,1024]{1,0:T(8,128)(2,1)S(1)} %constant_dynamic-slice_fusion.1), channel_id=1, source_target_pairs={{0,64},{64,0},{1,65},{65,1},{2,66},{66,2},{3,67},{67,3},{4,68},{68... | collective-permute-start | bytes 786440 | tf_op jit(solution)/shard_map/ppermute | solution.py:277
  5.1 0.1 collective-permute-start.1
  5.2 6.2 %collective-permute-done.b_ref = bf16[128,1024]{1,0:T(8,128)(2,1)S(1)} collective-permute-done((bf16[128,1024]{1,0:T(8,128)(2,1)S(1)}, bf16[128,1024]{1,0:T(8,128)(2,1)S(1)}, u32[]{:S(2)}, u32[]{:S(2)}) %collective-permute-start) | collective-permute-done | bytes 262176 | tf_op jit(solution)/shard_map/ppermute | solution.py:277
  11.4 0.0 collective-permute-start.2
  11.4 1.5 %collective-permute-done.2.d_ref = bf16[128,1024]{1,0:T(8,128)(2,1)S(1)} collective-permute-done((bf16[128,1024]{1,0:T(8,128)(2,1)S(1)}, bf16[128,1024]{1,0:T(8,128)(2,1)S(1)}, u32[]{:S(2)}, u32[]{:S(2)}) %collective-permute-start.2) | collective-permute-done | bytes 262176 | tf_op jit(solution)/shard_map/ppermute | solution.py:279
  12.9 0.1 broadcast_in_dim.7.e_ref
  13.0 1.0 %center_gram.1 = (bf16[512,1024]{1,0:T(8,128)(2,1)S(1)}, f32[640,128]{1,0:T(8,128)S(1)}) custom-call(f32[128,128]{1,0:T(8,128)S(1)} %broadcast_in_dim.7.e_ref, bf16[128,1024]{1,0:T(8,128)(2,1)S(1)} %constant_dynamic-slice_fusion.a_ref, bf16[128,1024]{1,0:T(8,128)(2,1)S(1)} %collective-permute-done.b_ref, bf16[128,1024]{1,0:T(8,128)(2,1)S(1)} %collective-permute-done.1.c_ref, ...), custom_call_target="tpu_custom_call" | custom-call | tf_op jit(solution)/shard_map/center_gram/pallas_call | solution.py:235
  14.0 16.3 %all_to_all.10 = f32[16,40,128]{2,1,0:T(8,128)S(1)} all-to-all(f32[16,40,128]{2,1,0:T(8,128)S(1)} %bitcast.5), channel_id=1, replica_groups=mesh['high'=2,'core'=2,'z'=4,'x'=4,'low'=2] {'high','x','low'}, dimensions={0} | all-to-all | bytes 655360 | tf_op jit(solution)/shard_map/all_to_all | solution.py:284
  30.4 4.0 %collective-permute-start.3 = (f32[40,128]{1,0:T(8,128)S(1)}, f32[40,128]{1,0:T(8,128)S(1)}, u32[]{:S(2)}, u32[]{:S(2)}) collective-permute-start(f32[40,128]{1,0:T(8,128)S(1)} %reduce_sum.9), channel_id=1, source_target_pairs={{0,16},{8,24},{16,0},{24,8},{1,17},{9,25},{17,1},{25,9},{2,18},{10... | collective-permute-start | bytes 61448 | tf_op jit(solution)/shard_map/ppermute | solution.py:290
  34.3 1.0 %collective-permute-start.4 = (f32[40,128]{1,0:T(8,128)S(1)}, f32[40,128]{1,0:T(8,128)S(1)}, u32[]{:S(2)}, u32[]{:S(2)}) collective-permute-start(f32[40,128]{1,0:T(8,128)S(1)} %reduce_sum.9), channel_id=1, source_target_pairs={{0,8},{8,16},{16,24},{24,0},{1,9},{9,17},{17,25},{25,1},{2,10},{10... | collective-permute-start | bytes 61448 | tf_op jit(solution)/shard_map/ppermute | solution.py:290
  35.4 2.2 %collective-permute-start.5 = (f32[40,128]{1,0:T(8,128)S(1)}, f32[40,128]{1,0:T(8,128)S(1)}, u32[]{:S(2)}, u32[]{:S(2)}) collective-permute-start(f32[40,128]{1,0:T(8,128)S(1)} %reduce_sum.9), channel_id=1, source_target_pairs={{0,24},{8,0},{16,8},{24,16},{1,25},{9,1},{17,9},{25,17},{2,26},{10... | collective-permute-start | bytes 61448 | tf_op jit(solution)/shard_map/ppermute | solution.py:290
  37.6 1.8 %collective-permute-done.4 = f32[40,128]{1,0:T(8,128)S(1)} collective-permute-done((f32[40,128]{1,0:T(8,128)S(1)}, f32[40,128]{1,0:T(8,128)S(1)}, u32[]{:S(2)}, u32[]{:S(2)}) %collective-permute-start.4) | collective-permute-done | bytes 20512 | tf_op jit(solution)/shard_map/ppermute | solution.py:290
  39.4 12.3 %all_to_all.11 = f32[16,40,128]{2,1,0:T(8,128)S(1)} all-to-all(f32[16,40,128]{2,1,0:T(8,128)S(1)} %broadcast_in_dim.8), channel_id=1, replica_groups=mesh['high'=2,'core'=2,'z'=4,'x'=4,'low'=2] {'high','x','low'}, dimensions={0} | all-to-all | bytes 655360 | tf_op jit(solution)/shard_map/all_to_all | solution.py:294
  51.7 0.0 collective-permute-start.6
  51.7 1.6 %collective-permute-done.6.other_ref = f32[640,128]{1,0:T(8,128)S(1)} collective-permute-done((f32[640,128]{1,0:T(8,128)S(1)}, f32[640,128]{1,0:T(8,128)S(1)}, u32[]{:S(2)}, u32[]{:S(2)}) %collective-permute-start.6) | collective-permute-done | bytes 327712 | tf_op jit(solution)/shard_map/ppermute | solution.py:301
  53.3 12.3 %solve.1 = (f32[128,128]{1,0:T(8,128)S(1)}, f32[1,1024]{1,0:T(1,128)S(1)}) custom-call(f32[640,128]{1,0:T(8,128)S(1)} %bitcast.4, f32[640,128]{1,0:T(8,128)S(1)} %collective-permute-done.6.other_ref, bf16[512,1024]{1,0:T(8,128)(2,1)S(1)} %get-tuple-element.11.cent_ref), custom_call_target="tpu_custom_call" | custom-call | tf_op jit(solution)/shard_map/solve/pallas_call | solution.py:249
  65.6 1.6 %collective-permute-start.7 = (f32[1024]{0:T(1024)S(1)}, f32[1024]{0:T(1024)S(1)}, u32[]{:S(2)}, u32[]{:S(2)}) collective-permute-start(f32[1024]{0:T(1024)S(1)} %bitcast.6), channel_id=1, source_target_pairs={{0,64},{64,0},{1,65},{65,1},{2,66},{66,2},{3,67},{67,3},{4,68},{68... | collective-permute-start | bytes 12296 | tf_op jit(solution)/shard_map/ppermute | solution.py:305
  67.1 0.6 slice_reduce_fusion
  67.8 0.2 dynamic_update_slice.6
  67.9 2.8 %collective-permute-done.7 = f32[1024]{0:T(1024)S(1)} collective-permute-done((f32[1024]{0:T(1024)S(1)}, f32[1024]{0:T(1024)S(1)}, u32[]{:S(2)}, u32[]{:S(2)}) %collective-permute-start.7) | collective-permute-done | bytes 4128 | tf_op jit(solution)/shard_map/ppermute | solution.py:305
  70.8 0.2 dynamic_update_slice.7
  70.9 0.6 copy-done.1
  (13 shorter events, 0.1 us)
Async XLA Ops:
  0.6 1.0 %copy-start = (bf16[128,2048]{1,0:T(8,128)(2,1)S(1)}, bf16[128,2048]{1,0:T(8,128)(2,1)}, u32[]{:S(2)}) copy-start(bf16[128,2048]{1,0:T(8,128)(2,1)} %param.2) | copy-start | bytes 1572868
  1.7 9.7 %collective-permute-start = (bf16[128,1024]{1,0:T(8,128)(2,1)S(1)}, bf16[128,1024]{1,0:T(8,128)(2,1)S(1)}, u32[]{:S(2)}, u32[]{:S(2)}) collective-permute-start(bf16[128,1024]{1,0:T(8,128)(2,1)S(1)} %constant_dynamic-slice_fusion.1), channel_id=1, source_target_pairs={{0,64},{64,0},{1,65},{65,1},{2,66},{66,2},{3,67},{67,3},{4,68},{68... | collective-permute-start | bytes 786440 | tf_op jit(solution)/shard_map/ppermute | solution.py:277
  5.1 7.8 %copy-start.2 = (f32[128]{0:T(128)S(1)}, f32[128]{0:T(128)}, u32[]{:S(2)}) copy-start(f32[128]{0:T(128)} %param.3) | copy-start | bytes 1540
  5.1 6.3 %collective-permute-start.1 = (bf16[128,1024]{1,0:T(8,128)(2,1)S(1)}, bf16[128,1024]{1,0:T(8,128)(2,1)S(1)}, u32[]{:S(2)}, u32[]{:S(2)}) collective-permute-start(bf16[128,1024]{1,0:T(8,128)(2,1)S(1)} %constant_dynamic-slice_fusion.a_ref), channel_id=1, source_target_pairs={{0,32},{32,0},{1,33},{33,1},{2,34},{34,2},{3,35},{35,3},{4,36},{36... | collective-permute-start | bytes 786440 | tf_op jit(solution)/shard_map/ppermute | solution.py:278
  11.4 1.5 %collective-permute-start.2 = (bf16[128,1024]{1,0:T(8,128)(2,1)S(1)}, bf16[128,1024]{1,0:T(8,128)(2,1)S(1)}, u32[]{:S(2)}, u32[]{:S(2)}) collective-permute-start(bf16[128,1024]{1,0:T(8,128)(2,1)S(1)} %collective-permute-done.b_ref), channel_id=1, source_target_pairs={{0,32},{32,0},{1,33},{33,1},{2,34},{34,2},{3,35},{35,3},{4,36},{36... | collective-permute-start | bytes 786440 | tf_op jit(solution)/shard_map/ppermute | solution.py:279
  30.4 7.2 %collective-permute-start.3 = (f32[40,128]{1,0:T(8,128)S(1)}, f32[40,128]{1,0:T(8,128)S(1)}, u32[]{:S(2)}, u32[]{:S(2)}) collective-permute-start(f32[40,128]{1,0:T(8,128)S(1)} %reduce_sum.9), channel_id=1, source_target_pairs={{0,16},{8,24},{16,0},{24,8},{1,17},{9,25},{17,1},{25,9},{2,18},{10... | collective-permute-start | bytes 61448 | tf_op jit(solution)/shard_map/ppermute | solution.py:290
  34.3 5.0 %collective-permute-start.4 = (f32[40,128]{1,0:T(8,128)S(1)}, f32[40,128]{1,0:T(8,128)S(1)}, u32[]{:S(2)}, u32[]{:S(2)}) collective-permute-start(f32[40,128]{1,0:T(8,128)S(1)} %reduce_sum.9), channel_id=1, source_target_pairs={{0,8},{8,16},{16,24},{24,0},{1,9},{9,17},{17,25},{25,1},{2,10},{10... | collective-permute-start | bytes 61448 | tf_op jit(solution)/shard_map/ppermute | solution.py:290
  35.4 4.0 %collective-permute-start.5 = (f32[40,128]{1,0:T(8,128)S(1)}, f32[40,128]{1,0:T(8,128)S(1)}, u32[]{:S(2)}, u32[]{:S(2)}) collective-permute-start(f32[40,128]{1,0:T(8,128)S(1)} %reduce_sum.9), channel_id=1, source_target_pairs={{0,24},{8,0},{16,8},{24,16},{1,25},{9,1},{17,9},{25,17},{2,26},{10... | collective-permute-start | bytes 61448 | tf_op jit(solution)/shard_map/ppermute | solution.py:290
  51.7 1.6 %collective-permute-start.6 = (f32[640,128]{1,0:T(8,128)S(1)}, f32[640,128]{1,0:T(8,128)S(1)}, u32[]{:S(2)}, u32[]{:S(2)}) collective-permute-start(f32[640,128]{1,0:T(8,128)S(1)} %bitcast.3), channel_id=1, source_target_pairs={{0,32},{32,0},{1,33},{33,1},{2,34},{34,2},{3,35},{35,3},{4,36},{36... | collective-permute-start | bytes 983048 | tf_op jit(solution)/shard_map/ppermute | solution.py:301
  65.6 5.2 %collective-permute-start.7 = (f32[1024]{0:T(1024)S(1)}, f32[1024]{0:T(1024)S(1)}, u32[]{:S(2)}, u32[]{:S(2)}) collective-permute-start(f32[1024]{0:T(1024)S(1)} %bitcast.6), channel_id=1, source_target_pairs={{0,64},{64,0},{1,65},{65,1},{2,66},{66,2},{3,67},{67,3},{4,68},{68... | collective-permute-start | bytes 12296 | tf_op jit(solution)/shard_map/ppermute | solution.py:305
  70.9 0.6 copy-start.1
